TPU v7x, 32 devices: a whole 2x2x4 slice. The times are simulated.
32 devices in a mesh: pts: 16 (over z, y, x), ctr: 2 (over core).
Axes of the slice: x: 2, y: 2, z: 4, core: 2. Of those that a mesh axis runs over, the one named last changes fastest.
Arguments:
- points: bfloat16 [32, 32768], P(None, 'pts'), may hold values from -6 to 6
- centres: bfloat16 [32, 16384], P(None, 'ctr'), may hold values from -6 to 6
- coef: float32 [16, 16384], P(None, 'ctr'), may hold values from -6 to 6
- resid: float32 [16, 16384], P(None, 'ctr'), may hold values from -6 to 6
- direction: float32 [16, 16384], P(None, 'ctr'), may hold values from -6 to 6
- precond: float32 [16384], P('ctr'), may hold values from 0.5 to 4
Outputs:
- coef_next: float32 [16, 16384], P(None, 'ctr')
- resid_next: float32 [16, 16384], P(None, 'ctr')
- dir_next: float32 [16, 16384], P(None, 'ctr')
All inputs are finite; a program needn't handle non-finite values.
Results may differ from a plain program's by a relative error of at most 0.0012.
Values may be sent and summed in bfloat16 or wider, within the bound.
No kernel may reach another device: no remote copies, remote signals or barrier semaphores. Data moves between devices by JAX's collectives and lax.ppermute only.
A program may use at most 128 MiB of HBM per device.

v0:
```python
import jax
import jax.numpy as jnp
from jax import lax
from jax.sharding import PartitionSpec as P


def build_kernel(points, centres):
    cent32 = centres.astype(jnp.float32)
    csq = jnp.sum(cent32 * cent32, axis=0)
    feat = points.shape[0]
    rows = points.shape[1]
    width = min(256, rows)
    count = rows // width
    pieces = points.reshape(feat, count, width).transpose(1, 0, 2)

    def one_block(block):
        pts32 = block.astype(jnp.float32)
        xsq = jnp.sum(pts32 * pts32, axis=0)
        cross = lax.dot_general(
            block, centres, (((0,), (0,)), ((), ())), preferred_element_type=jnp.float32
        )
        return jnp.exp(-0.125 * (xsq[:, None] + csq[None, :] - 2.0 * cross)).astype(jnp.bfloat16)

    tiles = lax.map(one_block, pieces)
    return tiles.reshape(rows, centres.shape[1])


def shards(points, centres, coef, resid, direction, precond):
    kern = build_kernel(points, centres)
    dirb = direction.astype(jnp.bfloat16)
    fit_part = lax.dot_general(
        dirb, kern, (((1,), (1,)), ((), ())), preferred_element_type=jnp.float32
    )
    fitted = lax.psum(fit_part.astype(jnp.bfloat16), "ctr")
    col_part = jnp.dot(fitted, kern, preferred_element_type=jnp.float32)
    num_pts = lax.axis_size("pts")
    scale = 2048.0 / (points.shape[1] * num_pts)
    colsum = lax.psum(col_part, "pts")
    image = colsum * scale + 0.5 * direction
    rz_part = jnp.sum(resid * resid * precond[None, :], axis=1)
    curv, rz = lax.psum((jnp.sum(direction * image, axis=1), rz_part), "ctr")
    alpha = rz / curv
    coef_next = coef + alpha[:, None] * direction
    resid_next = resid - alpha[:, None] * image
    scaled = precond[None, :] * resid_next
    rz_new = lax.psum(jnp.sum(resid_next * scaled, axis=1), "ctr")
    dir_next = scaled + (rz_new / rz)[:, None] * direction
    return (coef_next, resid_next, dir_next)


def solution(mesh):
    return jax.shard_map(
        shards,
        mesh=mesh,
        in_specs=(
            P(None, "pts"),
            P(None, "ctr"),
            P(None, "ctr"),
            P(None, "ctr"),
            P(None, "ctr"),
            P("ctr"),
        ),
        out_specs=(P(None, "ctr"), P(None, "ctr"), P(None, "ctr")),
        check_vma=False,
    )
```

profile of v0, /device:TPU:0, one launch (start us, length us, event | category | flops | bytes accessed | tf_op | source)
XLA Modules:
  0.0 231.3 jit_solution(10259404867447155018)
XLA Ops:
  7.2 0.0 copy-start
  7.2 0.0 all-reduce.4.cloned.1.call-start
  7.2 1.0 copy.10
  8.2 1.2 multiply_reduce_fusion.1
  9.4 42.5 %while.10 = (s32[]{:T(128)}, bf16[8,256,8192]{2,1,0:T(8,128)(2,1)}, bf16[8,32,256]{2,1,0:T(8,128)(2,1)S(1)}, f32[8192]{0:T(1024)S(1)}, bf16[32,8192]{1,0:T(8,128)(2,1)}, /*index=5*/s32[]{:T(128)}) while((s32[]{:T(128)}, bf16[8,256,8192]{2,1,0:T(8,128)(2,1)}, bf16[8,32,256]{2,1,0:T(8,128)(2,1)S(1)}, f32[8192]{0:T(1024)S(1)}, ...), condition=%wide.region_5.6_spmd, body=%wide.region_3.5_spmd.sunk | while | flops 144727808 | bytes 4787273 | solution.py:24
  9.5 5.3 %fusion.22 = bf16[8,256,8192]{2,1,0:T(8,128)(2,1)} fusion(bf16[8,256,8192]{2,1,0:T(8,128)(2,1)} %get-tuple-element.89, s32[]{:T(128)} %get-tuple-element.88, bf16[32,8192]{1,0:T(8,128)(2,1)} %get-tuple-element.98, f32[8192]{0:T(1024)S(1)} %get-tuple-element.97, f32[256]{0:T(256)S(1)} %multiply_reduce_fusion.5, ...), kind=kOutput, calls=%fused_computation.6.clone.1 | convolution fusion | flops 144703488 | bytes 4769792 | tf_op jit(solution)/shard_map/while/body/eval_jaxpr/dot_general | solution.py:19
  14.8 5.3 %fusion.22 = bf16[8,256,8192]{2,1,0:T(8,128)(2,1)} fusion(bf16[8,256,8192]{2,1,0:T(8,128)(2,1)} %get-tuple-element.89, s32[]{:T(128)} %get-tuple-element.88, bf16[32,8192]{1,0:T(8,128)(2,1)} %get-tuple-element.98, f32[8192]{0:T(1024)S(1)} %get-tuple-element.97, f32[256]{0:T(256)S(1)} %multiply_reduce_fusion.5, ...), kind=kOutput, calls=%fused_computation.6.clone.1 | convolution fusion | flops 144703488 | bytes 4769792 | tf_op jit(solution)/shard_map/while/body/eval_jaxpr/dot_general | solution.py:19
  20.1 5.3 %fusion.22 = bf16[8,256,8192]{2,1,0:T(8,128)(2,1)} fusion(bf16[8,256,8192]{2,1,0:T(8,128)(2,1)} %get-tuple-element.89, s32[]{:T(128)} %get-tuple-element.88, bf16[32,8192]{1,0:T(8,128)(2,1)} %get-tuple-element.98, f32[8192]{0:T(1024)S(1)} %get-tuple-element.97, f32[256]{0:T(256)S(1)} %multiply_reduce_fusion.5, ...), kind=kOutput, calls=%fused_computation.6.clone.1 | convolution fusion | flops 144703488 | bytes 4769792 | tf_op jit(solution)/shard_map/while/body/eval_jaxpr/dot_general | solution.py:19
  25.4 5.3 %fusion.22 = bf16[8,256,8192]{2,1,0:T(8,128)(2,1)} fusion(bf16[8,256,8192]{2,1,0:T(8,128)(2,1)} %get-tuple-element.89, s32[]{:T(128)} %get-tuple-element.88, bf16[32,8192]{1,0:T(8,128)(2,1)} %get-tuple-element.98, f32[8192]{0:T(1024)S(1)} %get-tuple-element.97, f32[256]{0:T(256)S(1)} %multiply_reduce_fusion.5, ...), kind=kOutput, calls=%fused_computation.6.clone.1 | convolution fusion | flops 144703488 | bytes 4769792 | tf_op jit(solution)/shard_map/while/body/eval_jaxpr/dot_general | solution.py:19
  30.7 5.2 %fusion.22 = bf16[8,256,8192]{2,1,0:T(8,128)(2,1)} fusion(bf16[8,256,8192]{2,1,0:T(8,128)(2,1)} %get-tuple-element.89, s32[]{:T(128)} %get-tuple-element.88, bf16[32,8192]{1,0:T(8,128)(2,1)} %get-tuple-element.98, f32[8192]{0:T(1024)S(1)} %get-tuple-element.97, f32[256]{0:T(256)S(1)} %multiply_reduce_fusion.5, ...), kind=kOutput, calls=%fused_computation.6.clone.1 | convolution fusion | flops 144703488 | bytes 4769792 | tf_op jit(solution)/shard_map/while/body/eval_jaxpr/dot_general | solution.py:19
  36.0 5.3 %fusion.22 = bf16[8,256,8192]{2,1,0:T(8,128)(2,1)} fusion(bf16[8,256,8192]{2,1,0:T(8,128)(2,1)} %get-tuple-element.89, s32[]{:T(128)} %get-tuple-element.88, bf16[32,8192]{1,0:T(8,128)(2,1)} %get-tuple-element.98, f32[8192]{0:T(1024)S(1)} %get-tuple-element.97, f32[256]{0:T(256)S(1)} %multiply_reduce_fusion.5, ...), kind=kOutput, calls=%fused_computation.6.clone.1 | convolution fusion | flops 144703488 | bytes 4769792 | tf_op jit(solution)/shard_map/while/body/eval_jaxpr/dot_general | solution.py:19
  41.3 5.3 %fusion.22 = bf16[8,256,8192]{2,1,0:T(8,128)(2,1)} fusion(bf16[8,256,8192]{2,1,0:T(8,128)(2,1)} %get-tuple-element.89, s32[]{:T(128)} %get-tuple-element.88, bf16[32,8192]{1,0:T(8,128)(2,1)} %get-tuple-element.98, f32[8192]{0:T(1024)S(1)} %get-tuple-element.97, f32[256]{0:T(256)S(1)} %multiply_reduce_fusion.5, ...), kind=kOutput, calls=%fused_computation.6.clone.1 | convolution fusion | flops 144703488 | bytes 4769792 | tf_op jit(solution)/shard_map/while/body/eval_jaxpr/dot_general | solution.py:19
  46.6 5.3 %fusion.22 = bf16[8,256,8192]{2,1,0:T(8,128)(2,1)} fusion(bf16[8,256,8192]{2,1,0:T(8,128)(2,1)} %get-tuple-element.89, s32[]{:T(128)} %get-tuple-element.88, bf16[32,8192]{1,0:T(8,128)(2,1)} %get-tuple-element.98, f32[8192]{0:T(1024)S(1)} %get-tuple-element.97, f32[256]{0:T(256)S(1)} %multiply_reduce_fusion.5, ...), kind=kOutput, calls=%fused_computation.6.clone.1 | convolution fusion | flops 144703488 | bytes 4769792 | tf_op jit(solution)/shard_map/while/body/eval_jaxpr/dot_general | solution.py:19
  51.9 0.0 copy-done
  51.9 0.0 copy-start.1
  51.9 16.0 %fusion.9 = bf16[16,2048]{0,1:T(8,128)(2,1)} fusion(bf16[2048,8192]{1,0:T(8,128)(2,1)} %bitcast.27, f32[16,8192]{1,0:T(8,128)S(1)} %copy-done), kind=kOutput, calls=%fused_computation.12 | convolution fusion | flops 537034752 | bytes 34144256 | tf_op jit(solution)/shard_map/dot_general | solution.py:31
  67.9 0.0 all-reduce.4.cloned.1.call-update
  67.9 0.0 all-reduce.6.cloned.1.call-start
  68.0 21.5 %all-reduce.4.cloned.1.call-done = bf16[16,2048]{0,1:T(8,128)(2,1)} async-done(((bf16[16,2048]{0,1:T(8,128)(2,1)}), bf16[16,2048]{0,1:T(8,128)(2,1)}) %all-reduce.4.cloned.1.call-update) | async-done | bytes 65552 | tf_op jit(solution)/shard_map/psum | solution.py:34
  89.5 16.0 %fusion.12 = f32[16,8192]{1,0:T(8,128)} fusion(bf16[16,2048]{0,1:T(8,128)(2,1)} %all-reduce.4.cloned.1.call-done, bf16[2048,8192]{1,0:T(8,128)(2,1)} %bitcast.28), kind=kOutput, calls=%fused_computation.23 | convolution fusion | flops 536870912 | bytes 34144256 | tf_op jit(solution)/shard_map/dot_general | solution.py:35
  105.5 0.0 all-reduce.6.cloned.1.call-update
  105.5 0.0 copy-done.1
  105.5 0.0 copy-done.4
  105.5 0.2 multiply_reduce_fusion.3
  105.7 109.4 %all-reduce.6.cloned.1.call-done = f32[16,8192]{1,0:T(8,128)} async-done(((f32[16,8192]{1,0:T(8,128)}), f32[16,8192]{1,0:T(8,128)}) %all-reduce.6.cloned.1.call-update) | async-done | bytes 524304 | tf_op jit(solution)/shard_map/psum | solution.py:38
  215.1 1.2 multiply_reduce_fusion.2
  216.4 2.5 %all-reduce = (f32[16]{0:T(128)S(1)}, f32[16]{0:T(128)S(1)}) all-reduce(f32[16]{0:T(128)S(1)} %multiply_reduce_fusion.3, f32[16]{0:T(128)S(1)} %multiply_reduce_fusion.2), channel_id=1, replica_groups=mesh['pts'=16,'ctr'=2] {'ctr'}, use_global_device_ids=true, to_apply=%region_1.2 | all-reduce | flops 32 | bytes 256 | tf_op jit(solution)/shard_map/psum | solution.py:41
  218.8 0.0 copy-done.3
  218.8 2.2 fusion.10
  221.0 2.5 %psum.39 = f32[16]{0:T(128)S(1)} all-reduce(f32[16]{0:T(128)S(1)} %get-tuple-element.48), channel_id=1, replica_groups=mesh['pts'=16,'ctr'=2] {'ctr'}, use_global_device_ids=true, to_apply=%region_11.12 | all-reduce | flops 16 | bytes 128 | tf_op jit(solution)/shard_map/psum | solution.py:46
  223.5 0.9 multiply_add_fusion
  224.4 0.0 copy-done.2
  (15 shorter events, 0.3 us)
Async XLA Ops:
  7.2 44.7 %copy-start = (f32[16,8192]{1,0:T(8,128)S(1)}, f32[16,8192]{1,0:T(8,128)}, u32[]{:S(2)}) copy-start(f32[16,8192]{1,0:T(8,128)} %param.12) | copy-start | bytes 1572868
  7.2 82.3 %all-reduce.4.cloned.1.call-start = ((), (), s32[]{:S(2)}) async-start(), calls=%async_computation | async-start | bytes 1048576 | tf_op jit(solution)/shard_map/psum | solution.py:34
  51.9 53.6 %copy-start.1 = (f32[16,8192]{1,0:T(8,128)S(1)}, f32[16,8192]{1,0:T(8,128)}, u32[]{:S(2)}) copy-start(f32[16,8192]{1,0:T(8,128)} %param.11) | copy-start | bytes 1572868
  51.9 53.6 %copy-start.4 = (f32[8192]{0:T(1024)S(1)}, f32[8192]{0:T(1024)}, u32[]{:S(2)}) copy-start(f32[8192]{0:T(1024)} %param.13) | copy-start | bytes 98308
  51.9 166.9 %copy-start.3 = (f32[16,8192]{1,0:T(8,128)S(1)}, f32[16,8192]{1,0:T(8,128)}, u32[]{:S(2)}) copy-start(f32[16,8192]{1,0:T(8,128)} %param.10) | copy-start | bytes 1572868
  67.9 147.2 %all-reduce.6.cloned.1.call-start = ((), (), s32[]{:S(2)}) async-start(), calls=%async_computation.1 | async-start | bytes 1048576 | tf_op jit(solution)/shard_map/psum | solution.py:38
  221.0 3.4 %copy-start.2 = (f32[16,8192]{1,0:T(8,128)}, f32[16,8192]{1,0:T(8,128)S(1)}, u32[]{:S(2)}) copy-start(f32[16,8192]{1,0:T(8,128)S(1)} %get-tuple-element.49) | copy-start | bytes 1572868
Sparse Core Ops, SparseCore 0:
  68.0 21.4 all-reduce.3
  105.6 109.4 all-reduce.5
where the time goes:
time: 232 us; the launch traced here: 231 us
  waiting for transfers between devices  131 us (56%)
  matrix products  74.2 us (32%)
  between operations  14.1 us (6%)
  other arithmetic  5.95 us (3%)
  blocking collectives  4.93 us (2%)
    psum x1, waiting for transfers between devices, shards(): colsum = lax.psum(col_part, 'pts')  109 us
    dot_general x8, matrix products, one_block(): lax.dot_general(block, centres, (((0,), (0,)), ((), ())), preferred_eleme...  42.2 us
    psum x1, waiting for transfers between devices, shards(): fitted = lax.psum(fit_part.astype(jnp.bfloat16), 'ctr')  21.5 us
    dot_general x1, matrix products, shards(): col_part = jnp.dot(fitted, kern, preferred_element_type=jnp.float32)  16 us
    dot_general x1, matrix products, shards(): lax.dot_general(dirb, kern, (((1,), (1,)), ((), ())), preferred_element_t...  16 us
  transfers between devices with their start and end apart: 2, of which 2 were waited for; matrix products, arithmetic and copies ran while one was open for 0% of the time, Pallas kernels for 0%

commit v1 on v0

v1 whole, which is shorter than its diff:
```python
import functools
import math

import jax
import jax.numpy as jnp
from jax import lax
from jax.experimental import pallas as pl
from jax.experimental.pallas import tpu as pltpu
from jax.sharding import PartitionSpec as P

MIB = 2**20
F32 = jnp.float32
BF16 = jnp.bfloat16
RATE = 0.25 * math.log2(math.e)
DEPTH = 128
VMEM = pl.BlockSpec(memory_space=pltpu.VMEM)


def tile_of(index, size):
    return pl.ds(pl.multiple_of(index * size, size), size)


def split3(value):
    first = value.astype(BF16).astype(F32)
    rest = value - first
    second = rest.astype(BF16).astype(F32)
    return first, second, rest - second


def rows_of(rows, block):
    at = lax.broadcasted_iota(jnp.int32, block, 0)
    out = jnp.zeros(block, F32)
    for i, row in enumerate(rows):
        out = jnp.where(at == i, row, out)
    return out


def fit_kernel(parts, width, pts_ref, cen_ref, dir_ref, *refs):
    kern, (fit_ref, xa_ref, ca_ref, db_ref) = refs[:parts], refs[parts:]
    feat, num = pts_ref.shape
    ctr = cen_ref.shape[1]
    pts = pts_ref[...].astype(F32)
    terms = list(split3(pts * RATE))
    norm = split3(jnp.sum(pts * pts, axis=0, keepdims=True) * (-0.5 * RATE))
    terms.append(rows_of(list(norm) + [1.0, 1.0, 1.0], (DEPTH - 3 * feat, num)))
    xa_ref[...] = jnp.concatenate(terms, axis=0).T.astype(BF16)
    cen = cen_ref[...]
    for i in range(3):
        ca_ref[i * feat : (i + 1) * feat, :] = cen
    cen = cen.astype(F32)
    norm = split3(jnp.sum(cen * cen, axis=0, keepdims=True) * (-0.5 * RATE))
    ca_ref[3 * feat :, :] = rows_of([1.0, 1.0, 1.0] + list(norm), (DEPTH - 3 * feat, ctr)).astype(BF16)
    db_ref[...] = dir_ref[...].astype(BF16)
    rows = num // parts

    def body(j, acc):
        col = tile_of(j, width)
        out = []
        for p in range(parts):
            logk = jnp.dot(xa_ref[p * rows : (p + 1) * rows, :], ca_ref[:, col], preferred_element_type=F32)
            tile = jnp.exp2(logk).astype(BF16)
            kern[p][:, col] = tile
            out.append(lax.dot_general(db_ref[:, col], tile, (((1,), (1,)), ((), ())), preferred_element_type=F32))
        return acc + jnp.concatenate(out, axis=1)

    acc = lax.fori_loop(0, ctr // width, body, jnp.zeros(fit_ref.shape, F32))
    fit_ref[...] = acc.astype(BF16)


def col_kernel(parts, groups, width, *refs):
    fits, kern, (out_ref,) = refs[:groups], refs[groups : groups + parts], refs[groups + parts :]
    fitted = fits[0][...].astype(F32)
    for ref in fits[1:]:
        fitted = fitted + ref[...].astype(F32)
    fitted = fitted.astype(BF16)
    rows = kern[0].shape[0]
    steps = out_ref.shape[2] // width
    for chunk in range(out_ref.shape[0]):

        @pl.loop(0, steps)
        def _(j):
            col = tile_of(chunk * steps + j, width)
            acc = None
            for p in range(parts):
                term = jnp.dot(fitted[:, p * rows : (p + 1) * rows], kern[p][:, col], preferred_element_type=F32)
                acc = term if acc is None else acc + term
            out_ref[chunk, :, tile_of(j, width)] = acc


def width_of(size, most):
    width = most
    while size % width:
        width //= 2
    return width


def fit_parts(points, centres, direction, parts):
    num, ctr = points.shape[1], centres.shape[1]
    targets = direction.shape[0]
    out = pl.pallas_call(
        functools.partial(fit_kernel, parts, width_of(ctr, 1024)),
        out_shape=[jax.ShapeDtypeStruct((num // parts, ctr), BF16)] * parts + [jax.ShapeDtypeStruct((targets, num), BF16)],
        in_specs=[VMEM] * 3,
        out_specs=[VMEM] * (parts + 1),
        scratch_shapes=[pltpu.VMEM((num, DEPTH), BF16), pltpu.VMEM((DEPTH, ctr), BF16), pltpu.VMEM((targets, ctr), BF16)],
        compiler_params=pltpu.CompilerParams(vmem_limit_bytes=20 * MIB),
    )(points, centres, direction)
    return out[:parts], out[parts]


def col_sums(fits, kern, chunks):
    targets = fits[0].shape[0]
    ctr = kern[0].shape[1]
    size = ctr // chunks
    return pl.pallas_call(
        functools.partial(col_kernel, len(kern), len(fits), width_of(size, 1024)),
        out_shape=jax.ShapeDtypeStruct((chunks, targets, size), F32),
        in_specs=[VMEM] * (len(fits) + len(kern)),
        out_specs=VMEM,
        compiler_params=pltpu.CompilerParams(vmem_limit_bytes=8 * MIB),
    )(*fits, *kern)


def radices(size):
    out, prime = [], 2
    while size > 1:
        while size % prime == 0:
            out.append(prime)
            size //= prime
        prime += 1
    return out


def sum_over_pts(chunks):
    num_pts, num_ctr = lax.axis_size("pts"), lax.axis_size("ctr")
    me, odd = lax.axis_index("pts"), lax.axis_index("ctr") % 2

    def send(value, partner):
        pairs = [
            (p * num_ctr + c, partner(p, c % 2) * num_ctr + c) for p in range(num_pts) for c in range(num_ctr)
        ]
        return lax.ppermute(value, ("pts", "ctr"), pairs)

    def bit(phase, odd):
        return 1 + (odd ^ phase)

    digit = [(me // (1 + (odd ^ phase))) % 2 for phase in range(2)]
    value = chunks
    for phase in range(2):
        half = value.reshape((2, value.shape[0] // 2) + value.shape[1:])
        keep = lax.dynamic_index_in_dim(half, digit[phase], 0, False)
        give = lax.dynamic_index_in_dim(half, 1 - digit[phase], 0, False)
        value = keep + send(give, lambda p, c: p ^ bit(phase, c))
    stride = 4
    for radix in radices(num_pts // 4):
        mine = (me // stride) % radix
        got = [value]
        for k in range(1, radix):

            def partner(p, c):
                d = (p // stride) % radix
                return p + ((d + k) % radix - d) * stride

            got.append(send(value, partner))
        if radix == 2:
            value = got[0] + got[1]
        else:
            stack = jnp.stack(got)
            value = sum(lax.dynamic_index_in_dim(stack, (mine - d) % radix, 0, False) for d in range(radix))
        stride *= radix
    for phase in (1, 0):
        other = send(value, lambda p, c: p ^ bit(phase, c))
        pair = (jnp.concatenate([value, other]), jnp.concatenate([other, value]))
        value = jnp.where(digit[phase] == 0, pair[0], pair[1])
    return value


def shards(points, centres, coef, resid, direction, precond):
    num_pts, num_ctr = lax.axis_size("pts"), lax.axis_size("ctr")
    num, ctr = points.shape[1], centres.shape[1]
    parts = 4
    kern, part = fit_parts(points, centres, direction, parts)
    fits = [part]
    for k in range(1, num_ctr):
        fits.append(lax.ppermute(part, "ctr", [(c, (c + k) % num_ctr) for c in range(num_ctr)]))
    if num_ctr > 2:
        stack = jnp.stack(fits)
        fits = [
            lax.dynamic_index_in_dim(stack, (lax.axis_index("ctr") - c) % num_ctr, 0, False) for c in range(num_ctr)
        ]
    chunks = 4
    colsum = sum_over_pts(col_sums(fits, kern, chunks))
    colsum = colsum.transpose(1, 0, 2).reshape(direction.shape)
    scale = 2048.0 / (num * num_pts)
    image = colsum * scale + 0.5 * direction
    rz_part = jnp.sum(resid * resid * precond[None, :], axis=1)
    curv, rz = lax.psum((jnp.sum(direction * image, axis=1), rz_part), "ctr")
    alpha = rz / curv
    coef_next = coef + alpha[:, None] * direction
    resid_next = resid - alpha[:, None] * image
    scaled = precond[None, :] * resid_next
    rz_new = lax.psum(jnp.sum(resid_next * scaled, axis=1), "ctr")
    dir_next = scaled + (rz_new / rz)[:, None] * direction
    return (coef_next, resid_next, dir_next)


def solution(mesh):
    return jax.shard_map(
        shards,
        mesh=mesh,
        in_specs=(
            P(None, "pts"),
            P(None, "ctr"),
            P(None, "ctr"),
            P(None, "ctr"),
            P(None, "ctr"),
            P("ctr"),
        ),
        out_specs=(P(None, "ctr"), P(None, "ctr"), P(None, "ctr")),
        check_vma=False,
    )
```

time: 232 us -> 99.9 us (0.43)
  waiting for transfers between devices: 131 us -> 24.7 us
  matrix products: 74.2 us -> 0 us
  local copies, waits for them, and re-layouts: 1.02 us -> 29.5 us
  Pallas kernels: 0 us -> 22.9 us
  starting transfers between devices: 0.08 us -> 14.3 us
  between operations: 14.1 us -> 0.74 us
  other arithmetic: 5.95 us -> 2.44 us
    psum x2 -> x0, waiting for transfers between devices: 131 us -> none  [the longest x1 109 us: shards(): colsum = lax.psum(col_part, 'pts')]
    dot_general x10 -> x0, matrix products: 74.2 us -> none  [the longest x8 42.2 us: one_block(): lax.dot_general(block, centres, (((0,), (0,)), ((), ())), preferred_eleme...]
    unnamed x11 -> x32, local copies, waits for them, and re-layouts: 1 us -> 29.4 us
    ppermute x0 -> x7, waiting for transfers between devices: none -> 24.7 us  [the longest x6 23.8 us: send(): return lax.ppermute(value, ('pts', 'ctr'), pairs)]
    pallas_call x0 -> x2, Pallas kernels: none -> 22.9 us  [the longest x1 17.7 us: fit_parts(): pl.pallas_call(functools.partial(fit_kernel, parts, width_of(ctr, 1024)),...]
    ppermute x0 -> x7, starting transfers between devices: none -> 14.3 us  [the longest x6 13.8 us: send(): return lax.ppermute(value, ('pts', 'ctr'), pairs)]
  transfers between devices with their start and end apart: 2 -> 7, of which waited for: 2 -> 7; matrix products, arithmetic and copies ran while one was open for 0% -> 0% of each run, Pallas kernels for 0% -> 0%
where the time goes in v1:
time: 99.9 us; the launch traced here: 99.5 us
  local copies, waits for them, and re-layouts  29.5 us (30%)
  waiting for transfers between devices  24.7 us (25%)
  Pallas kernels  22.9 us (23%)
  starting transfers between devices  14.3 us (14%)
  blocking collectives  4.93 us (5%)
  other arithmetic  2.44 us (2%)
    unnamed x32, local copies, waits for them, and re-layouts  29.4 us
    ppermute x6, waiting for transfers between devices, send(): return lax.ppermute(value, ('pts', 'ctr'), pairs)  23.8 us
    pallas_call x1, Pallas kernels, fit_parts(): pl.pallas_call(functools.partial(fit_kernel, parts, width_of(ctr, 1024)),...  17.7 us
    ppermute x6, starting transfers between devices, send(): return lax.ppermute(value, ('pts', 'ctr'), pairs)  13.8 us
    pallas_call x1, Pallas kernels, col_sums(): pl.pallas_call(functools.partial(col_kernel, len(kern), len(fits), width_...  5.26 us
    psum x1, blocking collectives, shards(): rz_new = lax.psum(jnp.sum(resid_next * scaled, axis=1), 'ctr')  2.47 us
    psum x1, blocking collectives, shards(): curv, rz = lax.psum((jnp.sum(direction * image, axis=1), rz_part), 'ctr')  2.46 us
  transfers between devices with their start and end apart: 7, of which 7 were waited for; matrix products, arithmetic and copies ran while one was open for 0% of the time, Pallas kernels for 0%

profile of v1, /device:TPU:0, one launch (start us, length us, event | category | flops | bytes accessed | tf_op | source)
XLA Modules:
  0.0 99.5 jit_solution(1824193367445310969)
XLA Ops:
  0.6 1.0 %copy-done = f32[16,8192]{1,0:T(8,128)S(1)} copy-done((f32[16,8192]{1,0:T(8,128)S(1)}, f32[16,8192]{1,0:T(8,128)}, u32[]{:S(2)}) %copy-start) | copy-done | bytes 524312
  1.7 1.0 %copy-done.10 = bf16[32,8192]{1,0:T(8,128)(2,1)S(1)} copy-done((bf16[32,8192]{1,0:T(8,128)(2,1)S(1)}, bf16[32,8192]{1,0:T(8,128)(2,1)}, u32[]{:S(2)}) %copy-start.10) | copy-done | bytes 524312
  2.7 0.9 copy-done.11
  3.6 17.7 %shard_map.85 = (bf16[512,8192]{1,0:T(8,128)(2,1)S(1)}, bf16[512,8192]{1,0:T(8,128)(2,1)S(1)}, bf16[512,8192]{1,0:T(8,128)(2,1)S(1)}, bf16[512,8192]{1,0:T(8,128)(2,1)S(1)}, bf16[16,2048]{1,0:T(8,128)(2,1)S(1)}) custom-call(bf16[32,2048]{1,0:T(8,128)(2,1)S(1)} %copy-done.11, bf16[32,8192]{1,0:T(8,128)(2,1)S(1)} %copy-done.10, f32[16,8192]{1,0:T(8,128)S(1)} %copy-done), custom_call_target="tpu_custom_call" | custom-call | tf_op jit(solution)/shard_map/pallas_call | solution.py:100
  21.3 3.2 %copy-done.2 = bf16[512,8192]{1,0:T(8,128)(2,1)} copy-done((bf16[512,8192]{1,0:T(8,128)(2,1)}, bf16[512,8192]{1,0:T(8,128)(2,1)S(1)}, u32[]{:S(2)}) %copy-start.2) | copy-done | bytes 8388632
  24.5 3.2 %copy-done.4 = bf16[512,8192]{1,0:T(8,128)(2,1)} copy-done((bf16[512,8192]{1,0:T(8,128)(2,1)}, bf16[512,8192]{1,0:T(8,128)(2,1)S(1)}, u32[]{:S(2)}) %copy-start.4) | copy-done | bytes 8388632
  27.8 3.2 %copy-done.6 = bf16[512,8192]{1,0:T(8,128)(2,1)} copy-done((bf16[512,8192]{1,0:T(8,128)(2,1)}, bf16[512,8192]{1,0:T(8,128)(2,1)S(1)}, u32[]{:S(2)}) %copy-start.6) | copy-done | bytes 8388632
  31.0 3.2 %copy-done.8 = bf16[512,8192]{1,0:T(8,128)(2,1)} copy-done((bf16[512,8192]{1,0:T(8,128)(2,1)}, bf16[512,8192]{1,0:T(8,128)(2,1)S(1)}, u32[]{:S(2)}) %copy-start.8) | copy-done | bytes 8388632
  34.2 0.5 collective-permute-start
  34.6 0.9 collective-permute-done.refs_1_
  35.5 3.4 %copy-done.3 = bf16[512,8192]{1,0:T(8,128)(2,1)S(1)} copy-done((bf16[512,8192]{1,0:T(8,128)(2,1)S(1)}, bf16[512,8192]{1,0:T(8,128)(2,1)}, u32[]{:S(2)}) %copy-start.3) | copy-done | bytes 8388632
  38.9 3.4 %copy-done.5 = bf16[512,8192]{1,0:T(8,128)(2,1)S(1)} copy-done((bf16[512,8192]{1,0:T(8,128)(2,1)S(1)}, bf16[512,8192]{1,0:T(8,128)(2,1)}, u32[]{:S(2)}) %copy-start.5) | copy-done | bytes 8388632
  42.3 3.4 %copy-done.7 = bf16[512,8192]{1,0:T(8,128)(2,1)S(1)} copy-done((bf16[512,8192]{1,0:T(8,128)(2,1)S(1)}, bf16[512,8192]{1,0:T(8,128)(2,1)}, u32[]{:S(2)}) %copy-start.7) | copy-done | bytes 8388632
  45.7 3.4 %copy-done.9 = bf16[512,8192]{1,0:T(8,128)(2,1)S(1)} copy-done((bf16[512,8192]{1,0:T(8,128)(2,1)S(1)}, bf16[512,8192]{1,0:T(8,128)(2,1)}, u32[]{:S(2)}) %copy-start.9) | copy-done | bytes 8388632
  49.1 5.3 %shard_map.86 = f32[4,16,2048]{2,1,0:T(8,128)S(1)} custom-call(bf16[16,2048]{1,0:T(8,128)(2,1)S(1)} %get-tuple-element.8.refs_0_, bf16[16,2048]{1,0:T(8,128)(2,1)S(1)} %collective-permute-done.refs_1_, bf16[512,8192]{1,0:T(8,128)(2,1)S(1)} %copy-done.3, bf16[512,8192]{1,0:T(8,128)(2,1)S(1)} %copy-done.5, bf16[512,8192]{1,0:T(8,128)(2,1)S(1)} %copy-done.7, ...), custom_call_target="tpu_custom_call" | custom-call | tf_op jit(solution)/shard_map/pallas_call | solution.py:115
  54.4 2.9 %collective-permute-start.1 = (f32[2,16,2048]{2,1,0:T(8,128)S(1)}, f32[2,16,2048]{2,1,0:T(8,128)S(1)}, u32[]{:S(2)}, u32[]{:S(2)}) collective-permute-start(f32[2,16,2048]{2,1,0:T(8,128)S(1)} %dynamic-slice_bitcast_fusion), channel_id=1, source_target_pairs={{0,2},{1,5},{2,0},{3,7},{4,6},{5,1},{6,4},{7,3},{8,10},{9,13},{10,... | collective-permute-start | bytes 786440 | tf_op jit(solution)/shard_map/ppermute | solution.py:142
  57.3 4.4 %collective-permute-done.1 = f32[2,16,2048]{2,1,0:T(8,128)S(1)} collective-permute-done((f32[2,16,2048]{2,1,0:T(8,128)S(1)}, f32[2,16,2048]{2,1,0:T(8,128)S(1)}, u32[]{:S(2)}, u32[]{:S(2)}) %collective-permute-start.1) | collective-permute-done | bytes 262176 | tf_op jit(solution)/shard_map/ppermute | solution.py:142
  61.7 2.1 %collective-permute-start.2 = (f32[1,16,2048]{2,1,0:T(8,128)S(1)}, f32[1,16,2048]{2,1,0:T(8,128)S(1)}, u32[]{:S(2)}, u32[]{:S(2)}) collective-permute-start(f32[1,16,2048]{2,1,0:T(8,128)S(1)} %constant_dynamic-slice_fusion), channel_id=1, source_target_pairs={{0,4},{1,3},{2,6},{3,1},{4,0},{5,7},{6,2},{7,5},{8,12},{9,11},{10,... | collective-permute-start | bytes 393224 | tf_op jit(solution)/shard_map/ppermute | solution.py:142
  63.8 2.9 %collective-permute-done.2 = f32[1,16,2048]{2,1,0:T(8,128)S(1)} collective-permute-done((f32[1,16,2048]{2,1,0:T(8,128)S(1)}, f32[1,16,2048]{2,1,0:T(8,128)S(1)}, u32[]{:S(2)}, u32[]{:S(2)}) %collective-permute-start.2) | collective-permute-done | bytes 131104 | tf_op jit(solution)/shard_map/ppermute | solution.py:142
  66.8 2.2 %collective-permute-start.3 = (f32[1,16,2048]{2,1,0:T(8,128)S(1)}, f32[1,16,2048]{2,1,0:T(8,128)S(1)}, u32[]{:S(2)}, u32[]{:S(2)}) collective-permute-start(f32[1,16,2048]{2,1,0:T(8,128)S(1)} %dynamic-slice_add_fusion), channel_id=1, source_target_pairs={{0,8},{1,9},{2,10},{3,11},{4,12},{5,13},{6,14},{7,15},{8,0},{9,1},... | collective-permute-start | bytes 393224 | tf_op jit(solution)/shard_map/ppermute | solution.py:142
  69.0 2.9 %collective-permute-done.3 = f32[1,16,2048]{2,1,0:T(8,128)S(1)} collective-permute-done((f32[1,16,2048]{2,1,0:T(8,128)S(1)}, f32[1,16,2048]{2,1,0:T(8,128)S(1)}, u32[]{:S(2)}, u32[]{:S(2)}) %collective-permute-start.3) | collective-permute-done | bytes 131104 | tf_op jit(solution)/shard_map/ppermute | solution.py:142
  71.9 3.4 %collective-permute-start.4 = (f32[1,16,2048]{2,1,0:T(8,128)S(1)}, f32[1,16,2048]{2,1,0:T(8,128)S(1)}, u32[]{:S(2)}, u32[]{:S(2)}) collective-permute-start(f32[1,16,2048]{2,1,0:T(8,128)S(1)} %add.72), channel_id=1, source_target_pairs={{0,16},{1,17},{2,18},{3,19},{4,20},{5,21},{6,22},{7,23},{8,24},{9,... | collective-permute-start | bytes 393224 | tf_op jit(solution)/shard_map/ppermute | solution.py:142
  75.4 4.4 %collective-permute-done.4 = f32[1,16,2048]{2,1,0:T(8,128)S(1)} collective-permute-done((f32[1,16,2048]{2,1,0:T(8,128)S(1)}, f32[1,16,2048]{2,1,0:T(8,128)S(1)}, u32[]{:S(2)}, u32[]{:S(2)}) %collective-permute-start.4) | collective-permute-done | bytes 131104 | tf_op jit(solution)/shard_map/ppermute | solution.py:142
  79.8 1.7 %collective-permute-start.5 = (f32[1,16,2048]{2,1,0:T(8,128)S(1)}, f32[1,16,2048]{2,1,0:T(8,128)S(1)}, u32[]{:S(2)}, u32[]{:S(2)}) collective-permute-start(f32[1,16,2048]{2,1,0:T(8,128)S(1)} %add.73), channel_id=1, source_target_pairs={{0,4},{1,3},{2,6},{3,1},{4,0},{5,7},{6,2},{7,5},{8,12},{9,11},{10,... | collective-permute-start | bytes 393224 | tf_op jit(solution)/shard_map/ppermute | solution.py:142
  81.4 4.2 %collective-permute-done.5 = f32[1,16,2048]{2,1,0:T(8,128)S(1)} collective-permute-done((f32[1,16,2048]{2,1,0:T(8,128)S(1)}, f32[1,16,2048]{2,1,0:T(8,128)S(1)}, u32[]{:S(2)}, u32[]{:S(2)}) %collective-permute-start.5) | collective-permute-done | bytes 131104 | tf_op jit(solution)/shard_map/ppermute | solution.py:142
  85.7 1.5 %collective-permute-start.6 = (f32[2,16,2048]{2,1,0:T(8,128)S(1)}, f32[2,16,2048]{2,1,0:T(8,128)S(1)}, u32[]{:S(2)}, u32[]{:S(2)}) collective-permute-start(f32[2,16,2048]{2,1,0:T(8,128)S(1)} %maximum_select_fusion.1), channel_id=1, source_target_pairs={{0,2},{1,5},{2,0},{3,7},{4,6},{5,1},{6,4},{7,3},{8,10},{9,13},{10,... | collective-permute-start | bytes 786440 | tf_op jit(solution)/shard_map/ppermute | solution.py:142
  87.2 4.9 %collective-permute-done.6 = f32[2,16,2048]{2,1,0:T(8,128)S(1)} collective-permute-done((f32[2,16,2048]{2,1,0:T(8,128)S(1)}, f32[2,16,2048]{2,1,0:T(8,128)S(1)}, u32[]{:S(2)}, u32[]{:S(2)}) %collective-permute-start.6) | collective-permute-done | bytes 262176 | tf_op jit(solution)/shard_map/ppermute | solution.py:142
  92.3 0.3 multiply_reduce_fusion
  92.5 2.5 %all-reduce = (f32[16]{0:T(128)S(1)}, f32[16]{0:T(128)S(1)}) all-reduce(f32[16]{0:T(128)S(1)} %get-tuple-element.19, f32[16]{0:T(128)S(1)} %get-tuple-element.18), channel_id=1, replica_groups=mesh['pts'=16,'ctr'=2] {'ctr'}, use_global_device_ids=true, to_apply=%region_1.2 | all-reduce | flops 32 | bytes 256 | tf_op jit(solution)/shard_map/psum | solution.py:197
  95.0 1.1 %fusion = (f32[16]{0:T(128)S(1)}, f32[16,8192]{1,0:T(8,128)S(1)}, f32[16,8192]{1,0:T(8,128)}) fusion(f32[8192]{0:T(1024)S(1)} %copy-done.15, f32[16,8192]{1,0:T(8,128)S(1)} %copy-done.13, f32[16,8192]{1,0:T(8,128)S(1)} %bitcast.12, f32[16,8192]{1,0:T(8,128)S(1)} %copy-done.1, f32[16]{0:T(128)S(1)} %div.15, f32[16,8192]{1,0:T(8,128)S(1)} %copy-done.14), kind=kLoop, calls=%fused_computation.2 | loop fusion | flops 1179632 | bytes 3178624 | tf_op jit(solution)/shard_map/reduce_sum | solution.py:202
  96.1 2.5 %psum.23 = f32[16]{0:T(128)S(1)} all-reduce(f32[16]{0:T(128)S(1)} %get-tuple-element.15), channel_id=1, replica_groups=mesh['pts'=16,'ctr'=2] {'ctr'}, use_global_device_ids=true, to_apply=%region_5.6 | all-reduce | flops 16 | bytes 128 | tf_op jit(solution)/shard_map/psum | solution.py:202
  98.6 0.9 multiply_add_fusion
  (32 shorter events, 0.3 us)
Async XLA Ops:
  0.6 1.0 %copy-start = (f32[16,8192]{1,0:T(8,128)S(1)}, f32[16,8192]{1,0:T(8,128)}, u32[]{:S(2)}) copy-start(f32[16,8192]{1,0:T(8,128)} %dir_ref.1) | copy-start | bytes 1572868
  1.7 1.0 %copy-start.10 = (bf16[32,8192]{1,0:T(8,128)(2,1)S(1)}, bf16[32,8192]{1,0:T(8,128)(2,1)}, u32[]{:S(2)}) copy-start(bf16[32,8192]{1,0:T(8,128)(2,1)} %cen_ref.1) | copy-start | bytes 1572868
  2.7 0.9 copy-start.11
  21.3 3.2 %copy-start.2 = (bf16[512,8192]{1,0:T(8,128)(2,1)}, bf16[512,8192]{1,0:T(8,128)(2,1)S(1)}, u32[]{:S(2)}) copy-start(bf16[512,8192]{1,0:T(8,128)(2,1)S(1)} %get-tuple-element.9.refs_2_) | copy-start | bytes 25165828
  24.5 3.2 %copy-start.4 = (bf16[512,8192]{1,0:T(8,128)(2,1)}, bf16[512,8192]{1,0:T(8,128)(2,1)S(1)}, u32[]{:S(2)}) copy-start(bf16[512,8192]{1,0:T(8,128)(2,1)S(1)} %get-tuple-element.10.refs_3_) | copy-start | bytes 25165828
  27.7 3.2 %copy-start.6 = (bf16[512,8192]{1,0:T(8,128)(2,1)}, bf16[512,8192]{1,0:T(8,128)(2,1)S(1)}, u32[]{:S(2)}) copy-start(bf16[512,8192]{1,0:T(8,128)(2,1)S(1)} %get-tuple-element.11.refs_4_) | copy-start | bytes 25165828
  31.0 3.2 %copy-start.8 = (bf16[512,8192]{1,0:T(8,128)(2,1)}, bf16[512,8192]{1,0:T(8,128)(2,1)S(1)}, u32[]{:S(2)}) copy-start(bf16[512,8192]{1,0:T(8,128)(2,1)S(1)} %get-tuple-element.12.refs_5_) | copy-start | bytes 25165828
  34.2 1.4 %collective-permute-start = (bf16[16,2048]{1,0:T(8,128)(2,1)S(1)}, bf16[16,2048]{1,0:T(8,128)(2,1)S(1)}, u32[]{:S(2)}, u32[]{:S(2)}) collective-permute-start(bf16[16,2048]{1,0:T(8,128)(2,1)S(1)} %get-tuple-element.8.refs_0_), channel_id=1, source_target_pairs={{0,1},{1,0},{2,3},{3,2},{4,5},{5,4},{6,7},{7,6},{8,9},{9,8},{10,11... | collective-permute-start | bytes 196616 | tf_op jit(solution)/shard_map/ppermute | solution.py:185
  35.5 3.4 %copy-start.3 = (bf16[512,8192]{1,0:T(8,128)(2,1)S(1)}, bf16[512,8192]{1,0:T(8,128)(2,1)}, u32[]{:S(2)}) copy-start(bf16[512,8192]{1,0:T(8,128)(2,1)} %copy-done.2) | copy-start | bytes 25165828
  38.9 3.4 %copy-start.5 = (bf16[512,8192]{1,0:T(8,128)(2,1)S(1)}, bf16[512,8192]{1,0:T(8,128)(2,1)}, u32[]{:S(2)}) copy-start(bf16[512,8192]{1,0:T(8,128)(2,1)} %copy-done.4) | copy-start | bytes 25165828
  42.3 3.4 %copy-start.7 = (bf16[512,8192]{1,0:T(8,128)(2,1)S(1)}, bf16[512,8192]{1,0:T(8,128)(2,1)}, u32[]{:S(2)}) copy-start(bf16[512,8192]{1,0:T(8,128)(2,1)} %copy-done.6) | copy-start | bytes 25165828
  45.7 3.4 %copy-start.9 = (bf16[512,8192]{1,0:T(8,128)(2,1)S(1)}, bf16[512,8192]{1,0:T(8,128)(2,1)}, u32[]{:S(2)}) copy-start(bf16[512,8192]{1,0:T(8,128)(2,1)} %copy-done.8) | copy-start | bytes 25165828
  49.1 43.2 %copy-start.1 = (f32[16,8192]{1,0:T(8,128)S(1)}, f32[16,8192]{1,0:T(8,128)}, u32[]{:S(2)}) copy-start(f32[16,8192]{1,0:T(8,128)} %dir_ref.1) | copy-start | bytes 1572868
  49.1 43.2 %copy-start.13 = (f32[16,8192]{1,0:T(8,128)S(1)}, f32[16,8192]{1,0:T(8,128)}, u32[]{:S(2)}) copy-start(f32[16,8192]{1,0:T(8,128)} %param.9) | copy-start | bytes 1572868
  49.1 43.2 %copy-start.15 = (f32[8192]{0:T(1024)S(1)}, f32[8192]{0:T(1024)}, u32[]{:S(2)}) copy-start(f32[8192]{0:T(1024)} %param.11) | copy-start | bytes 98308
  49.1 45.9 %copy-start.14 = (f32[16,8192]{1,0:T(8,128)S(1)}, f32[16,8192]{1,0:T(8,128)}, u32[]{:S(2)}) copy-start(f32[16,8192]{1,0:T(8,128)} %param.8) | copy-start | bytes 1572868
  54.4 7.3 %collective-permute-start.1 = (f32[2,16,2048]{2,1,0:T(8,128)S(1)}, f32[2,16,2048]{2,1,0:T(8,128)S(1)}, u32[]{:S(2)}, u32[]{:S(2)}) collective-permute-start(f32[2,16,2048]{2,1,0:T(8,128)S(1)} %dynamic-slice_bitcast_fusion), channel_id=1, source_target_pairs={{0,2},{1,5},{2,0},{3,7},{4,6},{5,1},{6,4},{7,3},{8,10},{9,13},{10,... | collective-permute-start | bytes 786440 | tf_op jit(solution)/shard_map/ppermute | solution.py:142
  61.7 5.1 %collective-permute-start.2 = (f32[1,16,2048]{2,1,0:T(8,128)S(1)}, f32[1,16,2048]{2,1,0:T(8,128)S(1)}, u32[]{:S(2)}, u32[]{:S(2)}) collective-permute-start(f32[1,16,2048]{2,1,0:T(8,128)S(1)} %constant_dynamic-slice_fusion), channel_id=1, source_target_pairs={{0,4},{1,3},{2,6},{3,1},{4,0},{5,7},{6,2},{7,5},{8,12},{9,11},{10,... | collective-permute-start | bytes 393224 | tf_op jit(solution)/shard_map/ppermute | solution.py:142
  66.8 5.1 %collective-permute-start.3 = (f32[1,16,2048]{2,1,0:T(8,128)S(1)}, f32[1,16,2048]{2,1,0:T(8,128)S(1)}, u32[]{:S(2)}, u32[]{:S(2)}) collective-permute-start(f32[1,16,2048]{2,1,0:T(8,128)S(1)} %dynamic-slice_add_fusion), channel_id=1, source_target_pairs={{0,8},{1,9},{2,10},{3,11},{4,12},{5,13},{6,14},{7,15},{8,0},{9,1},... | collective-permute-start | bytes 393224 | tf_op jit(solution)/shard_map/ppermute | solution.py:142
  71.9 7.8 %collective-permute-start.4 = (f32[1,16,2048]{2,1,0:T(8,128)S(1)}, f32[1,16,2048]{2,1,0:T(8,128)S(1)}, u32[]{:S(2)}, u32[]{:S(2)}) collective-permute-start(f32[1,16,2048]{2,1,0:T(8,128)S(1)} %add.72), channel_id=1, source_target_pairs={{0,16},{1,17},{2,18},{3,19},{4,20},{5,21},{6,22},{7,23},{8,24},{9,... | collective-permute-start | bytes 393224 | tf_op jit(solution)/shard_map/ppermute | solution.py:142
  79.8 5.9 %collective-permute-start.5 = (f32[1,16,2048]{2,1,0:T(8,128)S(1)}, f32[1,16,2048]{2,1,0:T(8,128)S(1)}, u32[]{:S(2)}, u32[]{:S(2)}) collective-permute-start(f32[1,16,2048]{2,1,0:T(8,128)S(1)} %add.73), channel_id=1, source_target_pairs={{0,4},{1,3},{2,6},{3,1},{4,0},{5,7},{6,2},{7,5},{8,12},{9,11},{10,... | collective-permute-start | bytes 393224 | tf_op jit(solution)/shard_map/ppermute | solution.py:142
  85.7 6.4 %collective-permute-start.6 = (f32[2,16,2048]{2,1,0:T(8,128)S(1)}, f32[2,16,2048]{2,1,0:T(8,128)S(1)}, u32[]{:S(2)}, u32[]{:S(2)}) collective-permute-start(f32[2,16,2048]{2,1,0:T(8,128)S(1)} %maximum_select_fusion.1), channel_id=1, source_target_pairs={{0,2},{1,5},{2,0},{3,7},{4,6},{5,1},{6,4},{7,3},{8,10},{9,13},{10,... | collective-permute-start | bytes 786440 | tf_op jit(solution)/shard_map/ppermute | solution.py:142
  96.1 3.4 %copy-start.12 = (f32[16,8192]{1,0:T(8,128)}, f32[16,8192]{1,0:T(8,128)S(1)}, u32[]{:S(2)}) copy-start(f32[16,8192]{1,0:T(8,128)S(1)} %get-tuple-element.16) | copy-start | bytes 1572868

commit v2 on v1

v2 whole, which is shorter than its diff:
```python
import functools
import math

import jax
import jax.numpy as jnp
from jax import lax
from jax.experimental import pallas as pl
from jax.experimental.pallas import tpu as pltpu
from jax.sharding import PartitionSpec as P

MIB = 2**20
F32 = jnp.float32
BF16 = jnp.bfloat16
RATE = 0.25 * math.log2(math.e)
DEPTH = 128
VMEM = pl.BlockSpec(memory_space=pltpu.VMEM)


def tile_of(index, size):
    return pl.ds(pl.multiple_of(index * size, size), size)


def split3(value):
    first = value.astype(BF16).astype(F32)
    rest = value - first
    second = rest.astype(BF16).astype(F32)
    return first, second, rest - second


def rows_of(rows, block):
    at = lax.broadcasted_iota(jnp.int32, block, 0)
    out = jnp.zeros(block, F32)
    for i, row in enumerate(rows):
        out = jnp.where(at == i, row, out)
    return out


def fit_kernel(parts, width, pts_ref, cen_ref, dir_ref, *refs):
    kern, (fit_ref, xa_ref, ca_ref, db_ref) = refs[:parts], refs[parts:]
    feat, num = pts_ref.shape
    ctr = cen_ref.shape[1]
    pts = pts_ref[...].astype(F32)
    terms = list(split3(pts * RATE))
    norm = split3(jnp.sum(pts * pts, axis=0, keepdims=True) * (-0.5 * RATE))
    terms.append(rows_of(list(norm) + [1.0, 1.0, 1.0], (DEPTH - 3 * feat, num)))
    xa_ref[...] = jnp.concatenate(terms, axis=0).T.astype(BF16)
    cen = cen_ref[...]
    for i in range(3):
        ca_ref[i * feat : (i + 1) * feat, :] = cen
    cen = cen.astype(F32)
    norm = split3(jnp.sum(cen * cen, axis=0, keepdims=True) * (-0.5 * RATE))
    ca_ref[3 * feat :, :] = rows_of([1.0, 1.0, 1.0] + list(norm), (DEPTH - 3 * feat, ctr)).astype(BF16)
    db_ref[...] = dir_ref[...].astype(BF16)
    rows = num // parts

    def body(j, acc):
        col = tile_of(j, width)
        out = []
        for p in range(parts):
            logk = jnp.dot(xa_ref[p * rows : (p + 1) * rows, :], ca_ref[:, col], preferred_element_type=F32)
            tile = jnp.exp2(logk).astype(BF16)
            kern[p][:, col] = tile
            out.append(lax.dot_general(db_ref[:, col], tile, (((1,), (1,)), ((), ())), preferred_element_type=F32))
        return acc + jnp.concatenate(out, axis=1)

    acc = lax.fori_loop(0, ctr // width, body, jnp.zeros(fit_ref.shape, F32))
    fit_ref[...] = acc.astype(BF16)


def digits():
    me, odd = lax.axis_index("pts"), lax.axis_index("ctr") % 2
    low, high = me % 2, (me // 2) % 2
    return jnp.where(odd == 0, low, high), jnp.where(odd == 0, high, low)


def chunk_ids():
    a, b = digits()
    return 2 * (1 - a) + (1 - b), 2 * (1 - a) + b, 2 * a + (1 - b), 2 * a + b


def col_kernel(parts, groups, width, which, *refs):
    fits, kern, outs = refs[:groups], refs[groups : groups + parts], refs[groups + parts :]
    fitted = fits[0][...].astype(F32)
    for ref in fits[1:]:
        fitted = fitted + ref[...].astype(F32)
    fitted = fitted.astype(BF16)
    rows = kern[0].shape[0]
    steps = outs[0].shape[1] // width
    ids = chunk_ids()
    for i, out in zip(which, outs):

        @pl.loop(0, steps)
        def _(j):
            col = tile_of(ids[i] * steps + j, width)
            acc = None
            for p in range(parts):
                term = jnp.dot(fitted[:, p * rows : (p + 1) * rows], kern[p][:, col], preferred_element_type=F32)
                acc = term if acc is None else acc + term
            out[:, tile_of(j, width)] = acc


def width_of(size, most):
    width = most
    while size % width:
        width //= 2
    return width


def fit_parts(points, centres, direction, parts):
    num, ctr = points.shape[1], centres.shape[1]
    targets = direction.shape[0]
    out = pl.pallas_call(
        functools.partial(fit_kernel, parts, width_of(ctr, 1024)),
        out_shape=[jax.ShapeDtypeStruct((num // parts, ctr), BF16)] * parts + [jax.ShapeDtypeStruct((targets, num), BF16)],
        in_specs=[VMEM] * 3,
        out_specs=[VMEM] * (parts + 1),
        scratch_shapes=[pltpu.VMEM((num, DEPTH), BF16), pltpu.VMEM((DEPTH, ctr), BF16), pltpu.VMEM((targets, ctr), BF16)],
        compiler_params=pltpu.CompilerParams(vmem_limit_bytes=8 * MIB),
    )(points, centres, direction)
    return out[:parts], out[parts]


def col_sums(fits, kern, which):
    targets = fits[0].shape[0]
    size = kern[0].shape[1] // 4
    return pl.pallas_call(
        functools.partial(col_kernel, len(kern), len(fits), width_of(size, 1024), which),
        out_shape=[jax.ShapeDtypeStruct((targets, size), F32)] * len(which),
        in_specs=[VMEM] * (len(fits) + len(kern)),
        out_specs=[VMEM] * len(which),
        compiler_params=pltpu.CompilerParams(vmem_limit_bytes=4 * MIB),
    )(*fits, *kern)


def radices(size):
    out, prime = [], 2
    while size > 1:
        while size % prime == 0:
            out.append(prime)
            size //= prime
        prime += 1
    return out


def send_pts(value, partner):
    num_pts, num_ctr = lax.axis_size("pts"), lax.axis_size("ctr")
    pairs = [(p * num_ctr + c, partner(p, c % 2) * num_ctr + c) for p in range(num_pts) for c in range(num_ctr)]
    return lax.ppermute(value, ("pts", "ctr"), pairs)


def along(phase):
    return lambda p, odd: p ^ (1 + (odd ^ phase))


def sum_over_rest(value):
    me, stride = lax.axis_index("pts"), 4
    for radix in radices(lax.axis_size("pts") // 4):
        got = [value]
        for k in range(1, radix):

            def partner(p, odd):
                d = (p // stride) % radix
                return p + ((d + k) % radix - d) * stride

            got.append(send_pts(value, partner))
        if radix == 2:
            value = got[0] + got[1]
        else:
            mine, stack = (me // stride) % radix, jnp.stack(got)
            value = sum(lax.dynamic_index_in_dim(stack, (mine - d) % radix, 0, False) for d in range(radix))
        stride *= radix
    return value


def over_ctr(value):
    num_ctr = lax.axis_size("ctr")
    return [value] + [
        lax.ppermute(value, "ctr", [(c, (c + k) % num_ctr) for c in range(num_ctr)]) for k in range(1, num_ctr)
    ]


def total(refs):
    value = refs[0][...]
    for ref in refs[1:]:
        value = value + ref[...]
    return value[:, :1]


def image_kernel(scale, *refs):
    chunks, (dir_ref, res_ref, pre_ref, image_ref, curv_ref, rz_ref) = refs[:4], refs[4:]
    size = chunks[0].shape[1]
    curv = jnp.zeros(curv_ref.shape, F32)
    for chunk, i in zip(chunks, chunk_ids()):
        col = tile_of(i, size)
        direction = dir_ref[:, col]
        image = chunk[...] * scale + 0.5 * direction
        image_ref[:, col] = image
        curv = curv + jnp.sum(direction * image, axis=1, keepdims=True)
    curv_ref[...] = curv
    resid = res_ref[...]
    rz_ref[...] = jnp.zeros(rz_ref.shape, F32) + jnp.sum(resid * resid * pre_ref[...], axis=1, keepdims=True)


def step_kernel(groups, *refs):
    curvs, rzs = refs[:groups], refs[groups : 2 * groups]
    image_ref, dir_ref, res_ref, pre_ref, coef_ref, coef_out, res_out, new_ref = refs[2 * groups :]
    alpha = total(rzs) / total(curvs)
    coef_out[...] = coef_ref[...] + alpha * dir_ref[...]
    resid = res_ref[...] - alpha * image_ref[...]
    res_out[...] = resid
    new_ref[...] = jnp.zeros(new_ref.shape, F32) + jnp.sum(resid * (pre_ref[...] * resid), axis=1, keepdims=True)


def turn_kernel(groups, *refs):
    news, rzs = refs[:groups], refs[groups : 2 * groups]
    res_ref, pre_ref, dir_ref, out_ref = refs[2 * groups :]
    out_ref[...] = pre_ref[...] * res_ref[...] + (total(news) / total(rzs)) * dir_ref[...]


def small_call(kernel, outs, *args):
    return pl.pallas_call(
        kernel,
        out_shape=[jax.ShapeDtypeStruct(shape, F32) for shape in outs],
        in_specs=[VMEM] * len(args),
        out_specs=[VMEM] * len(outs),
        compiler_params=pltpu.CompilerParams(vmem_limit_bytes=8 * MIB),
    )(*args)


def shards(points, centres, coef, resid, direction, precond):
    num_pts, num_ctr = lax.axis_size("pts"), lax.axis_size("ctr")
    num, full = points.shape[1], direction.shape
    kern, part = fit_parts(points, centres, direction, 4)
    fits = over_ctr(part)
    (give_a,) = col_sums(fits, kern, (0,))
    got_a = send_pts(give_a, along(0))
    (give_b,) = col_sums(fits, kern, (1,))
    got_b = send_pts(give_b, along(0))
    keep_a, keep_b = col_sums(fits, kern, (2, 3))
    mine = send_pts(keep_a + got_a, along(1)) + (keep_b + got_b)
    mine = sum_over_rest(mine)
    near = send_pts(mine, along(1))
    far = send_pts(mine, along(0))
    last = send_pts(near, along(0))
    scale = 2048.0 / (num * num_pts)
    short = (full[0], 128)
    pre = precond.reshape(1, full[1])
    image, curv, rz = small_call(
        functools.partial(image_kernel, scale), [full, short, short], last, far, near, mine, direction, resid, pre
    )
    curvs, rzs = over_ctr(curv), over_ctr(rz)
    coef_next, resid_next, new = small_call(
        functools.partial(step_kernel, num_ctr), [full, full, short], *curvs, *rzs, image, direction, resid, pre, coef
    )
    (dir_next,) = small_call(
        functools.partial(turn_kernel, num_ctr), [full], *over_ctr(new), *rzs, resid_next, pre, direction
    )
    return (coef_next, resid_next, dir_next)


def solution(mesh):
    return jax.shard_map(
        shards,
        mesh=mesh,
        in_specs=(
            P(None, "pts"),
            P(None, "ctr"),
            P(None, "ctr"),
            P(None, "ctr"),
            P(None, "ctr"),
            P("ctr"),
        ),
        out_specs=(P(None, "ctr"), P(None, "ctr"), P(None, "ctr")),
        check_vma=False,
    )
```

time: 99.9 us -> 65.9 us (0.66)
  local copies, waits for them, and re-layouts: 29.5 us -> 4.05 us
  waiting for transfers between devices: 24.7 us -> 17.5 us
  blocking collectives: 4.93 us -> 0 us
  starting transfers between devices: 14.3 us -> 17.9 us
  Pallas kernels: 22.9 us -> 25.4 us
  other arithmetic: 2.44 us -> 0.09 us
    unnamed x32 -> x16, local copies, waits for them, and re-layouts: 29.4 us -> 4.05 us
    ppermute x7 -> x12, waiting for transfers between devices: 24.7 us -> 17.5 us  [the longest x8 14.9 us: send_pts(): return lax.ppermute(value, ('pts', 'ctr'), pairs)]
    psum x2 -> x0, blocking collectives: 4.93 us -> none  [the longest x1 2.47 us: shards(): rz_new = lax.psum(jnp.sum(resid_next * scaled, axis=1), 'ctr')]
    ppermute x7 -> x12, starting transfers between devices: 14.3 us -> 17.9 us  [the longest x8 16.6 us: send_pts(): return lax.ppermute(value, ('pts', 'ctr'), pairs)]
    pallas_call x0 -> x3, Pallas kernels: none -> 2.49 us  [small_call(): pl.pallas_call(kernel, out_shape=[jax.ShapeDtypeStruct(shape, F32) for sh...]
    reduce_sum x2 -> x0, other arithmetic: 1.37 us -> none  [the longest x1 1.11 us: shards(): rz_new = lax.psum(jnp.sum(resid_next * scaled, axis=1), 'ctr')]
    pallas_call x1 -> x3, Pallas kernels: 5.26 us -> 5.28 us  [col_sums(): pl.pallas_call(functools.partial(col_kernel, len(kern), len(fits), width_...]
  transfers between devices with their start and end apart: 7 -> 12, of which waited for: 7 -> 10; matrix products, arithmetic and copies ran while one was open for 0% -> 0% of each run, Pallas kernels for 0% -> 6%
where the time goes in v2:
time: 65.9 us; the launch traced here: 65.7 us
  Pallas kernels  25.4 us (39%)
  starting transfers between devices  17.9 us (27%)
  waiting for transfers between devices  17.5 us (27%)
  local copies, waits for them, and re-layouts  4.05 us (6%)
  between operations  0.7 us (1%)
    pallas_call x1, Pallas kernels, fit_parts(): pl.pallas_call(functools.partial(fit_kernel, parts, width_of(ctr, 1024)),...  17.7 us
    ppermute x8, starting transfers between devices, send_pts(): return lax.ppermute(value, ('pts', 'ctr'), pairs)  16.6 us
    ppermute x8, waiting for transfers between devices, send_pts(): return lax.ppermute(value, ('pts', 'ctr'), pairs)  14.9 us
    pallas_call x3, Pallas kernels, col_sums(): pl.pallas_call(functools.partial(col_kernel, len(kern), len(fits), width_...  5.28 us
    unnamed x16, local copies, waits for them, and re-layouts  4.05 us
    ppermute x4, waiting for transfers between devices, over_ctr(): lax.ppermute(value, 'ctr', [(c, (c + k) % num_ctr) for c in range(num_ctr)])  2.56 us
    pallas_call x3, Pallas kernels, small_call(): pl.pallas_call(kernel, out_shape=[jax.ShapeDtypeStruct(shape, F32) for sh...  2.49 us
    ppermute x4, starting transfers between devices, over_ctr(): lax.ppermute(value, 'ctr', [(c, (c + k) % num_ctr) for c in range(num_ctr)])  1.32 us
  transfers between devices with their start and end apart: 12, of which 10 were waited for; matrix products, arithmetic and copies ran while one was open for 0% of the time, Pallas kernels for 6%

profile of v2, /device:TPU:0, one launch (start us, length us, event | category | flops | bytes accessed | tf_op | source)
XLA Modules:
  0.0 65.7 jit_solution(14396741732661909395)
XLA Ops:
  0.6 1.0 %copy-done = f32[16,8192]{1,0:T(8,128)S(1)} copy-done((f32[16,8192]{1,0:T(8,128)S(1)}, f32[16,8192]{1,0:T(8,128)}, u32[]{:S(2)}) %copy-start) | copy-done | bytes 524312
  1.7 1.0 %copy-done.4 = bf16[32,8192]{1,0:T(8,128)(2,1)S(1)} copy-done((bf16[32,8192]{1,0:T(8,128)(2,1)S(1)}, bf16[32,8192]{1,0:T(8,128)(2,1)}, u32[]{:S(2)}) %copy-start.4) | copy-done | bytes 524312
  2.7 0.9 %copy-done.7 = bf16[32,2048]{1,0:T(8,128)(2,1)S(1)} copy-done((bf16[32,2048]{1,0:T(8,128)(2,1)S(1)}, bf16[32,2048]{1,0:T(8,128)(2,1)}, u32[]{:S(2)}) %copy-start.7) | copy-done | bytes 131096
  3.6 17.7 %shard_map.85 = (bf16[512,8192]{1,0:T(8,128)(2,1)S(1)}, bf16[512,8192]{1,0:T(8,128)(2,1)S(1)}, bf16[512,8192]{1,0:T(8,128)(2,1)S(1)}, bf16[512,8192]{1,0:T(8,128)(2,1)S(1)}, bf16[16,2048]{1,0:T(8,128)(2,1)S(1)}) custom-call(bf16[32,2048]{1,0:T(8,128)(2,1)S(1)} %copy-done.7, bf16[32,8192]{1,0:T(8,128)(2,1)S(1)} %copy-done.4, f32[16,8192]{1,0:T(8,128)S(1)} %copy-done), custom_call_target="tpu_custom_call" | custom-call | tf_op jit(solution)/shard_map/pallas_call | solution.py:112
  21.3 0.5 collective-permute-start
  21.8 0.9 %collective-permute-done.refs_1_ = bf16[16,2048]{1,0:T(8,128)(2,1)S(1)} collective-permute-done((bf16[16,2048]{1,0:T(8,128)(2,1)S(1)}, bf16[16,2048]{1,0:T(8,128)(2,1)S(1)}, u32[]{:S(2)}, u32[]{:S(2)}) %collective-permute-start) | collective-permute-done | bytes 65568 | tf_op jit(solution)/shard_map/ppermute | solution.py:178
  22.7 1.3 %shard_map.87 = f32[16,2048]{1,0:T(8,128)S(1)} custom-call(bf16[16,2048]{1,0:T(8,128)(2,1)S(1)} %get-tuple-element.16.refs_0_, bf16[16,2048]{1,0:T(8,128)(2,1)S(1)} %collective-permute-done.refs_1_, bf16[512,8192]{1,0:T(8,128)(2,1)S(1)} %get-tuple-element.17.refs_2_, bf16[512,8192]{1,0:T(8,128)(2,1)S(1)} %get-tuple-element.18.refs_3_, ...), custom_call_target="tpu_custom_call" | custom-call | tf_op jit(solution)/shard_map/pallas_call | solution.py:126
  24.0 2.9 %collective-permute-start.1 = (f32[16,2048]{1,0:T(8,128)S(1)}, f32[16,2048]{1,0:T(8,128)S(1)}, u32[]{:S(2)}, u32[]{:S(2)}) collective-permute-start(f32[16,2048]{1,0:T(8,128)S(1)} %shard_map.87), channel_id=1, source_target_pairs={{0,2},{1,5},{2,0},{3,7},{4,6},{5,1},{6,4},{7,3},{8,10},{9,13},{10,... | collective-permute-start | bytes 393224 | tf_op jit(solution)/shard_map/ppermute | solution.py:148
  26.8 1.3 %shard_map.88 = f32[16,2048]{1,0:T(8,128)S(1)} custom-call(bf16[16,2048]{1,0:T(8,128)(2,1)S(1)} %get-tuple-element.16.refs_0_, bf16[16,2048]{1,0:T(8,128)(2,1)S(1)} %collective-permute-done.refs_1_, bf16[512,8192]{1,0:T(8,128)(2,1)S(1)} %get-tuple-element.17.refs_2_, bf16[512,8192]{1,0:T(8,128)(2,1)S(1)} %get-tuple-element.18.refs_3_, ...), custom_call_target="tpu_custom_call" | custom-call | tf_op jit(solution)/shard_map/pallas_call | solution.py:126
  28.2 0.1 collective-permute-start.3
  28.3 2.6 %shard_map.86 = (f32[16,2048]{1,0:T(8,128)S(1)}, f32[16,2048]{1,0:T(8,128)S(1)}) custom-call(bf16[16,2048]{1,0:T(8,128)(2,1)S(1)} %get-tuple-element.16.refs_0_, bf16[16,2048]{1,0:T(8,128)(2,1)S(1)} %collective-permute-done.refs_1_, bf16[512,8192]{1,0:T(8,128)(2,1)S(1)} %get-tuple-element.17.refs_2_, bf16[512,8192]{1,0:T(8,128)(2,1)S(1)} %get-tuple-element.18.refs_3_, ...), custom_call_target="tpu_custom_call" | custom-call | tf_op jit(solution)/shard_map/pallas_call | solution.py:126
  30.9 2.1 %collective-permute-start.2 = (f32[16,2048]{1,0:T(8,128)S(1)}, f32[16,2048]{1,0:T(8,128)S(1)}, u32[]{:S(2)}, u32[]{:S(2)}) collective-permute-start(f32[16,2048]{1,0:T(8,128)S(1)} %add.15), channel_id=1, source_target_pairs={{0,4},{1,3},{2,6},{3,1},{4,0},{5,7},{6,2},{7,5},{8,12},{9,11},{10,... | collective-permute-start | bytes 393224 | tf_op jit(solution)/shard_map/ppermute | solution.py:148
  33.0 0.2 collective-permute-done.3
  33.2 2.8 %collective-permute-done.2 = f32[16,2048]{1,0:T(8,128)S(1)} collective-permute-done((f32[16,2048]{1,0:T(8,128)S(1)}, f32[16,2048]{1,0:T(8,128)S(1)}, u32[]{:S(2)}, u32[]{:S(2)}) %collective-permute-start.2) | collective-permute-done | bytes 131104 | tf_op jit(solution)/shard_map/ppermute | solution.py:148
  36.0 2.2 %collective-permute-start.4 = (f32[16,2048]{1,0:T(8,128)S(1)}, f32[16,2048]{1,0:T(8,128)S(1)}, u32[]{:S(2)}, u32[]{:S(2)}) collective-permute-start(f32[16,2048]{1,0:T(8,128)S(1)} %add_add_fusion), channel_id=1, source_target_pairs={{0,8},{1,9},{2,10},{3,11},{4,12},{5,13},{6,14},{7,15},{8,0},{9,1},... | collective-permute-start | bytes 393224 | tf_op jit(solution)/shard_map/ppermute | solution.py:148
  38.2 2.9 %collective-permute-done.4 = f32[16,2048]{1,0:T(8,128)S(1)} collective-permute-done((f32[16,2048]{1,0:T(8,128)S(1)}, f32[16,2048]{1,0:T(8,128)S(1)}, u32[]{:S(2)}, u32[]{:S(2)}) %collective-permute-start.4) | collective-permute-done | bytes 131104 | tf_op jit(solution)/shard_map/ppermute | solution.py:148
  41.2 3.1 %collective-permute-start.5 = (f32[16,2048]{1,0:T(8,128)S(1)}, f32[16,2048]{1,0:T(8,128)S(1)}, u32[]{:S(2)}, u32[]{:S(2)}) collective-permute-start(f32[16,2048]{1,0:T(8,128)S(1)} %add.18), channel_id=1, source_target_pairs={{0,16},{1,17},{2,18},{3,19},{4,20},{5,21},{6,22},{7,23},{8,24},{9,... | collective-permute-start | bytes 393224 | tf_op jit(solution)/shard_map/ppermute | solution.py:148
  44.2 3.0 %collective-permute-done.5 = f32[16,2048]{1,0:T(8,128)S(1)} collective-permute-done((f32[16,2048]{1,0:T(8,128)S(1)}, f32[16,2048]{1,0:T(8,128)S(1)}, u32[]{:S(2)}, u32[]{:S(2)}) %collective-permute-start.5) | collective-permute-done | bytes 131104 | tf_op jit(solution)/shard_map/ppermute | solution.py:148
  47.2 3.3 %collective-permute-start.6 = (f32[16,2048]{1,0:T(8,128)S(1)}, f32[16,2048]{1,0:T(8,128)S(1)}, u32[]{:S(2)}, u32[]{:S(2)}) collective-permute-start(f32[16,2048]{1,0:T(8,128)S(1)} %add.19.refs_3_), channel_id=1, source_target_pairs={{0,4},{1,3},{2,6},{3,1},{4,0},{5,7},{6,2},{7,5},{8,12},{9,11},{10,... | collective-permute-start | bytes 393224 | tf_op jit(solution)/shard_map/ppermute | solution.py:148
  50.5 1.5 %collective-permute-start.8 = (f32[16,2048]{1,0:T(8,128)S(1)}, f32[16,2048]{1,0:T(8,128)S(1)}, u32[]{:S(2)}, u32[]{:S(2)}) collective-permute-start(f32[16,2048]{1,0:T(8,128)S(1)} %add.19.refs_3_), channel_id=1, source_target_pairs={{0,2},{1,5},{2,0},{3,7},{4,6},{5,1},{6,4},{7,3},{8,10},{9,13},{10,... | collective-permute-start | bytes 393224 | tf_op jit(solution)/shard_map/ppermute | solution.py:148
  52.0 2.6 %collective-permute-done.6.refs_2_ = f32[16,2048]{1,0:T(8,128)S(1)} collective-permute-done((f32[16,2048]{1,0:T(8,128)S(1)}, f32[16,2048]{1,0:T(8,128)S(1)}, u32[]{:S(2)}, u32[]{:S(2)}) %collective-permute-start.6) | collective-permute-done | bytes 131104 | tf_op jit(solution)/shard_map/ppermute | solution.py:148
  54.6 1.5 %collective-permute-start.7 = (f32[16,2048]{1,0:T(8,128)S(1)}, f32[16,2048]{1,0:T(8,128)S(1)}, u32[]{:S(2)}, u32[]{:S(2)}) collective-permute-start(f32[16,2048]{1,0:T(8,128)S(1)} %collective-permute-done.6.refs_2_), channel_id=1, source_target_pairs={{0,2},{1,5},{2,0},{3,7},{4,6},{5,1},{6,4},{7,3},{8,10},{9,13},{10,... | collective-permute-start | bytes 393224 | tf_op jit(solution)/shard_map/ppermute | solution.py:148
  56.2 3.4 %collective-permute-done.7.refs_0_ = f32[16,2048]{1,0:T(8,128)S(1)} collective-permute-done((f32[16,2048]{1,0:T(8,128)S(1)}, f32[16,2048]{1,0:T(8,128)S(1)}, u32[]{:S(2)}, u32[]{:S(2)}) %collective-permute-start.7) | collective-permute-done | bytes 131104 | tf_op jit(solution)/shard_map/ppermute | solution.py:148
  59.6 0.3 shard_map.89
  59.9 0.5 collective-permute-start.10
  60.4 0.7 %collective-permute-done.9.refs_1_ = f32[16,128]{1,0:T(8,128)S(1)} collective-permute-done((f32[16,128]{1,0:T(8,128)S(1)}, f32[16,128]{1,0:T(8,128)S(1)}, u32[]{:S(2)}, u32[]{:S(2)}) %collective-permute-start.9) | collective-permute-done | bytes 8224 | tf_op jit(solution)/shard_map/ppermute | solution.py:178
  61.1 0.2 collective-permute-done.10.refs_3_
  61.2 1.3 %shard_map.90 = (f32[16,8192]{1,0:T(8,128)}, f32[16,8192]{1,0:T(8,128)}, f32[16,128]{1,0:T(8,128)S(1)}) custom-call(f32[16,128]{1,0:T(8,128)S(1)} %get-tuple-element.23.refs_0_, f32[16,128]{1,0:T(8,128)S(1)} %collective-permute-done.9.refs_1_, f32[16,128]{1,0:T(8,128)S(1)} %get-tuple-element.24.refs_2_, f32[16,128]{1,0:T(8,128)S(1)} %collective-permute-done.10.refs_3_, ...), custom_call_target="tpu_custom_call" | custom-call | tf_op jit(solution)/shard_map/pallas_call | solution.py:221
  62.5 0.3 collective-permute-start.11
  62.8 0.8 %collective-permute-done.11.refs_1_ = f32[16,128]{1,0:T(8,128)S(1)} collective-permute-done((f32[16,128]{1,0:T(8,128)S(1)}, f32[16,128]{1,0:T(8,128)S(1)}, u32[]{:S(2)}, u32[]{:S(2)}) %collective-permute-start.11) | collective-permute-done | bytes 8224 | tf_op jit(solution)/shard_map/ppermute | solution.py:178
  63.7 1.0 %copy-done.3 = f32[16,8192]{1,0:T(8,128)S(1)} copy-done((f32[16,8192]{1,0:T(8,128)S(1)}, f32[16,8192]{1,0:T(8,128)}, u32[]{:S(2)}) %copy-start.3) | copy-done | bytes 524312
  64.7 0.9 %shard_map.91 = f32[16,8192]{1,0:T(8,128)} custom-call(f32[16,128]{1,0:T(8,128)S(1)} %get-tuple-element.28.refs_0_, f32[16,128]{1,0:T(8,128)S(1)} %collective-permute-done.11.refs_1_, f32[16,128]{1,0:T(8,128)S(1)} %get-tuple-element.24.refs_2_, f32[16,128]{1,0:T(8,128)S(1)} %collective-permute-done.10.refs_3_, f32[16,8192]{1,0:T(8,128)S(1)} %copy-done.3, ...), custom_call_target="tpu_custom_call" | custom-call | tf_op jit(solution)/shard_map/pallas_call | solution.py:221
  (19 shorter events, 0.1 us)
Async XLA Ops:
  0.6 1.0 %copy-start = (f32[16,8192]{1,0:T(8,128)S(1)}, f32[16,8192]{1,0:T(8,128)}, u32[]{:S(2)}) copy-start(f32[16,8192]{1,0:T(8,128)} %refs_6_.3) | copy-start | bytes 1572868
  1.7 1.0 %copy-start.4 = (bf16[32,8192]{1,0:T(8,128)(2,1)S(1)}, bf16[32,8192]{1,0:T(8,128)(2,1)}, u32[]{:S(2)}) copy-start(bf16[32,8192]{1,0:T(8,128)(2,1)} %cen_ref.1) | copy-start | bytes 1572868
  2.7 0.9 %copy-start.7 = (bf16[32,2048]{1,0:T(8,128)(2,1)S(1)}, bf16[32,2048]{1,0:T(8,128)(2,1)}, u32[]{:S(2)}) copy-start(bf16[32,2048]{1,0:T(8,128)(2,1)} %pts_ref.1) | copy-start | bytes 393220
  21.3 1.4 %collective-permute-start = (bf16[16,2048]{1,0:T(8,128)(2,1)S(1)}, bf16[16,2048]{1,0:T(8,128)(2,1)S(1)}, u32[]{:S(2)}, u32[]{:S(2)}) collective-permute-start(bf16[16,2048]{1,0:T(8,128)(2,1)S(1)} %get-tuple-element.16.refs_0_), channel_id=1, source_target_pairs={{0,1},{1,0},{2,3},{3,2},{4,5},{5,4},{6,7},{7,6},{8,9},{9,8},{10,11... | collective-permute-start | bytes 196616 | tf_op jit(solution)/shard_map/ppermute | solution.py:178
  24.0 6.9 %collective-permute-start.1 = (f32[16,2048]{1,0:T(8,128)S(1)}, f32[16,2048]{1,0:T(8,128)S(1)}, u32[]{:S(2)}, u32[]{:S(2)}) collective-permute-start(f32[16,2048]{1,0:T(8,128)S(1)} %shard_map.87), channel_id=1, source_target_pairs={{0,2},{1,5},{2,0},{3,7},{4,6},{5,1},{6,4},{7,3},{8,10},{9,13},{10,... | collective-permute-start | bytes 393224 | tf_op jit(solution)/shard_map/ppermute | solution.py:148
  28.2 31.4 %copy-start.1 = (f32[16,8192]{1,0:T(8,128)S(1)}, f32[16,8192]{1,0:T(8,128)}, u32[]{:S(2)}) copy-start(f32[16,8192]{1,0:T(8,128)} %refs_6_.3) | copy-start | bytes 1572868
  28.2 31.4 %copy-start.2 = (f32[16,8192]{1,0:T(8,128)S(1)}, f32[16,8192]{1,0:T(8,128)}, u32[]{:S(2)}) copy-start(f32[16,8192]{1,0:T(8,128)} %refs_6_.2) | copy-start | bytes 1572868
  28.2 31.4 %copy-start.6 = (f32[8192]{0:T(1024)S(1)}, f32[8192]{0:T(1024)}, u32[]{:S(2)}) copy-start(f32[8192]{0:T(1024)} %param.11) | copy-start | bytes 98308
  28.2 33.1 %copy-start.5 = (f32[16,8192]{1,0:T(8,128)S(1)}, f32[16,8192]{1,0:T(8,128)}, u32[]{:S(2)}) copy-start(f32[16,8192]{1,0:T(8,128)} %refs_8_.1) | copy-start | bytes 1572868
  28.2 5.0 %collective-permute-start.3 = (f32[16,2048]{1,0:T(8,128)S(1)}, f32[16,2048]{1,0:T(8,128)S(1)}, u32[]{:S(2)}, u32[]{:S(2)}) collective-permute-start(f32[16,2048]{1,0:T(8,128)S(1)} %shard_map.88), channel_id=1, source_target_pairs={{0,2},{1,5},{2,0},{3,7},{4,6},{5,1},{6,4},{7,3},{8,10},{9,13},{10,... | collective-permute-start | bytes 393224 | tf_op jit(solution)/shard_map/ppermute | solution.py:148
  30.9 5.0 %collective-permute-start.2 = (f32[16,2048]{1,0:T(8,128)S(1)}, f32[16,2048]{1,0:T(8,128)S(1)}, u32[]{:S(2)}, u32[]{:S(2)}) collective-permute-start(f32[16,2048]{1,0:T(8,128)S(1)} %add.15), channel_id=1, source_target_pairs={{0,4},{1,3},{2,6},{3,1},{4,0},{5,7},{6,2},{7,5},{8,12},{9,11},{10,... | collective-permute-start | bytes 393224 | tf_op jit(solution)/shard_map/ppermute | solution.py:148
  36.0 5.1 %collective-permute-start.4 = (f32[16,2048]{1,0:T(8,128)S(1)}, f32[16,2048]{1,0:T(8,128)S(1)}, u32[]{:S(2)}, u32[]{:S(2)}) collective-permute-start(f32[16,2048]{1,0:T(8,128)S(1)} %add_add_fusion), channel_id=1, source_target_pairs={{0,8},{1,9},{2,10},{3,11},{4,12},{5,13},{6,14},{7,15},{8,0},{9,1},... | collective-permute-start | bytes 393224 | tf_op jit(solution)/shard_map/ppermute | solution.py:148
  41.2 6.0 %collective-permute-start.5 = (f32[16,2048]{1,0:T(8,128)S(1)}, f32[16,2048]{1,0:T(8,128)S(1)}, u32[]{:S(2)}, u32[]{:S(2)}) collective-permute-start(f32[16,2048]{1,0:T(8,128)S(1)} %add.18), channel_id=1, source_target_pairs={{0,16},{1,17},{2,18},{3,19},{4,20},{5,21},{6,22},{7,23},{8,24},{9,... | collective-permute-start | bytes 393224 | tf_op jit(solution)/shard_map/ppermute | solution.py:148
  47.2 7.4 %collective-permute-start.6 = (f32[16,2048]{1,0:T(8,128)S(1)}, f32[16,2048]{1,0:T(8,128)S(1)}, u32[]{:S(2)}, u32[]{:S(2)}) collective-permute-start(f32[16,2048]{1,0:T(8,128)S(1)} %add.19.refs_3_), channel_id=1, source_target_pairs={{0,4},{1,3},{2,6},{3,1},{4,0},{5,7},{6,2},{7,5},{8,12},{9,11},{10,... | collective-permute-start | bytes 393224 | tf_op jit(solution)/shard_map/ppermute | solution.py:148
  50.5 5.6 %collective-permute-start.8 = (f32[16,2048]{1,0:T(8,128)S(1)}, f32[16,2048]{1,0:T(8,128)S(1)}, u32[]{:S(2)}, u32[]{:S(2)}) collective-permute-start(f32[16,2048]{1,0:T(8,128)S(1)} %add.19.refs_3_), channel_id=1, source_target_pairs={{0,2},{1,5},{2,0},{3,7},{4,6},{5,1},{6,4},{7,3},{8,10},{9,13},{10,... | collective-permute-start | bytes 393224 | tf_op jit(solution)/shard_map/ppermute | solution.py:148
  54.6 5.0 %collective-permute-start.7 = (f32[16,2048]{1,0:T(8,128)S(1)}, f32[16,2048]{1,0:T(8,128)S(1)}, u32[]{:S(2)}, u32[]{:S(2)}) collective-permute-start(f32[16,2048]{1,0:T(8,128)S(1)} %collective-permute-done.6.refs_2_), channel_id=1, source_target_pairs={{0,2},{1,5},{2,0},{3,7},{4,6},{5,1},{6,4},{7,3},{8,10},{9,13},{10,... | collective-permute-start | bytes 393224 | tf_op jit(solution)/shard_map/ppermute | solution.py:148
  59.9 1.2 %collective-permute-start.9 = (f32[16,128]{1,0:T(8,128)S(1)}, f32[16,128]{1,0:T(8,128)S(1)}, u32[]{:S(2)}, u32[]{:S(2)}) collective-permute-start(f32[16,128]{1,0:T(8,128)S(1)} %get-tuple-element.23.refs_0_), channel_id=1, source_target_pairs={{0,1},{1,0},{2,3},{3,2},{4,5},{5,4},{6,7},{7,6},{8,9},{9,8},{10,11... | collective-permute-start | bytes 24584 | tf_op jit(solution)/shard_map/ppermute | solution.py:178
  59.9 1.3 %collective-permute-start.10 = (f32[16,128]{1,0:T(8,128)S(1)}, f32[16,128]{1,0:T(8,128)S(1)}, u32[]{:S(2)}, u32[]{:S(2)}) collective-permute-start(f32[16,128]{1,0:T(8,128)S(1)} %get-tuple-element.24.refs_2_), channel_id=1, source_target_pairs={{0,1},{1,0},{2,3},{3,2},{4,5},{5,4},{6,7},{7,6},{8,9},{9,8},{10,11... | collective-permute-start | bytes 24584 | tf_op jit(solution)/shard_map/ppermute | solution.py:178
  62.5 1.2 %collective-permute-start.11 = (f32[16,128]{1,0:T(8,128)S(1)}, f32[16,128]{1,0:T(8,128)S(1)}, u32[]{:S(2)}, u32[]{:S(2)}) collective-permute-start(f32[16,128]{1,0:T(8,128)S(1)} %get-tuple-element.28.refs_0_), channel_id=1, source_target_pairs={{0,1},{1,0},{2,3},{3,2},{4,5},{5,4},{6,7},{7,6},{8,9},{9,8},{10,11... | collective-permute-start | bytes 24584 | tf_op jit(solution)/shard_map/ppermute | solution.py:178
  63.7 1.0 %copy-start.3 = (f32[16,8192]{1,0:T(8,128)S(1)}, f32[16,8192]{1,0:T(8,128)}, u32[]{:S(2)}) copy-start(f32[16,8192]{1,0:T(8,128)} %get-tuple-element.14.refs_4_) | copy-start | bytes 1572868

commit v3 on v2

--- a/solution.py
+++ b/solution.py
@@ -35,21 +35,28 @@
     return out
 
 
-def fit_kernel(parts, width, pts_ref, cen_ref, dir_ref, *refs):
-    kern, (fit_ref, xa_ref, ca_ref, db_ref) = refs[:parts], refs[parts:]
+def fit_kernel(parts, width, pts_hbm, cen_hbm, dir_hbm, *refs):
+    kern, (fit_ref, pts_ref, cen_ref, dir_ref, xa_ref, ca_ref, db_ref, sems) = refs[:parts], refs[parts:]
+    pairs = ((pts_hbm, pts_ref), (cen_hbm, cen_ref), (dir_hbm, dir_ref))
+    copies = [pltpu.make_async_copy(source, target, sems.at[i]) for i, (source, target) in enumerate(pairs)]
+    for copy in copies:
+        copy.start()
     feat, num = pts_ref.shape
     ctr = cen_ref.shape[1]
+    copies[0].wait()
     pts = pts_ref[...].astype(F32)
     terms = list(split3(pts * RATE))
     norm = split3(jnp.sum(pts * pts, axis=0, keepdims=True) * (-0.5 * RATE))
     terms.append(rows_of(list(norm) + [1.0, 1.0, 1.0], (DEPTH - 3 * feat, num)))
     xa_ref[...] = jnp.concatenate(terms, axis=0).T.astype(BF16)
+    copies[1].wait()
     cen = cen_ref[...]
     for i in range(3):
         ca_ref[i * feat : (i + 1) * feat, :] = cen
     cen = cen.astype(F32)
     norm = split3(jnp.sum(cen * cen, axis=0, keepdims=True) * (-0.5 * RATE))
     ca_ref[3 * feat :, :] = rows_of([1.0, 1.0, 1.0] + list(norm), (DEPTH - 3 * feat, ctr)).astype(BF16)
+    copies[2].wait()
     db_ref[...] = dir_ref[...].astype(BF16)
     rows = num // parts
 
@@ -112,11 +119,19 @@
     out = pl.pallas_call(
         functools.partial(fit_kernel, parts, width_of(ctr, 1024)),
         out_shape=[jax.ShapeDtypeStruct((num // parts, ctr), BF16)] * parts + [jax.ShapeDtypeStruct((targets, num), BF16)],
-        in_specs=[VMEM] * 3,
+        in_specs=[pl.BlockSpec(memory_space=pl.ANY)] * 3,
         out_specs=[VMEM] * (parts + 1),
-        scratch_shapes=[pltpu.VMEM((num, DEPTH), BF16), pltpu.VMEM((DEPTH, ctr), BF16), pltpu.VMEM((targets, ctr), BF16)],
+        scratch_shapes=[
+            pltpu.VMEM(points.shape, BF16),
+            pltpu.VMEM(centres.shape, BF16),
+            pltpu.VMEM(direction.shape, F32),
+            pltpu.VMEM((num, DEPTH), BF16),
+            pltpu.VMEM((DEPTH, ctr), BF16),
+            pltpu.VMEM((targets, ctr), BF16),
+            pltpu.SemaphoreType.DMA((3,)),
+        ],
         compiler_params=pltpu.CompilerParams(vmem_limit_bytes=8 * MIB),
-    )(points, centres, direction)
+    )(*[pltpu.with_memory_space_constraint(value, pltpu.HBM) for value in (points, centres, direction)])
     return out[:parts], out[parts]
 
 
@@ -153,8 +168,13 @@
 
 
 def sum_over_rest(value):
-    me, stride = lax.axis_index("pts"), 4
-    for radix in radices(lax.axis_size("pts") // 4):
+    rest = lax.axis_size("pts") // 4
+    twos = rest & -rest
+    for k in range(twos.bit_length() - 1):
+        mask = 4 * (2 * 2**k - 1)
+        value = value + send_pts(value, lambda p, odd: p ^ mask)
+    me, stride = lax.axis_index("pts"), 4 * twos
+    for radix in radices(rest // twos):
         got = [value]
         for k in range(1, radix):
 
@@ -163,11 +183,8 @@
                 return p + ((d + k) % radix - d) * stride
 
             got.append(send_pts(value, partner))
-        if radix == 2:
-            value = got[0] + got[1]
-        else:
-            mine, stack = (me // stride) % radix, jnp.stack(got)
-            value = sum(lax.dynamic_index_in_dim(stack, (mine - d) % radix, 0, False) for d in range(radix))
+        mine, stack = (me // stride) % radix, jnp.stack(got)
+        value = sum(lax.dynamic_index_in_dim(stack, (mine - d) % radix, 0, False) for d in range(radix))
         stride *= radix
     return value
 
@@ -179,42 +196,36 @@
     ]
 
 
-def total(refs):
-    value = refs[0][...]
-    for ref in refs[1:]:
-        value = value + ref[...]
-    return value[:, :1]
-
-
 def image_kernel(scale, *refs):
-    chunks, (dir_ref, res_ref, pre_ref, image_ref, curv_ref, rz_ref) = refs[:4], refs[4:]
+    chunks, (dir_ref, res_ref, pre_ref, image_ref, sums_ref) = refs[:4], refs[4:]
     size = chunks[0].shape[1]
-    curv = jnp.zeros(curv_ref.shape, F32)
+    targets = sums_ref.shape[0] // 4
+    sums = [jnp.zeros((targets, 1), F32)] * 4
     for chunk, i in zip(chunks, chunk_ids()):
         col = tile_of(i, size)
-        direction = dir_ref[:, col]
+        direction, resid, pre = dir_ref[:, col], res_ref[:, col], pre_ref[:, col]
         image = chunk[...] * scale + 0.5 * direction
         image_ref[:, col] = image
-        curv = curv + jnp.sum(direction * image, axis=1, keepdims=True)
-    curv_ref[...] = curv
-    resid = res_ref[...]
-    rz_ref[...] = jnp.zeros(rz_ref.shape, F32) + jnp.sum(resid * resid * pre_ref[...], axis=1, keepdims=True)
+        terms = (resid * resid * pre, direction * image, resid * pre * image, image * image * pre)
+        sums = [old + jnp.sum(term, axis=1, keepdims=True) for old, term in zip(sums, terms)]
+    for i, value in enumerate(sums):
+        sums_ref[i * targets : (i + 1) * targets, :] = jnp.broadcast_to(value, (targets, 128))
 
 
 def step_kernel(groups, *refs):
-    curvs, rzs = refs[:groups], refs[groups : 2 * groups]
-    image_ref, dir_ref, res_ref, pre_ref, coef_ref, coef_out, res_out, new_ref = refs[2 * groups :]
-    alpha = total(rzs) / total(curvs)
-    coef_out[...] = coef_ref[...] + alpha * dir_ref[...]
+    image_ref, dir_ref, res_ref, pre_ref, coef_ref, coef_out, res_out, dir_out = refs[groups:]
+    targets = dir_ref.shape[0]
+    total = refs[0][...]
+    for ref in refs[1:groups]:
+        total = total + ref[...]
+    rz, curv, cross, square = [total[i * targets : (i + 1) * targets, :1] for i in range(4)]
+    alpha = rz / curv
+    direction = dir_ref[...]
+    coef_out[...] = coef_ref[...] + alpha * direction
     resid = res_ref[...] - alpha * image_ref[...]
     res_out[...] = resid
-    new_ref[...] = jnp.zeros(new_ref.shape, F32) + jnp.sum(resid * (pre_ref[...] * resid), axis=1, keepdims=True)
-
-
-def turn_kernel(groups, *refs):
-    news, rzs = refs[:groups], refs[groups : 2 * groups]
-    res_ref, pre_ref, dir_ref, out_ref = refs[2 * groups :]
-    out_ref[...] = pre_ref[...] * res_ref[...] + (total(news) / total(rzs)) * dir_ref[...]
+    rz_new = rz - alpha * (2.0 * cross - alpha * square)
+    dir_out[...] = pre_ref[...] * resid + (rz_new / rz) * direction
 
 
 def small_call(kernel, outs, *args):
@@ -243,19 +254,13 @@
     far = send_pts(mine, along(0))
     last = send_pts(near, along(0))
     scale = 2048.0 / (num * num_pts)
-    short = (full[0], 128)
     pre = precond.reshape(1, full[1])
-    image, curv, rz = small_call(
-        functools.partial(image_kernel, scale), [full, short, short], last, far, near, mine, direction, resid, pre
+    image, sums = small_call(
+        functools.partial(image_kernel, scale), [full, (4 * full[0], 128)], last, far, near, mine, direction, resid, pre
     )
-    curvs, rzs = over_ctr(curv), over_ctr(rz)
-    coef_next, resid_next, new = small_call(
-        functools.partial(step_kernel, num_ctr), [full, full, short], *curvs, *rzs, image, direction, resid, pre, coef
+    return small_call(
+        functools.partial(step_kernel, num_ctr), [full] * 3, *over_ctr(sums), image, direction, resid, pre, coef
     )
-    (dir_next,) = small_call(
-        functools.partial(turn_kernel, num_ctr), [full], *over_ctr(new), *rzs, resid_next, pre, direction
-    )
-    return (coef_next, resid_next, dir_next)
 
 
 def solution(mesh):

time: 65.9 us -> 60.5 us (0.918)
  local copies, waits for them, and re-layouts: 4.05 us -> 0.03 us
  starting transfers between devices: 17.9 us -> 16.7 us
    unnamed x16 -> x8, local copies, waits for them, and re-layouts: 4.05 us -> 0.03 us
    pallas_call x1, Pallas kernels: 17.7 us -> 18.7 us  [fit_parts(): pl.pallas_call(functools.partial(fit_kernel, parts, width_of(ctr, 1024)),...]
    pallas_call x3 -> x2, Pallas kernels: 2.49 us -> 1.69 us  [small_call(): pl.pallas_call(kernel, out_shape=[jax.ShapeDtypeStruct(shape, F32) for sh...]
    ppermute x4 -> x2, starting transfers between devices: 1.32 us -> 0.56 us  [over_ctr(): lax.ppermute(value, 'ctr', [(c, (c + k) % num_ctr) for c in range(num_ctr)])]
    ppermute x4 -> x2, waiting for transfers between devices: 2.56 us -> 2.1 us  [over_ctr(): lax.ppermute(value, 'ctr', [(c, (c + k) % num_ctr) for c in range(num_ctr)])]
  transfers between devices with their start and end apart: 12 -> 10, of which waited for: 10 -> 8; matrix products, arithmetic and copies ran while one was open for 0% -> 0% of each run, Pallas kernels for 6% -> 7%
where the time goes in v3:
time: 60.5 us; the launch traced here: 60.3 us
  Pallas kernels  25.7 us (42%)
  waiting for transfers between devices  17.2 us (28%)
  starting transfers between devices  16.7 us (28%)
  between operations  0.7 us (1%)
    pallas_call x1, Pallas kernels, fit_parts(): pl.pallas_call(functools.partial(fit_kernel, parts, width_of(ctr, 1024)),...  18.7 us
    ppermute x8, starting transfers between devices, send_pts(): return lax.ppermute(value, ('pts', 'ctr'), pairs)  16.1 us
    ppermute x8, waiting for transfers between devices, send_pts(): return lax.ppermute(value, ('pts', 'ctr'), pairs)  15.1 us
    pallas_call x3, Pallas kernels, col_sums(): pl.pallas_call(functools.partial(col_kernel, len(kern), len(fits), width_...  5.28 us
    ppermute x2, waiting for transfers between devices, over_ctr(): lax.ppermute(value, 'ctr', [(c, (c + k) % num_ctr) for c in range(num_ctr)])  2.1 us
    pallas_call x2, Pallas kernels, small_call(): pl.pallas_call(kernel, out_shape=[jax.ShapeDtypeStruct(shape, F32) for sh...  1.69 us
  transfers between devices with their start and end apart: 10, of which 8 were waited for; matrix products, arithmetic and copies ran while one was open for 0% of the time, Pallas kernels for 7%

profile of v3, /device:TPU:0, one launch (start us, length us, event | category | flops | bytes accessed | tf_op | source)
XLA Modules:
  0.0 60.3 jit_solution(11845220357705104910)
XLA Ops:
  0.6 18.7 %shard_map.85 = (bf16[512,8192]{1,0:T(8,128)(2,1)S(1)}, bf16[512,8192]{1,0:T(8,128)(2,1)S(1)}, bf16[512,8192]{1,0:T(8,128)(2,1)S(1)}, bf16[512,8192]{1,0:T(8,128)(2,1)S(1)}, bf16[16,2048]{1,0:T(8,128)(2,1)S(1)}) custom-call(bf16[32,2048]{1,0:T(8,128)(2,1)} %pts_hbm.1, bf16[32,8192]{1,0:T(8,128)(2,1)} %cen_hbm.1, f32[16,8192]{1,0:T(8,128)} %refs_3_.1), custom_call_target="tpu_custom_call" | custom-call | tf_op jit(solution)/shard_map/pallas_call | solution.py:119
  19.4 0.5 collective-permute-start
  19.9 0.9 %collective-permute-done.refs_1_ = bf16[16,2048]{1,0:T(8,128)(2,1)S(1)} collective-permute-done((bf16[16,2048]{1,0:T(8,128)(2,1)S(1)}, bf16[16,2048]{1,0:T(8,128)(2,1)S(1)}, u32[]{:S(2)}, u32[]{:S(2)}) %collective-permute-start) | collective-permute-done | bytes 65568 | tf_op jit(solution)/shard_map/ppermute | solution.py:195
  20.8 1.3 %shard_map.87 = f32[16,2048]{1,0:T(8,128)S(1)} custom-call(bf16[16,2048]{1,0:T(8,128)(2,1)S(1)} %get-tuple-element.12.refs_0_, bf16[16,2048]{1,0:T(8,128)(2,1)S(1)} %collective-permute-done.refs_1_, bf16[512,8192]{1,0:T(8,128)(2,1)S(1)} %get-tuple-element.13.refs_2_, bf16[512,8192]{1,0:T(8,128)(2,1)S(1)} %get-tuple-element.14.refs_3_, ...), custom_call_target="tpu_custom_call" | custom-call | tf_op jit(solution)/shard_map/pallas_call | solution.py:141
  22.1 2.9 %collective-permute-start.1 = (f32[16,2048]{1,0:T(8,128)S(1)}, f32[16,2048]{1,0:T(8,128)S(1)}, u32[]{:S(2)}, u32[]{:S(2)}) collective-permute-start(f32[16,2048]{1,0:T(8,128)S(1)} %shard_map.87), channel_id=1, source_target_pairs={{0,2},{1,5},{2,0},{3,7},{4,6},{5,1},{6,4},{7,3},{8,10},{9,13},{10,... | collective-permute-start | bytes 393224 | tf_op jit(solution)/shard_map/ppermute | solution.py:163
  25.0 1.3 %shard_map.88 = f32[16,2048]{1,0:T(8,128)S(1)} custom-call(bf16[16,2048]{1,0:T(8,128)(2,1)S(1)} %get-tuple-element.12.refs_0_, bf16[16,2048]{1,0:T(8,128)(2,1)S(1)} %collective-permute-done.refs_1_, bf16[512,8192]{1,0:T(8,128)(2,1)S(1)} %get-tuple-element.13.refs_2_, bf16[512,8192]{1,0:T(8,128)(2,1)S(1)} %get-tuple-element.14.refs_3_, ...), custom_call_target="tpu_custom_call" | custom-call | tf_op jit(solution)/shard_map/pallas_call | solution.py:141
  26.3 0.0 copy-start
  26.3 0.0 copy-start.2
  26.4 0.1 collective-permute-start.3
  26.4 2.6 %shard_map.86 = (f32[16,2048]{1,0:T(8,128)S(1)}, f32[16,2048]{1,0:T(8,128)S(1)}) custom-call(bf16[16,2048]{1,0:T(8,128)(2,1)S(1)} %get-tuple-element.12.refs_0_, bf16[16,2048]{1,0:T(8,128)(2,1)S(1)} %collective-permute-done.refs_1_, bf16[512,8192]{1,0:T(8,128)(2,1)S(1)} %get-tuple-element.13.refs_2_, bf16[512,8192]{1,0:T(8,128)(2,1)S(1)} %get-tuple-element.14.refs_3_, ...), custom_call_target="tpu_custom_call" | custom-call | tf_op jit(solution)/shard_map/pallas_call | solution.py:141
  29.1 0.0 collective-permute-done.1
  29.1 2.0 %collective-permute-start.2 = (f32[16,2048]{1,0:T(8,128)S(1)}, f32[16,2048]{1,0:T(8,128)S(1)}, u32[]{:S(2)}, u32[]{:S(2)}) collective-permute-start(f32[16,2048]{1,0:T(8,128)S(1)} %add.15), channel_id=1, source_target_pairs={{0,4},{1,3},{2,6},{3,1},{4,0},{5,7},{6,2},{7,5},{8,12},{9,11},{10,... | collective-permute-start | bytes 393224 | tf_op jit(solution)/shard_map/ppermute | solution.py:163
  31.2 0.2 collective-permute-done.3
  31.4 2.8 %collective-permute-done.2 = f32[16,2048]{1,0:T(8,128)S(1)} collective-permute-done((f32[16,2048]{1,0:T(8,128)S(1)}, f32[16,2048]{1,0:T(8,128)S(1)}, u32[]{:S(2)}, u32[]{:S(2)}) %collective-permute-start.2) | collective-permute-done | bytes 131104 | tf_op jit(solution)/shard_map/ppermute | solution.py:163
  34.2 2.2 %collective-permute-start.4 = (f32[16,2048]{1,0:T(8,128)S(1)}, f32[16,2048]{1,0:T(8,128)S(1)}, u32[]{:S(2)}, u32[]{:S(2)}) collective-permute-start(f32[16,2048]{1,0:T(8,128)S(1)} %add_add_fusion), channel_id=1, source_target_pairs={{0,8},{1,9},{2,10},{3,11},{4,12},{5,13},{6,14},{7,15},{8,0},{9,1},... | collective-permute-start | bytes 393224 | tf_op jit(solution)/shard_map/ppermute | solution.py:163
  36.3 2.9 %collective-permute-done.4 = f32[16,2048]{1,0:T(8,128)S(1)} collective-permute-done((f32[16,2048]{1,0:T(8,128)S(1)}, f32[16,2048]{1,0:T(8,128)S(1)}, u32[]{:S(2)}, u32[]{:S(2)}) %collective-permute-start.4) | collective-permute-done | bytes 131104 | tf_op jit(solution)/shard_map/ppermute | solution.py:163
  39.3 4.0 %collective-permute-start.5 = (f32[16,2048]{1,0:T(8,128)S(1)}, f32[16,2048]{1,0:T(8,128)S(1)}, u32[]{:S(2)}, u32[]{:S(2)}) collective-permute-start(f32[16,2048]{1,0:T(8,128)S(1)} %add.18), channel_id=1, source_target_pairs={{0,24},{1,25},{2,26},{3,27},{4,28},{5,29},{6,30},{7,31},{8,16},{9,... | collective-permute-start | bytes 393224 | tf_op jit(solution)/shard_map/ppermute | solution.py:163
  43.3 3.1 %collective-permute-done.5 = f32[16,2048]{1,0:T(8,128)S(1)} collective-permute-done((f32[16,2048]{1,0:T(8,128)S(1)}, f32[16,2048]{1,0:T(8,128)S(1)}, u32[]{:S(2)}, u32[]{:S(2)}) %collective-permute-start.5) | collective-permute-done | bytes 131104 | tf_op jit(solution)/shard_map/ppermute | solution.py:163
  46.4 1.8 %collective-permute-start.6 = (f32[16,2048]{1,0:T(8,128)S(1)}, f32[16,2048]{1,0:T(8,128)S(1)}, u32[]{:S(2)}, u32[]{:S(2)}) collective-permute-start(f32[16,2048]{1,0:T(8,128)S(1)} %add.19.refs_3_), channel_id=1, source_target_pairs={{0,4},{1,3},{2,6},{3,1},{4,0},{5,7},{6,2},{7,5},{8,12},{9,11},{10,... | collective-permute-start | bytes 393224 | tf_op jit(solution)/shard_map/ppermute | solution.py:163
  48.2 1.5 %collective-permute-start.8 = (f32[16,2048]{1,0:T(8,128)S(1)}, f32[16,2048]{1,0:T(8,128)S(1)}, u32[]{:S(2)}, u32[]{:S(2)}) collective-permute-start(f32[16,2048]{1,0:T(8,128)S(1)} %add.19.refs_3_), channel_id=1, source_target_pairs={{0,2},{1,5},{2,0},{3,7},{4,6},{5,1},{6,4},{7,3},{8,10},{9,13},{10,... | collective-permute-start | bytes 393224 | tf_op jit(solution)/shard_map/ppermute | solution.py:163
  49.7 2.7 %collective-permute-done.6.refs_2_ = f32[16,2048]{1,0:T(8,128)S(1)} collective-permute-done((f32[16,2048]{1,0:T(8,128)S(1)}, f32[16,2048]{1,0:T(8,128)S(1)}, u32[]{:S(2)}, u32[]{:S(2)}) %collective-permute-start.6) | collective-permute-done | bytes 131104 | tf_op jit(solution)/shard_map/ppermute | solution.py:163
  52.4 1.6 %collective-permute-start.7 = (f32[16,2048]{1,0:T(8,128)S(1)}, f32[16,2048]{1,0:T(8,128)S(1)}, u32[]{:S(2)}, u32[]{:S(2)}) collective-permute-start(f32[16,2048]{1,0:T(8,128)S(1)} %collective-permute-done.6.refs_2_), channel_id=1, source_target_pairs={{0,2},{1,5},{2,0},{3,7},{4,6},{5,1},{6,4},{7,3},{8,10},{9,13},{10,... | collective-permute-start | bytes 393224 | tf_op jit(solution)/shard_map/ppermute | solution.py:163
  54.0 0.0 collective-permute-done.8.refs_1_
  54.0 3.4 %collective-permute-done.7.refs_0_ = f32[16,2048]{1,0:T(8,128)S(1)} collective-permute-done((f32[16,2048]{1,0:T(8,128)S(1)}, f32[16,2048]{1,0:T(8,128)S(1)}, u32[]{:S(2)}, u32[]{:S(2)}) %collective-permute-start.7) | collective-permute-done | bytes 131104 | tf_op jit(solution)/shard_map/ppermute | solution.py:163
  57.4 0.0 copy-done
  57.4 0.0 copy-done.1
  57.4 0.0 copy-done.3
  57.4 0.4 shard_map.89
  57.8 0.1 collective-permute-start.9
  57.8 1.2 %collective-permute-done.9.refs_1_ = f32[64,128]{1,0:T(8,128)S(1)} collective-permute-done((f32[64,128]{1,0:T(8,128)S(1)}, f32[64,128]{1,0:T(8,128)S(1)}, u32[]{:S(2)}, u32[]{:S(2)}) %collective-permute-start.9) | collective-permute-done | bytes 32800 | tf_op jit(solution)/shard_map/ppermute | solution.py:195
  59.0 0.0 copy-done.2
  59.0 1.3 %shard_map.90 = (f32[16,8192]{1,0:T(8,128)}, f32[16,8192]{1,0:T(8,128)}, f32[16,8192]{1,0:T(8,128)}) custom-call(f32[64,128]{1,0:T(8,128)S(1)} %get-tuple-element.19.refs_0_, f32[64,128]{1,0:T(8,128)S(1)} %collective-permute-done.9.refs_1_, f32[16,8192]{1,0:T(8,128)S(1)} %get-tuple-element.20.refs_2_, f32[16,8192]{1,0:T(8,128)S(1)} %copy-done, ...), custom_call_target="tpu_custom_call" | custom-call | tf_op jit(solution)/shard_map/pallas_call | solution.py:232
  (6 shorter events, 0.1 us)
Async XLA Ops:
  19.4 1.4 %collective-permute-start = (bf16[16,2048]{1,0:T(8,128)(2,1)S(1)}, bf16[16,2048]{1,0:T(8,128)(2,1)S(1)}, u32[]{:S(2)}, u32[]{:S(2)}) collective-permute-start(bf16[16,2048]{1,0:T(8,128)(2,1)S(1)} %get-tuple-element.12.refs_0_), channel_id=1, source_target_pairs={{0,1},{1,0},{2,3},{3,2},{4,5},{5,4},{6,7},{7,6},{8,9},{9,8},{10,11... | collective-permute-start | bytes 196616 | tf_op jit(solution)/shard_map/ppermute | solution.py:195
  22.1 7.0 %collective-permute-start.1 = (f32[16,2048]{1,0:T(8,128)S(1)}, f32[16,2048]{1,0:T(8,128)S(1)}, u32[]{:S(2)}, u32[]{:S(2)}) collective-permute-start(f32[16,2048]{1,0:T(8,128)S(1)} %shard_map.87), channel_id=1, source_target_pairs={{0,2},{1,5},{2,0},{3,7},{4,6},{5,1},{6,4},{7,3},{8,10},{9,13},{10,... | collective-permute-start | bytes 393224 | tf_op jit(solution)/shard_map/ppermute | solution.py:163
  26.3 31.1 %copy-start = (f32[16,8192]{1,0:T(8,128)S(1)}, f32[16,8192]{1,0:T(8,128)}, u32[]{:S(2)}) copy-start(f32[16,8192]{1,0:T(8,128)} %refs_3_.1) | copy-start | bytes 1572868
  26.3 31.1 %copy-start.1 = (f32[16,8192]{1,0:T(8,128)S(1)}, f32[16,8192]{1,0:T(8,128)}, u32[]{:S(2)}) copy-start(f32[16,8192]{1,0:T(8,128)} %refs_4_.3) | copy-start | bytes 1572868
  26.3 31.1 %copy-start.3 = (f32[8192]{0:T(1024)S(1)}, f32[8192]{0:T(1024)}, u32[]{:S(2)}) copy-start(f32[8192]{0:T(1024)} %param.11) | copy-start | bytes 98308
  26.3 32.7 %copy-start.2 = (f32[16,8192]{1,0:T(8,128)S(1)}, f32[16,8192]{1,0:T(8,128)}, u32[]{:S(2)}) copy-start(f32[16,8192]{1,0:T(8,128)} %refs_6_.1) | copy-start | bytes 1572868
  26.4 5.0 %collective-permute-start.3 = (f32[16,2048]{1,0:T(8,128)S(1)}, f32[16,2048]{1,0:T(8,128)S(1)}, u32[]{:S(2)}, u32[]{:S(2)}) collective-permute-start(f32[16,2048]{1,0:T(8,128)S(1)} %shard_map.88), channel_id=1, source_target_pairs={{0,2},{1,5},{2,0},{3,7},{4,6},{5,1},{6,4},{7,3},{8,10},{9,13},{10,... | collective-permute-start | bytes 393224 | tf_op jit(solution)/shard_map/ppermute | solution.py:163
  29.1 5.0 %collective-permute-start.2 = (f32[16,2048]{1,0:T(8,128)S(1)}, f32[16,2048]{1,0:T(8,128)S(1)}, u32[]{:S(2)}, u32[]{:S(2)}) collective-permute-start(f32[16,2048]{1,0:T(8,128)S(1)} %add.15), channel_id=1, source_target_pairs={{0,4},{1,3},{2,6},{3,1},{4,0},{5,7},{6,2},{7,5},{8,12},{9,11},{10,... | collective-permute-start | bytes 393224 | tf_op jit(solution)/shard_map/ppermute | solution.py:163
  34.2 5.1 %collective-permute-start.4 = (f32[16,2048]{1,0:T(8,128)S(1)}, f32[16,2048]{1,0:T(8,128)S(1)}, u32[]{:S(2)}, u32[]{:S(2)}) collective-permute-start(f32[16,2048]{1,0:T(8,128)S(1)} %add_add_fusion), channel_id=1, source_target_pairs={{0,8},{1,9},{2,10},{3,11},{4,12},{5,13},{6,14},{7,15},{8,0},{9,1},... | collective-permute-start | bytes 393224 | tf_op jit(solution)/shard_map/ppermute | solution.py:163
  39.3 7.1 %collective-permute-start.5 = (f32[16,2048]{1,0:T(8,128)S(1)}, f32[16,2048]{1,0:T(8,128)S(1)}, u32[]{:S(2)}, u32[]{:S(2)}) collective-permute-start(f32[16,2048]{1,0:T(8,128)S(1)} %add.18), channel_id=1, source_target_pairs={{0,24},{1,25},{2,26},{3,27},{4,28},{5,29},{6,30},{7,31},{8,16},{9,... | collective-permute-start | bytes 393224 | tf_op jit(solution)/shard_map/ppermute | solution.py:163
  46.4 6.0 %collective-permute-start.6 = (f32[16,2048]{1,0:T(8,128)S(1)}, f32[16,2048]{1,0:T(8,128)S(1)}, u32[]{:S(2)}, u32[]{:S(2)}) collective-permute-start(f32[16,2048]{1,0:T(8,128)S(1)} %add.19.refs_3_), channel_id=1, source_target_pairs={{0,4},{1,3},{2,6},{3,1},{4,0},{5,7},{6,2},{7,5},{8,12},{9,11},{10,... | collective-permute-start | bytes 393224 | tf_op jit(solution)/shard_map/ppermute | solution.py:163
  48.2 5.7 %collective-permute-start.8 = (f32[16,2048]{1,0:T(8,128)S(1)}, f32[16,2048]{1,0:T(8,128)S(1)}, u32[]{:S(2)}, u32[]{:S(2)}) collective-permute-start(f32[16,2048]{1,0:T(8,128)S(1)} %add.19.refs_3_), channel_id=1, source_target_pairs={{0,2},{1,5},{2,0},{3,7},{4,6},{5,1},{6,4},{7,3},{8,10},{9,13},{10,... | collective-permute-start | bytes 393224 | tf_op jit(solution)/shard_map/ppermute | solution.py:163
  52.4 5.0 %collective-permute-start.7 = (f32[16,2048]{1,0:T(8,128)S(1)}, f32[16,2048]{1,0:T(8,128)S(1)}, u32[]{:S(2)}, u32[]{:S(2)}) collective-permute-start(f32[16,2048]{1,0:T(8,128)S(1)} %collective-permute-done.6.refs_2_), channel_id=1, source_target_pairs={{0,2},{1,5},{2,0},{3,7},{4,6},{5,1},{6,4},{7,3},{8,10},{9,13},{10,... | collective-permute-start | bytes 393224 | tf_op jit(solution)/shard_map/ppermute | solution.py:163
  57.8 1.3 %collective-permute-start.9 = (f32[64,128]{1,0:T(8,128)S(1)}, f32[64,128]{1,0:T(8,128)S(1)}, u32[]{:S(2)}, u32[]{:S(2)}) collective-permute-start(f32[64,128]{1,0:T(8,128)S(1)} %get-tuple-element.19.refs_0_), channel_id=1, source_target_pairs={{0,1},{1,0},{2,3},{3,2},{4,5},{5,4},{6,7},{7,6},{8,9},{9,8},{10,11... | collective-permute-start | bytes 98312 | tf_op jit(solution)/shard_map/ppermute | solution.py:195

commit v4 on v3

--- a/solution.py
+++ b/solution.py
@@ -245,10 +245,12 @@
     fits = over_ctr(part)
     (give_a,) = col_sums(fits, kern, (0,))
     got_a = send_pts(give_a, along(0))
+    (keep_a,) = col_sums(fits, kern, (2,))
     (give_b,) = col_sums(fits, kern, (1,))
     got_b = send_pts(give_b, along(0))
-    keep_a, keep_b = col_sums(fits, kern, (2, 3))
-    mine = send_pts(keep_a + got_a, along(1)) + (keep_b + got_b)
+    moved = send_pts(keep_a + got_a, along(1))
+    (keep_b,) = col_sums(fits, kern, (3,))
+    mine = moved + (keep_b + got_b)
     mine = sum_over_rest(mine)
     near = send_pts(mine, along(1))
     far = send_pts(mine, along(0))

time: 60.5 us -> 59.5 us (0.983)
  waiting for transfers between devices: 17.2 us -> 16.5 us
    ppermute x8, waiting for transfers between devices: 15.1 us -> 14.4 us  [send_pts(): return lax.ppermute(value, ('pts', 'ctr'), pairs)]
    pallas_call x3 -> x4, Pallas kernels: 5.28 us -> 5.28 us  [col_sums(): pl.pallas_call(functools.partial(col_kernel, len(kern), len(fits), width_...]
  transfers between devices with their start and end apart: 10 -> 10, of which waited for: 8 -> 9; matrix products, arithmetic and copies ran while one was open for 0% -> 0% of each run, Pallas kernels for 7% -> 7%
where the time goes in v4:
time: 59.5 us; the launch traced here: 59.3 us
  Pallas kernels  25.7 us (43%)
  waiting for transfers between devices  16.5 us (28%)
  starting transfers between devices  16.3 us (27%)
  between operations  0.71 us (1%)
    pallas_call x1, Pallas kernels, fit_parts(): pl.pallas_call(functools.partial(fit_kernel, parts, width_of(ctr, 1024)),...  18.7 us
    ppermute x8, starting transfers between devices, send_pts(): return lax.ppermute(value, ('pts', 'ctr'), pairs)  15.7 us
    ppermute x8, waiting for transfers between devices, send_pts(): return lax.ppermute(value, ('pts', 'ctr'), pairs)  14.4 us
    pallas_call x4, Pallas kernels, col_sums(): pl.pallas_call(functools.partial(col_kernel, len(kern), len(fits), width_...  5.28 us
    ppermute x2, waiting for transfers between devices, over_ctr(): lax.ppermute(value, 'ctr', [(c, (c + k) % num_ctr) for c in range(num_ctr)])  2.1 us
    pallas_call x2, Pallas kernels, small_call(): pl.pallas_call(kernel, out_shape=[jax.ShapeDtypeStruct(shape, F32) for sh...  1.69 us
  transfers between devices with their start and end apart: 10, of which 9 were waited for; matrix products, arithmetic and copies ran while one was open for 0% of the time, Pallas kernels for 7%

profile of v4, /device:TPU:0, one launch (start us, length us, event | category | flops | bytes accessed | tf_op | source)
XLA Modules:
  0.0 59.3 jit_solution(642754315743530268)
XLA Ops:
  0.6 18.7 %shard_map.85 = (bf16[512,8192]{1,0:T(8,128)(2,1)S(1)}, bf16[512,8192]{1,0:T(8,128)(2,1)S(1)}, bf16[512,8192]{1,0:T(8,128)(2,1)S(1)}, bf16[512,8192]{1,0:T(8,128)(2,1)S(1)}, bf16[16,2048]{1,0:T(8,128)(2,1)S(1)}) custom-call(bf16[32,2048]{1,0:T(8,128)(2,1)} %pts_hbm.1, bf16[32,8192]{1,0:T(8,128)(2,1)} %cen_hbm.1, f32[16,8192]{1,0:T(8,128)} %refs_3_.1), custom_call_target="tpu_custom_call" | custom-call | tf_op jit(solution)/shard_map/pallas_call | solution.py:119
  19.4 0.5 collective-permute-start
  19.9 0.9 %collective-permute-done.refs_1_ = bf16[16,2048]{1,0:T(8,128)(2,1)S(1)} collective-permute-done((bf16[16,2048]{1,0:T(8,128)(2,1)S(1)}, bf16[16,2048]{1,0:T(8,128)(2,1)S(1)}, u32[]{:S(2)}, u32[]{:S(2)}) %collective-permute-start) | collective-permute-done | bytes 65568 | tf_op jit(solution)/shard_map/ppermute | solution.py:195
  20.8 1.3 %shard_map.87 = f32[16,2048]{1,0:T(8,128)S(1)} custom-call(bf16[16,2048]{1,0:T(8,128)(2,1)S(1)} %get-tuple-element.10.refs_0_, bf16[16,2048]{1,0:T(8,128)(2,1)S(1)} %collective-permute-done.refs_1_, bf16[512,8192]{1,0:T(8,128)(2,1)S(1)} %get-tuple-element.11.refs_2_, bf16[512,8192]{1,0:T(8,128)(2,1)S(1)} %get-tuple-element.12.refs_3_, ...), custom_call_target="tpu_custom_call" | custom-call | tf_op jit(solution)/shard_map/pallas_call | solution.py:141
  22.1 2.9 %collective-permute-start.1 = (f32[16,2048]{1,0:T(8,128)S(1)}, f32[16,2048]{1,0:T(8,128)S(1)}, u32[]{:S(2)}, u32[]{:S(2)}) collective-permute-start(f32[16,2048]{1,0:T(8,128)S(1)} %shard_map.87), channel_id=1, source_target_pairs={{0,2},{1,5},{2,0},{3,7},{4,6},{5,1},{6,4},{7,3},{8,10},{9,13},{10,... | collective-permute-start | bytes 393224 | tf_op jit(solution)/shard_map/ppermute | solution.py:163
  25.0 1.3 %shard_map.89 = f32[16,2048]{1,0:T(8,128)S(1)} custom-call(bf16[16,2048]{1,0:T(8,128)(2,1)S(1)} %get-tuple-element.10.refs_0_, bf16[16,2048]{1,0:T(8,128)(2,1)S(1)} %collective-permute-done.refs_1_, bf16[512,8192]{1,0:T(8,128)(2,1)S(1)} %get-tuple-element.11.refs_2_, bf16[512,8192]{1,0:T(8,128)(2,1)S(1)} %get-tuple-element.12.refs_3_, ...), custom_call_target="tpu_custom_call" | custom-call | tf_op jit(solution)/shard_map/pallas_call | solution.py:141
  26.3 0.0 collective-permute-start.3
  26.3 1.3 %shard_map.86 = f32[16,2048]{1,0:T(8,128)S(1)} custom-call(bf16[16,2048]{1,0:T(8,128)(2,1)S(1)} %get-tuple-element.10.refs_0_, bf16[16,2048]{1,0:T(8,128)(2,1)S(1)} %collective-permute-done.refs_1_, bf16[512,8192]{1,0:T(8,128)(2,1)S(1)} %get-tuple-element.11.refs_2_, bf16[512,8192]{1,0:T(8,128)(2,1)S(1)} %get-tuple-element.12.refs_3_, ...), custom_call_target="tpu_custom_call" | custom-call | tf_op jit(solution)/shard_map/pallas_call | solution.py:141
  27.7 0.3 collective-permute-done.1
  28.0 0.0 copy-start
  28.0 0.0 copy-start.1
  28.0 0.0 copy-start.3
  28.0 0.0 copy-start.2
  28.0 2.1 %collective-permute-start.2 = (f32[16,2048]{1,0:T(8,128)S(1)}, f32[16,2048]{1,0:T(8,128)S(1)}, u32[]{:S(2)}, u32[]{:S(2)}) collective-permute-start(f32[16,2048]{1,0:T(8,128)S(1)} %add.15), channel_id=1, source_target_pairs={{0,4},{1,3},{2,6},{3,1},{4,0},{5,7},{6,2},{7,5},{8,12},{9,11},{10,... | collective-permute-start | bytes 393224 | tf_op jit(solution)/shard_map/ppermute | solution.py:163
  30.1 1.3 %shard_map.88 = f32[16,2048]{1,0:T(8,128)S(1)} custom-call(bf16[16,2048]{1,0:T(8,128)(2,1)S(1)} %get-tuple-element.10.refs_0_, bf16[16,2048]{1,0:T(8,128)(2,1)S(1)} %collective-permute-done.refs_1_, bf16[512,8192]{1,0:T(8,128)(2,1)S(1)} %get-tuple-element.11.refs_2_, bf16[512,8192]{1,0:T(8,128)(2,1)S(1)} %get-tuple-element.12.refs_3_, ...), custom_call_target="tpu_custom_call" | custom-call | tf_op jit(solution)/shard_map/pallas_call | solution.py:141
  31.4 1.0 %collective-permute-done.3 = f32[16,2048]{1,0:T(8,128)S(1)} collective-permute-done((f32[16,2048]{1,0:T(8,128)S(1)}, f32[16,2048]{1,0:T(8,128)S(1)}, u32[]{:S(2)}, u32[]{:S(2)}) %collective-permute-start.3) | collective-permute-done | bytes 131104 | tf_op jit(solution)/shard_map/ppermute | solution.py:163
  32.4 0.6 %collective-permute-done.2 = f32[16,2048]{1,0:T(8,128)S(1)} collective-permute-done((f32[16,2048]{1,0:T(8,128)S(1)}, f32[16,2048]{1,0:T(8,128)S(1)}, u32[]{:S(2)}, u32[]{:S(2)}) %collective-permute-start.2) | collective-permute-done | bytes 131104 | tf_op jit(solution)/shard_map/ppermute | solution.py:163
  33.1 2.2 %collective-permute-start.4 = (f32[16,2048]{1,0:T(8,128)S(1)}, f32[16,2048]{1,0:T(8,128)S(1)}, u32[]{:S(2)}, u32[]{:S(2)}) collective-permute-start(f32[16,2048]{1,0:T(8,128)S(1)} %add_add_fusion), channel_id=1, source_target_pairs={{0,8},{1,9},{2,10},{3,11},{4,12},{5,13},{6,14},{7,15},{8,0},{9,1},... | collective-permute-start | bytes 393224 | tf_op jit(solution)/shard_map/ppermute | solution.py:163
  35.2 3.1 %collective-permute-done.4 = f32[16,2048]{1,0:T(8,128)S(1)} collective-permute-done((f32[16,2048]{1,0:T(8,128)S(1)}, f32[16,2048]{1,0:T(8,128)S(1)}, u32[]{:S(2)}, u32[]{:S(2)}) %collective-permute-start.4) | collective-permute-done | bytes 131104 | tf_op jit(solution)/shard_map/ppermute | solution.py:163
  38.3 3.9 %collective-permute-start.5 = (f32[16,2048]{1,0:T(8,128)S(1)}, f32[16,2048]{1,0:T(8,128)S(1)}, u32[]{:S(2)}, u32[]{:S(2)}) collective-permute-start(f32[16,2048]{1,0:T(8,128)S(1)} %add.18), channel_id=1, source_target_pairs={{0,24},{1,25},{2,26},{3,27},{4,28},{5,29},{6,30},{7,31},{8,16},{9,... | collective-permute-start | bytes 393224 | tf_op jit(solution)/shard_map/ppermute | solution.py:163
  42.3 3.1 %collective-permute-done.5 = f32[16,2048]{1,0:T(8,128)S(1)} collective-permute-done((f32[16,2048]{1,0:T(8,128)S(1)}, f32[16,2048]{1,0:T(8,128)S(1)}, u32[]{:S(2)}, u32[]{:S(2)}) %collective-permute-start.5) | collective-permute-done | bytes 131104 | tf_op jit(solution)/shard_map/ppermute | solution.py:163
  45.3 1.8 %collective-permute-start.6 = (f32[16,2048]{1,0:T(8,128)S(1)}, f32[16,2048]{1,0:T(8,128)S(1)}, u32[]{:S(2)}, u32[]{:S(2)}) collective-permute-start(f32[16,2048]{1,0:T(8,128)S(1)} %add.19.refs_3_), channel_id=1, source_target_pairs={{0,4},{1,3},{2,6},{3,1},{4,0},{5,7},{6,2},{7,5},{8,12},{9,11},{10,... | collective-permute-start | bytes 393224 | tf_op jit(solution)/shard_map/ppermute | solution.py:163
  47.2 1.5 %collective-permute-start.8 = (f32[16,2048]{1,0:T(8,128)S(1)}, f32[16,2048]{1,0:T(8,128)S(1)}, u32[]{:S(2)}, u32[]{:S(2)}) collective-permute-start(f32[16,2048]{1,0:T(8,128)S(1)} %add.19.refs_3_), channel_id=1, source_target_pairs={{0,2},{1,5},{2,0},{3,7},{4,6},{5,1},{6,4},{7,3},{8,10},{9,13},{10,... | collective-permute-start | bytes 393224 | tf_op jit(solution)/shard_map/ppermute | solution.py:163
  48.6 2.7 %collective-permute-done.6.refs_2_ = f32[16,2048]{1,0:T(8,128)S(1)} collective-permute-done((f32[16,2048]{1,0:T(8,128)S(1)}, f32[16,2048]{1,0:T(8,128)S(1)}, u32[]{:S(2)}, u32[]{:S(2)}) %collective-permute-start.6) | collective-permute-done | bytes 131104 | tf_op jit(solution)/shard_map/ppermute | solution.py:163
  51.4 1.4 %collective-permute-start.7 = (f32[16,2048]{1,0:T(8,128)S(1)}, f32[16,2048]{1,0:T(8,128)S(1)}, u32[]{:S(2)}, u32[]{:S(2)}) collective-permute-start(f32[16,2048]{1,0:T(8,128)S(1)} %collective-permute-done.6.refs_2_), channel_id=1, source_target_pairs={{0,2},{1,5},{2,0},{3,7},{4,6},{5,1},{6,4},{7,3},{8,10},{9,13},{10,... | collective-permute-start | bytes 393224 | tf_op jit(solution)/shard_map/ppermute | solution.py:163
  52.7 0.0 collective-permute-done.8.refs_1_
  52.7 3.6 %collective-permute-done.7.refs_0_ = f32[16,2048]{1,0:T(8,128)S(1)} collective-permute-done((f32[16,2048]{1,0:T(8,128)S(1)}, f32[16,2048]{1,0:T(8,128)S(1)}, u32[]{:S(2)}, u32[]{:S(2)}) %collective-permute-start.7) | collective-permute-done | bytes 131104 | tf_op jit(solution)/shard_map/ppermute | solution.py:163
  56.4 0.0 copy-done.1
  56.4 0.4 shard_map.90
  56.7 0.1 collective-permute-start.9
  56.8 1.2 %collective-permute-done.9.refs_1_ = f32[64,128]{1,0:T(8,128)S(1)} collective-permute-done((f32[64,128]{1,0:T(8,128)S(1)}, f32[64,128]{1,0:T(8,128)S(1)}, u32[]{:S(2)}, u32[]{:S(2)}) %collective-permute-start.9) | collective-permute-done | bytes 32800 | tf_op jit(solution)/shard_map/ppermute | solution.py:195
  58.0 1.3 %shard_map.91 = (f32[16,8192]{1,0:T(8,128)}, f32[16,8192]{1,0:T(8,128)}, f32[16,8192]{1,0:T(8,128)}) custom-call(f32[64,128]{1,0:T(8,128)S(1)} %get-tuple-element.15.refs_0_, f32[64,128]{1,0:T(8,128)S(1)} %collective-permute-done.9.refs_1_, f32[16,8192]{1,0:T(8,128)S(1)} %get-tuple-element.16.refs_2_, f32[16,8192]{1,0:T(8,128)S(1)} %copy-done, ...), custom_call_target="tpu_custom_call" | custom-call | tf_op jit(solution)/shard_map/pallas_call | solution.py:232
  (7 shorter events, 0.1 us)
Async XLA Ops:
  19.4 1.4 %collective-permute-start = (bf16[16,2048]{1,0:T(8,128)(2,1)S(1)}, bf16[16,2048]{1,0:T(8,128)(2,1)S(1)}, u32[]{:S(2)}, u32[]{:S(2)}) collective-permute-start(bf16[16,2048]{1,0:T(8,128)(2,1)S(1)} %get-tuple-element.10.refs_0_), channel_id=1, source_target_pairs={{0,1},{1,0},{2,3},{3,2},{4,5},{5,4},{6,7},{7,6},{8,9},{9,8},{10,11... | collective-permute-start | bytes 196616 | tf_op jit(solution)/shard_map/ppermute | solution.py:195
  22.1 5.9 %collective-permute-start.1 = (f32[16,2048]{1,0:T(8,128)S(1)}, f32[16,2048]{1,0:T(8,128)S(1)}, u32[]{:S(2)}, u32[]{:S(2)}) collective-permute-start(f32[16,2048]{1,0:T(8,128)S(1)} %shard_map.87), channel_id=1, source_target_pairs={{0,2},{1,5},{2,0},{3,7},{4,6},{5,1},{6,4},{7,3},{8,10},{9,13},{10,... | collective-permute-start | bytes 393224 | tf_op jit(solution)/shard_map/ppermute | solution.py:163
  26.3 6.1 %collective-permute-start.3 = (f32[16,2048]{1,0:T(8,128)S(1)}, f32[16,2048]{1,0:T(8,128)S(1)}, u32[]{:S(2)}, u32[]{:S(2)}) collective-permute-start(f32[16,2048]{1,0:T(8,128)S(1)} %shard_map.89), channel_id=1, source_target_pairs={{0,2},{1,5},{2,0},{3,7},{4,6},{5,1},{6,4},{7,3},{8,10},{9,13},{10,... | collective-permute-start | bytes 393224 | tf_op jit(solution)/shard_map/ppermute | solution.py:163
  28.0 28.4 %copy-start = (f32[16,8192]{1,0:T(8,128)S(1)}, f32[16,8192]{1,0:T(8,128)}, u32[]{:S(2)}) copy-start(f32[16,8192]{1,0:T(8,128)} %refs_3_.1) | copy-start | bytes 1572868
  28.0 28.4 %copy-start.1 = (f32[16,8192]{1,0:T(8,128)S(1)}, f32[16,8192]{1,0:T(8,128)}, u32[]{:S(2)}) copy-start(f32[16,8192]{1,0:T(8,128)} %refs_4_.3) | copy-start | bytes 1572868
  28.0 28.4 %copy-start.3 = (f32[8192]{0:T(1024)S(1)}, f32[8192]{0:T(1024)}, u32[]{:S(2)}) copy-start(f32[8192]{0:T(1024)} %param.11) | copy-start | bytes 98308
  28.0 30.0 %copy-start.2 = (f32[16,8192]{1,0:T(8,128)S(1)}, f32[16,8192]{1,0:T(8,128)}, u32[]{:S(2)}) copy-start(f32[16,8192]{1,0:T(8,128)} %refs_6_.1) | copy-start | bytes 1572868
  28.0 5.0 %collective-permute-start.2 = (f32[16,2048]{1,0:T(8,128)S(1)}, f32[16,2048]{1,0:T(8,128)S(1)}, u32[]{:S(2)}, u32[]{:S(2)}) collective-permute-start(f32[16,2048]{1,0:T(8,128)S(1)} %add.15), channel_id=1, source_target_pairs={{0,4},{1,3},{2,6},{3,1},{4,0},{5,7},{6,2},{7,5},{8,12},{9,11},{10,... | collective-permute-start | bytes 393224 | tf_op jit(solution)/shard_map/ppermute | solution.py:163
  33.1 5.2 %collective-permute-start.4 = (f32[16,2048]{1,0:T(8,128)S(1)}, f32[16,2048]{1,0:T(8,128)S(1)}, u32[]{:S(2)}, u32[]{:S(2)}) collective-permute-start(f32[16,2048]{1,0:T(8,128)S(1)} %add_add_fusion), channel_id=1, source_target_pairs={{0,8},{1,9},{2,10},{3,11},{4,12},{5,13},{6,14},{7,15},{8,0},{9,1},... | collective-permute-start | bytes 393224 | tf_op jit(solution)/shard_map/ppermute | solution.py:163
  38.3 7.0 %collective-permute-start.5 = (f32[16,2048]{1,0:T(8,128)S(1)}, f32[16,2048]{1,0:T(8,128)S(1)}, u32[]{:S(2)}, u32[]{:S(2)}) collective-permute-start(f32[16,2048]{1,0:T(8,128)S(1)} %add.18), channel_id=1, source_target_pairs={{0,24},{1,25},{2,26},{3,27},{4,28},{5,29},{6,30},{7,31},{8,16},{9,... | collective-permute-start | bytes 393224 | tf_op jit(solution)/shard_map/ppermute | solution.py:163
  45.3 6.0 %collective-permute-start.6 = (f32[16,2048]{1,0:T(8,128)S(1)}, f32[16,2048]{1,0:T(8,128)S(1)}, u32[]{:S(2)}, u32[]{:S(2)}) collective-permute-start(f32[16,2048]{1,0:T(8,128)S(1)} %add.19.refs_3_), channel_id=1, source_target_pairs={{0,4},{1,3},{2,6},{3,1},{4,0},{5,7},{6,2},{7,5},{8,12},{9,11},{10,... | collective-permute-start | bytes 393224 | tf_op jit(solution)/shard_map/ppermute | solution.py:163
  47.2 5.6 %collective-permute-start.8 = (f32[16,2048]{1,0:T(8,128)S(1)}, f32[16,2048]{1,0:T(8,128)S(1)}, u32[]{:S(2)}, u32[]{:S(2)}) collective-permute-start(f32[16,2048]{1,0:T(8,128)S(1)} %add.19.refs_3_), channel_id=1, source_target_pairs={{0,2},{1,5},{2,0},{3,7},{4,6},{5,1},{6,4},{7,3},{8,10},{9,13},{10,... | collective-permute-start | bytes 393224 | tf_op jit(solution)/shard_map/ppermute | solution.py:163
  51.4 5.0 %collective-permute-start.7 = (f32[16,2048]{1,0:T(8,128)S(1)}, f32[16,2048]{1,0:T(8,128)S(1)}, u32[]{:S(2)}, u32[]{:S(2)}) collective-permute-start(f32[16,2048]{1,0:T(8,128)S(1)} %collective-permute-done.6.refs_2_), channel_id=1, source_target_pairs={{0,2},{1,5},{2,0},{3,7},{4,6},{5,1},{6,4},{7,3},{8,10},{9,13},{10,... | collective-permute-start | bytes 393224 | tf_op jit(solution)/shard_map/ppermute | solution.py:163
  56.7 1.3 %collective-permute-start.9 = (f32[64,128]{1,0:T(8,128)S(1)}, f32[64,128]{1,0:T(8,128)S(1)}, u32[]{:S(2)}, u32[]{:S(2)}) collective-permute-start(f32[64,128]{1,0:T(8,128)S(1)} %get-tuple-element.15.refs_0_), channel_id=1, source_target_pairs={{0,1},{1,0},{2,3},{3,2},{4,5},{5,4},{6,7},{7,6},{8,9},{9,8},{10,11... | collective-permute-start | bytes 98312 | tf_op jit(solution)/shard_map/ppermute | solution.py:195

commit v5 on v4

--- a/solution.py
+++ b/solution.py
@@ -86,24 +86,23 @@
 
 
 def col_kernel(parts, groups, width, which, *refs):
-    fits, kern, outs = refs[:groups], refs[groups : groups + parts], refs[groups + parts :]
+    fits, kern, (out,) = refs[:groups], refs[groups : groups + parts], refs[groups + parts :]
     fitted = fits[0][...].astype(F32)
     for ref in fits[1:]:
         fitted = fitted + ref[...].astype(F32)
     fitted = fitted.astype(BF16)
     rows = kern[0].shape[0]
-    steps = outs[0].shape[1] // width
-    ids = chunk_ids()
-    for i, out in zip(which, outs):
-
-        @pl.loop(0, steps)
-        def _(j):
-            col = tile_of(ids[i] * steps + j, width)
-            acc = None
-            for p in range(parts):
-                term = jnp.dot(fitted[:, p * rows : (p + 1) * rows], kern[p][:, col], preferred_element_type=F32)
-                acc = term if acc is None else acc + term
-            out[:, tile_of(j, width)] = acc
+    steps = out.shape[1] // width
+    first = chunk_ids()[which] * steps
+
+    @pl.loop(0, steps)
+    def _(j):
+        col = tile_of(first + j, width)
+        acc = None
+        for p in range(parts):
+            term = jnp.dot(fitted[:, p * rows : (p + 1) * rows], kern[p][:, col], preferred_element_type=F32)
+            acc = term if acc is None else acc + term
+        out[:, tile_of(j, width)] = acc
 
 
 def width_of(size, most):
@@ -139,10 +138,10 @@
     targets = fits[0].shape[0]
     size = kern[0].shape[1] // 4
     return pl.pallas_call(
-        functools.partial(col_kernel, len(kern), len(fits), width_of(size, 1024), which),
-        out_shape=[jax.ShapeDtypeStruct((targets, size), F32)] * len(which),
+        functools.partial(col_kernel, len(kern), len(fits), width_of(size, 2048), which),
+        out_shape=jax.ShapeDtypeStruct((targets, size), F32),
         in_specs=[VMEM] * (len(fits) + len(kern)),
-        out_specs=[VMEM] * len(which),
+        out_specs=VMEM,
         compiler_params=pltpu.CompilerParams(vmem_limit_bytes=4 * MIB),
     )(*fits, *kern)
 
@@ -197,14 +196,16 @@
 
 
 def image_kernel(scale, *refs):
-    chunks, (dir_ref, res_ref, pre_ref, image_ref, sums_ref) = refs[:4], refs[4:]
-    size = chunks[0].shape[1]
+    pieces, (dir_ref, res_ref, pre_ref, image_ref, sums_ref) = refs[:-5], refs[-5:]
+    size = pieces[0].shape[1]
+    each = len(pieces) // 4
     targets = sums_ref.shape[0] // 4
     sums = [jnp.zeros((targets, 1), F32)] * 4
-    for chunk, i in zip(chunks, chunk_ids()):
-        col = tile_of(i, size)
+    places = [chunk * each + i for chunk in chunk_ids() for i in range(each)]
+    for piece, place in zip(pieces, places):
+        col = tile_of(place, size)
         direction, resid, pre = dir_ref[:, col], res_ref[:, col], pre_ref[:, col]
-        image = chunk[...] * scale + 0.5 * direction
+        image = piece[...] * scale + 0.5 * direction
         image_ref[:, col] = image
         terms = (resid * resid * pre, direction * image, resid * pre * image, image * image * pre)
         sums = [old + jnp.sum(term, axis=1, keepdims=True) for old, term in zip(sums, terms)]
@@ -243,18 +244,17 @@
     num, full = points.shape[1], direction.shape
     kern, part = fit_parts(points, centres, direction, 4)
     fits = over_ctr(part)
-    (give_a,) = col_sums(fits, kern, (0,))
+    give_a = col_sums(fits, kern, 0)
     got_a = send_pts(give_a, along(0))
-    (keep_a,) = col_sums(fits, kern, (2,))
-    (give_b,) = col_sums(fits, kern, (1,))
+    keep_a = col_sums(fits, kern, 2)
+    give_b = col_sums(fits, kern, 1)
     got_b = send_pts(give_b, along(0))
     moved = send_pts(keep_a + got_a, along(1))
-    (keep_b,) = col_sums(fits, kern, (3,))
-    mine = moved + (keep_b + got_b)
-    mine = sum_over_rest(mine)
+    keep_b = col_sums(fits, kern, 3)
+    mine = sum_over_rest(moved + (keep_b + got_b))
     near = send_pts(mine, along(1))
     far = send_pts(mine, along(0))
-    last = send_pts(near, along(0))
+    last = send_pts(mine, lambda p, odd: p ^ 3)
     scale = 2048.0 / (num * num_pts)
     pre = precond.reshape(1, full[1])
     image, sums = small_call(

time: 59.5 us -> 56.6 us (0.951)
  waiting for transfers between devices: 16.5 us -> 15.1 us
  starting transfers between devices: 16.3 us -> 15.3 us
    ppermute x8, waiting for transfers between devices: 14.4 us -> 13 us  [send_pts(): return lax.ppermute(value, ('pts', 'ctr'), pairs)]
    ppermute x8, starting transfers between devices: 15.7 us -> 14.8 us  [send_pts(): return lax.ppermute(value, ('pts', 'ctr'), pairs)]
  transfers between devices with their start and end apart: 10 -> 10, of which waited for: 9 -> 10; matrix products, arithmetic and copies ran while one was open for 0% -> 0% of each run, Pallas kernels for 7% -> 6%
where the time goes in v5:
time: 56.6 us; the launch traced here: 56.4 us
  Pallas kernels  25.2 us (45%)
  starting transfers between devices  15.3 us (27%)
  waiting for transfers between devices  15.1 us (27%)
  between operations  0.71 us (1%)
    pallas_call x1, Pallas kernels, fit_parts(): pl.pallas_call(functools.partial(fit_kernel, parts, width_of(ctr, 1024)),...  18.7 us
    ppermute x8, starting transfers between devices, send_pts(): return lax.ppermute(value, ('pts', 'ctr'), pairs)  14.8 us
    ppermute x8, waiting for transfers between devices, send_pts(): return lax.ppermute(value, ('pts', 'ctr'), pairs)  13 us
    pallas_call x4, Pallas kernels, col_sums(): pl.pallas_call(functools.partial(col_kernel, len(kern), len(fits), width_...  4.76 us
    ppermute x2, waiting for transfers between devices, over_ctr(): lax.ppermute(value, 'ctr', [(c, (c + k) % num_ctr) for c in range(num_ctr)])  2.1 us
    pallas_call x2, Pallas kernels, small_call(): pl.pallas_call(kernel, out_shape=[jax.ShapeDtypeStruct(shape, F32) for sh...  1.69 us
  transfers between devices with their start and end apart: 10, of which 10 were waited for; matrix products, arithmetic and copies ran while one was open for 0% of the time, Pallas kernels for 6%

profile of v5, /device:TPU:0, one launch (start us, length us, event | category | flops | bytes accessed | tf_op | source)
XLA Modules:
  0.0 56.4 jit_solution(1248044691753425877)
XLA Ops:
  0.6 18.7 %shard_map.85 = (bf16[512,8192]{1,0:T(8,128)(2,1)S(1)}, bf16[512,8192]{1,0:T(8,128)(2,1)S(1)}, bf16[512,8192]{1,0:T(8,128)(2,1)S(1)}, bf16[512,8192]{1,0:T(8,128)(2,1)S(1)}, bf16[16,2048]{1,0:T(8,128)(2,1)S(1)}) custom-call(bf16[32,2048]{1,0:T(8,128)(2,1)} %pts_hbm.1, bf16[32,8192]{1,0:T(8,128)(2,1)} %cen_hbm.1, f32[16,8192]{1,0:T(8,128)} %refs_3_.1), custom_call_target="tpu_custom_call" | custom-call | tf_op jit(solution)/shard_map/pallas_call | solution.py:118
  19.4 0.5 collective-permute-start
  19.9 0.9 %collective-permute-done.refs_1_ = bf16[16,2048]{1,0:T(8,128)(2,1)S(1)} collective-permute-done((bf16[16,2048]{1,0:T(8,128)(2,1)S(1)}, bf16[16,2048]{1,0:T(8,128)(2,1)S(1)}, u32[]{:S(2)}, u32[]{:S(2)}) %collective-permute-start) | collective-permute-done | bytes 65568 | tf_op jit(solution)/shard_map/ppermute | solution.py:194
  20.8 1.2 %shard_map.87 = f32[16,2048]{1,0:T(8,128)S(1)} custom-call(bf16[16,2048]{1,0:T(8,128)(2,1)S(1)} %get-tuple-element.10.refs_0_, bf16[16,2048]{1,0:T(8,128)(2,1)S(1)} %collective-permute-done.refs_1_, bf16[512,8192]{1,0:T(8,128)(2,1)S(1)} %get-tuple-element.11.refs_2_, bf16[512,8192]{1,0:T(8,128)(2,1)S(1)} %get-tuple-element.12.refs_3_, ...), custom_call_target="tpu_custom_call" | custom-call | tf_op jit(solution)/shard_map/pallas_call | solution.py:140
  22.0 2.9 %collective-permute-start.1 = (f32[16,2048]{1,0:T(8,128)S(1)}, f32[16,2048]{1,0:T(8,128)S(1)}, u32[]{:S(2)}, u32[]{:S(2)}) collective-permute-start(f32[16,2048]{1,0:T(8,128)S(1)} %shard_map.87), channel_id=1, source_target_pairs={{0,2},{1,5},{2,0},{3,7},{4,6},{5,1},{6,4},{7,3},{8,10},{9,13},{10,... | collective-permute-start | bytes 393224 | tf_op jit(solution)/shard_map/ppermute | solution.py:162
  24.9 1.2 %shard_map.89 = f32[16,2048]{1,0:T(8,128)S(1)} custom-call(bf16[16,2048]{1,0:T(8,128)(2,1)S(1)} %get-tuple-element.10.refs_0_, bf16[16,2048]{1,0:T(8,128)(2,1)S(1)} %collective-permute-done.refs_1_, bf16[512,8192]{1,0:T(8,128)(2,1)S(1)} %get-tuple-element.11.refs_2_, bf16[512,8192]{1,0:T(8,128)(2,1)S(1)} %get-tuple-element.12.refs_3_, ...), custom_call_target="tpu_custom_call" | custom-call | tf_op jit(solution)/shard_map/pallas_call | solution.py:140
  26.1 0.0 collective-permute-start.3
  26.1 1.2 %shard_map.86 = f32[16,2048]{1,0:T(8,128)S(1)} custom-call(bf16[16,2048]{1,0:T(8,128)(2,1)S(1)} %get-tuple-element.10.refs_0_, bf16[16,2048]{1,0:T(8,128)(2,1)S(1)} %collective-permute-done.refs_1_, bf16[512,8192]{1,0:T(8,128)(2,1)S(1)} %get-tuple-element.11.refs_2_, bf16[512,8192]{1,0:T(8,128)(2,1)S(1)} %get-tuple-element.12.refs_3_, ...), custom_call_target="tpu_custom_call" | custom-call | tf_op jit(solution)/shard_map/pallas_call | solution.py:140
  27.3 0.5 collective-permute-done.1
  27.8 0.0 copy-start
  27.9 0.0 copy-start.1
  27.9 0.0 copy-start.3
  27.9 0.0 copy-start.2
  27.9 2.1 %collective-permute-start.2 = (f32[16,2048]{1,0:T(8,128)S(1)}, f32[16,2048]{1,0:T(8,128)S(1)}, u32[]{:S(2)}, u32[]{:S(2)}) collective-permute-start(f32[16,2048]{1,0:T(8,128)S(1)} %add.15), channel_id=1, source_target_pairs={{0,4},{1,3},{2,6},{3,1},{4,0},{5,7},{6,2},{7,5},{8,12},{9,11},{10,... | collective-permute-start | bytes 393224 | tf_op jit(solution)/shard_map/ppermute | solution.py:162
  30.0 1.2 %shard_map.88 = f32[16,2048]{1,0:T(8,128)S(1)} custom-call(bf16[16,2048]{1,0:T(8,128)(2,1)S(1)} %get-tuple-element.10.refs_0_, bf16[16,2048]{1,0:T(8,128)(2,1)S(1)} %collective-permute-done.refs_1_, bf16[512,8192]{1,0:T(8,128)(2,1)S(1)} %get-tuple-element.11.refs_2_, bf16[512,8192]{1,0:T(8,128)(2,1)S(1)} %get-tuple-element.12.refs_3_, ...), custom_call_target="tpu_custom_call" | custom-call | tf_op jit(solution)/shard_map/pallas_call | solution.py:140
  31.1 0.9 %collective-permute-done.3 = f32[16,2048]{1,0:T(8,128)S(1)} collective-permute-done((f32[16,2048]{1,0:T(8,128)S(1)}, f32[16,2048]{1,0:T(8,128)S(1)}, u32[]{:S(2)}, u32[]{:S(2)}) %collective-permute-start.3) | collective-permute-done | bytes 131104 | tf_op jit(solution)/shard_map/ppermute | solution.py:162
  32.0 0.9 %collective-permute-done.2 = f32[16,2048]{1,0:T(8,128)S(1)} collective-permute-done((f32[16,2048]{1,0:T(8,128)S(1)}, f32[16,2048]{1,0:T(8,128)S(1)}, u32[]{:S(2)}, u32[]{:S(2)}) %collective-permute-start.2) | collective-permute-done | bytes 131104 | tf_op jit(solution)/shard_map/ppermute | solution.py:162
  32.9 2.2 %collective-permute-start.4 = (f32[16,2048]{1,0:T(8,128)S(1)}, f32[16,2048]{1,0:T(8,128)S(1)}, u32[]{:S(2)}, u32[]{:S(2)}) collective-permute-start(f32[16,2048]{1,0:T(8,128)S(1)} %add_add_fusion), channel_id=1, source_target_pairs={{0,8},{1,9},{2,10},{3,11},{4,12},{5,13},{6,14},{7,15},{8,0},{9,1},... | collective-permute-start | bytes 393224 | tf_op jit(solution)/shard_map/ppermute | solution.py:162
  35.1 2.9 %collective-permute-done.4 = f32[16,2048]{1,0:T(8,128)S(1)} collective-permute-done((f32[16,2048]{1,0:T(8,128)S(1)}, f32[16,2048]{1,0:T(8,128)S(1)}, u32[]{:S(2)}, u32[]{:S(2)}) %collective-permute-start.4) | collective-permute-done | bytes 131104 | tf_op jit(solution)/shard_map/ppermute | solution.py:162
  38.1 4.0 %collective-permute-start.5 = (f32[16,2048]{1,0:T(8,128)S(1)}, f32[16,2048]{1,0:T(8,128)S(1)}, u32[]{:S(2)}, u32[]{:S(2)}) collective-permute-start(f32[16,2048]{1,0:T(8,128)S(1)} %add.18), channel_id=1, source_target_pairs={{0,24},{1,25},{2,26},{3,27},{4,28},{5,29},{6,30},{7,31},{8,16},{9,... | collective-permute-start | bytes 393224 | tf_op jit(solution)/shard_map/ppermute | solution.py:162
  42.1 3.1 %collective-permute-done.5 = f32[16,2048]{1,0:T(8,128)S(1)} collective-permute-done((f32[16,2048]{1,0:T(8,128)S(1)}, f32[16,2048]{1,0:T(8,128)S(1)}, u32[]{:S(2)}, u32[]{:S(2)}) %collective-permute-start.5) | collective-permute-done | bytes 131104 | tf_op jit(solution)/shard_map/ppermute | solution.py:162
  45.2 2.7 %collective-permute-start.6 = (f32[16,2048]{1,0:T(8,128)S(1)}, f32[16,2048]{1,0:T(8,128)S(1)}, u32[]{:S(2)}, u32[]{:S(2)}) collective-permute-start(f32[16,2048]{1,0:T(8,128)S(1)} %add.19.refs_3_), channel_id=1, source_target_pairs={{0,6},{1,7},{2,4},{3,5},{4,2},{5,3},{6,0},{7,1},{8,14},{9,15},{10,... | collective-permute-start | bytes 393224 | tf_op jit(solution)/shard_map/ppermute | solution.py:162
  47.9 0.5 collective-permute-start.7
  48.5 0.3 collective-permute-start.8
  48.8 2.4 %collective-permute-done.6.refs_0_ = f32[16,2048]{1,0:T(8,128)S(1)} collective-permute-done((f32[16,2048]{1,0:T(8,128)S(1)}, f32[16,2048]{1,0:T(8,128)S(1)}, u32[]{:S(2)}, u32[]{:S(2)}) %collective-permute-start.6) | collective-permute-done | bytes 131104 | tf_op jit(solution)/shard_map/ppermute | solution.py:162
  51.1 1.8 %collective-permute-done.7.refs_1_ = f32[16,2048]{1,0:T(8,128)S(1)} collective-permute-done((f32[16,2048]{1,0:T(8,128)S(1)}, f32[16,2048]{1,0:T(8,128)S(1)}, u32[]{:S(2)}, u32[]{:S(2)}) %collective-permute-start.7) | collective-permute-done | bytes 131104 | tf_op jit(solution)/shard_map/ppermute | solution.py:162
  52.9 0.5 collective-permute-done.8.refs_2_
  53.5 0.0 copy-done
  53.5 0.4 shard_map.90
  53.8 0.1 collective-permute-start.9
  53.9 1.2 %collective-permute-done.9.refs_1_ = f32[64,128]{1,0:T(8,128)S(1)} collective-permute-done((f32[64,128]{1,0:T(8,128)S(1)}, f32[64,128]{1,0:T(8,128)S(1)}, u32[]{:S(2)}, u32[]{:S(2)}) %collective-permute-start.9) | collective-permute-done | bytes 32800 | tf_op jit(solution)/shard_map/ppermute | solution.py:194
  55.1 1.3 %shard_map.91 = (f32[16,8192]{1,0:T(8,128)}, f32[16,8192]{1,0:T(8,128)}, f32[16,8192]{1,0:T(8,128)}) custom-call(f32[64,128]{1,0:T(8,128)S(1)} %get-tuple-element.15.refs_0_, f32[64,128]{1,0:T(8,128)S(1)} %collective-permute-done.9.refs_1_, f32[16,8192]{1,0:T(8,128)S(1)} %get-tuple-element.16.refs_2_, f32[16,8192]{1,0:T(8,128)S(1)} %copy-done, ...), custom_call_target="tpu_custom_call" | custom-call | tf_op jit(solution)/shard_map/pallas_call | solution.py:233
  (7 shorter events, 0.1 us)
Async XLA Ops:
  19.4 1.4 %collective-permute-start = (bf16[16,2048]{1,0:T(8,128)(2,1)S(1)}, bf16[16,2048]{1,0:T(8,128)(2,1)S(1)}, u32[]{:S(2)}, u32[]{:S(2)}) collective-permute-start(bf16[16,2048]{1,0:T(8,128)(2,1)S(1)} %get-tuple-element.10.refs_0_), channel_id=1, source_target_pairs={{0,1},{1,0},{2,3},{3,2},{4,5},{5,4},{6,7},{7,6},{8,9},{9,8},{10,11... | collective-permute-start | bytes 196616 | tf_op jit(solution)/shard_map/ppermute | solution.py:194
  22.0 5.9 %collective-permute-start.1 = (f32[16,2048]{1,0:T(8,128)S(1)}, f32[16,2048]{1,0:T(8,128)S(1)}, u32[]{:S(2)}, u32[]{:S(2)}) collective-permute-start(f32[16,2048]{1,0:T(8,128)S(1)} %shard_map.87), channel_id=1, source_target_pairs={{0,2},{1,5},{2,0},{3,7},{4,6},{5,1},{6,4},{7,3},{8,10},{9,13},{10,... | collective-permute-start | bytes 393224 | tf_op jit(solution)/shard_map/ppermute | solution.py:162
  26.1 6.0 %collective-permute-start.3 = (f32[16,2048]{1,0:T(8,128)S(1)}, f32[16,2048]{1,0:T(8,128)S(1)}, u32[]{:S(2)}, u32[]{:S(2)}) collective-permute-start(f32[16,2048]{1,0:T(8,128)S(1)} %shard_map.89), channel_id=1, source_target_pairs={{0,2},{1,5},{2,0},{3,7},{4,6},{5,1},{6,4},{7,3},{8,10},{9,13},{10,... | collective-permute-start | bytes 393224 | tf_op jit(solution)/shard_map/ppermute | solution.py:162
  27.8 25.6 %copy-start = (f32[16,8192]{1,0:T(8,128)S(1)}, f32[16,8192]{1,0:T(8,128)}, u32[]{:S(2)}) copy-start(f32[16,8192]{1,0:T(8,128)} %refs_3_.1) | copy-start | bytes 1572868
  27.9 25.6 %copy-start.1 = (f32[16,8192]{1,0:T(8,128)S(1)}, f32[16,8192]{1,0:T(8,128)}, u32[]{:S(2)}) copy-start(f32[16,8192]{1,0:T(8,128)} %refs_4_.3) | copy-start | bytes 1572868
  27.9 25.6 %copy-start.3 = (f32[8192]{0:T(1024)S(1)}, f32[8192]{0:T(1024)}, u32[]{:S(2)}) copy-start(f32[8192]{0:T(1024)} %param.11) | copy-start | bytes 98308
  27.9 27.2 %copy-start.2 = (f32[16,8192]{1,0:T(8,128)S(1)}, f32[16,8192]{1,0:T(8,128)}, u32[]{:S(2)}) copy-start(f32[16,8192]{1,0:T(8,128)} %refs_6_.1) | copy-start | bytes 1572868
  27.9 5.0 %collective-permute-start.2 = (f32[16,2048]{1,0:T(8,128)S(1)}, f32[16,2048]{1,0:T(8,128)S(1)}, u32[]{:S(2)}, u32[]{:S(2)}) collective-permute-start(f32[16,2048]{1,0:T(8,128)S(1)} %add.15), channel_id=1, source_target_pairs={{0,4},{1,3},{2,6},{3,1},{4,0},{5,7},{6,2},{7,5},{8,12},{9,11},{10,... | collective-permute-start | bytes 393224 | tf_op jit(solution)/shard_map/ppermute | solution.py:162
  32.9 5.1 %collective-permute-start.4 = (f32[16,2048]{1,0:T(8,128)S(1)}, f32[16,2048]{1,0:T(8,128)S(1)}, u32[]{:S(2)}, u32[]{:S(2)}) collective-permute-start(f32[16,2048]{1,0:T(8,128)S(1)} %add_add_fusion), channel_id=1, source_target_pairs={{0,8},{1,9},{2,10},{3,11},{4,12},{5,13},{6,14},{7,15},{8,0},{9,1},... | collective-permute-start | bytes 393224 | tf_op jit(solution)/shard_map/ppermute | solution.py:162
  38.1 7.1 %collective-permute-start.5 = (f32[16,2048]{1,0:T(8,128)S(1)}, f32[16,2048]{1,0:T(8,128)S(1)}, u32[]{:S(2)}, u32[]{:S(2)}) collective-permute-start(f32[16,2048]{1,0:T(8,128)S(1)} %add.18), channel_id=1, source_target_pairs={{0,24},{1,25},{2,26},{3,27},{4,28},{5,29},{6,30},{7,31},{8,16},{9,... | collective-permute-start | bytes 393224 | tf_op jit(solution)/shard_map/ppermute | solution.py:162
  45.2 5.9 %collective-permute-start.6 = (f32[16,2048]{1,0:T(8,128)S(1)}, f32[16,2048]{1,0:T(8,128)S(1)}, u32[]{:S(2)}, u32[]{:S(2)}) collective-permute-start(f32[16,2048]{1,0:T(8,128)S(1)} %add.19.refs_3_), channel_id=1, source_target_pairs={{0,6},{1,7},{2,4},{3,5},{4,2},{5,3},{6,0},{7,1},{8,14},{9,15},{10,... | collective-permute-start | bytes 393224 | tf_op jit(solution)/shard_map/ppermute | solution.py:162
  47.9 5.0 %collective-permute-start.7 = (f32[16,2048]{1,0:T(8,128)S(1)}, f32[16,2048]{1,0:T(8,128)S(1)}, u32[]{:S(2)}, u32[]{:S(2)}) collective-permute-start(f32[16,2048]{1,0:T(8,128)S(1)} %add.19.refs_3_), channel_id=1, source_target_pairs={{0,2},{1,5},{2,0},{3,7},{4,6},{5,1},{6,4},{7,3},{8,10},{9,13},{10,... | collective-permute-start | bytes 393224 | tf_op jit(solution)/shard_map/ppermute | solution.py:162
  48.5 5.0 %collective-permute-start.8 = (f32[16,2048]{1,0:T(8,128)S(1)}, f32[16,2048]{1,0:T(8,128)S(1)}, u32[]{:S(2)}, u32[]{:S(2)}) collective-permute-start(f32[16,2048]{1,0:T(8,128)S(1)} %add.19.refs_3_), channel_id=1, source_target_pairs={{0,4},{1,3},{2,6},{3,1},{4,0},{5,7},{6,2},{7,5},{8,12},{9,11},{10,... | collective-permute-start | bytes 393224 | tf_op jit(solution)/shard_map/ppermute | solution.py:162
  53.8 1.3 %collective-permute-start.9 = (f32[64,128]{1,0:T(8,128)S(1)}, f32[64,128]{1,0:T(8,128)S(1)}, u32[]{:S(2)}, u32[]{:S(2)}) collective-permute-start(f32[64,128]{1,0:T(8,128)S(1)} %get-tuple-element.15.refs_0_), channel_id=1, source_target_pairs={{0,1},{1,0},{2,3},{3,2},{4,5},{5,4},{6,7},{7,6},{8,9},{9,8},{10,11... | collective-permute-start | bytes 98312 | tf_op jit(solution)/shard_map/ppermute | solution.py:194

commit v6 on v5

v6 whole, which is shorter than its diff:
```python
import functools
import math

import jax
import jax.numpy as jnp
from jax import lax
from jax.experimental import pallas as pl
from jax.experimental.pallas import tpu as pltpu
from jax.sharding import PartitionSpec as P

MIB = 2**20
F32 = jnp.float32
BF16 = jnp.bfloat16
RATE = 0.25 * math.log2(math.e)
DEPTH = 128
VMEM = pl.BlockSpec(memory_space=pltpu.VMEM)


def tile_of(index, size):
    return pl.ds(pl.multiple_of(index * size, size), size)


def split3(value):
    first = value.astype(BF16).astype(F32)
    rest = value - first
    second = rest.astype(BF16).astype(F32)
    return first, second, rest - second


def rows_of(rows, block):
    at = lax.broadcasted_iota(jnp.int32, block, 0)
    out = jnp.zeros(block, F32)
    for i, row in enumerate(rows):
        out = jnp.where(at == i, row, out)
    return out


def digits():
    me, odd = lax.axis_index("pts"), lax.axis_index("ctr") % 2
    low, high = me % 2, (me // 2) % 2
    return jnp.where(odd == 0, low, high), jnp.where(odd == 0, high, low)


def chunk_ids():
    a, b = digits()
    return 2 * (1 - a) + (1 - b), 2 * (1 - a) + b, 2 * a + (1 - b), 2 * a + b


def fit_kernel(width, across, pts_hbm, cen_hbm, dir_hbm, *refs):
    kern, (fit_ref, pts_ref, cen_ref, dir_ref, xa_ref, ca_ref, db_ref, sum_ref, sems) = refs[:4], refs[4:]
    pairs = ((pts_hbm, pts_ref), (cen_hbm, cen_ref), (dir_hbm, dir_ref))
    copies = [pltpu.make_async_copy(source, target, sems.at[i]) for i, (source, target) in enumerate(pairs)]
    for copy in copies:
        copy.start()
    feat, num = pts_ref.shape
    ctr = cen_ref.shape[1]
    copies[0].wait()
    pts = pts_ref[...].astype(F32)
    terms = list(split3(pts * RATE))
    norm = split3(jnp.sum(pts * pts, axis=0, keepdims=True) * (-0.5 * RATE))
    terms.append(rows_of(list(norm) + [1.0, 1.0, 1.0], (DEPTH - 3 * feat, num)))
    xa_ref[...] = jnp.concatenate(terms, axis=0).astype(BF16)
    copies[1].wait()
    cen = cen_ref[...]
    for i in range(3):
        ca_ref[i * feat : (i + 1) * feat, :] = cen
    cen = cen.astype(F32)
    norm = split3(jnp.sum(cen * cen, axis=0, keepdims=True) * (-0.5 * RATE))
    ca_ref[3 * feat :, :] = rows_of([1.0, 1.0, 1.0] + list(norm), (DEPTH - 3 * feat, ctr)).astype(BF16)
    copies[2].wait()
    db_ref[...] = dir_ref[...].astype(BF16)
    sum_ref[...] = jnp.zeros(sum_ref.shape, F32)
    steps = ctr // 4 // width
    for i, out in zip(chunk_ids(), kern):

        @pl.loop(0, steps)
        def _(j):
            col = tile_of(i * steps + j, width)
            cen = ca_ref[:, col].T
            for p in range(num // across):
                row = slice(p * across, (p + 1) * across)
                tile = jnp.exp2(jnp.dot(cen, xa_ref[:, row], preferred_element_type=F32)).astype(BF16)
                out[tile_of(j, width), row] = tile
                sum_ref[:, row] += jnp.dot(db_ref[:, col], tile, preferred_element_type=F32)

    fit_ref[...] = sum_ref[...].astype(BF16)


def col_kernel(width, *refs):
    fits, kern, out = refs[:-2], refs[-2], refs[-1]
    fitted = fits[0][...].astype(F32)
    for ref in fits[1:]:
        fitted = fitted + ref[...].astype(F32)
    fitted = fitted.astype(BF16)

    @pl.loop(0, out.shape[1] // width)
    def _(j):
        rows = tile_of(j, width)
        out[:, rows] = lax.dot_general(fitted, kern[rows, :], (((1,), (1,)), ((), ())), preferred_element_type=F32)


def width_of(size, most):
    width = most
    while size % width:
        width //= 2
    return width


def fit_parts(points, centres, direction):
    num, ctr = points.shape[1], centres.shape[1]
    targets = direction.shape[0]
    out = pl.pallas_call(
        functools.partial(fit_kernel, width_of(ctr // 4, 2048), width_of(num, 512)),
        out_shape=[jax.ShapeDtypeStruct((ctr // 4, num), BF16)] * 4 + [jax.ShapeDtypeStruct((targets, num), BF16)],
        in_specs=[pl.BlockSpec(memory_space=pl.ANY)] * 3,
        out_specs=[VMEM] * 5,
        scratch_shapes=[
            pltpu.VMEM(points.shape, BF16),
            pltpu.VMEM(centres.shape, BF16),
            pltpu.VMEM(direction.shape, F32),
            pltpu.VMEM((DEPTH, num), BF16),
            pltpu.VMEM((DEPTH, ctr), BF16),
            pltpu.VMEM((targets, ctr), BF16),
            pltpu.VMEM((targets, num), F32),
            pltpu.SemaphoreType.DMA((3,)),
        ],
        compiler_params=pltpu.CompilerParams(vmem_limit_bytes=18 * MIB),
    )(*[pltpu.with_memory_space_constraint(value, pltpu.HBM) for value in (points, centres, direction)])
    return out[:4], out[4]


def col_sums(fits, kern):
    targets = fits[0].shape[0]
    size = kern.shape[0]
    return pl.pallas_call(
        functools.partial(col_kernel, width_of(size, 2048)),
        out_shape=jax.ShapeDtypeStruct((targets, size), F32),
        in_specs=[VMEM] * (len(fits) + 1),
        out_specs=VMEM,
        compiler_params=pltpu.CompilerParams(vmem_limit_bytes=4 * MIB),
    )(*fits, kern)


def radices(size):
    out, prime = [], 2
    while size > 1:
        while size % prime == 0:
            out.append(prime)
            size //= prime
        prime += 1
    return out


def send_pts(value, partner):
    num_pts, num_ctr = lax.axis_size("pts"), lax.axis_size("ctr")
    pairs = [(p * num_ctr + c, partner(p, c % 2) * num_ctr + c) for p in range(num_pts) for c in range(num_ctr)]
    return lax.ppermute(value, ("pts", "ctr"), pairs)


def along(phase):
    return lambda p, odd: p ^ (1 + (odd ^ phase))


def sum_over_rest(value):
    rest = lax.axis_size("pts") // 4
    twos = rest & -rest
    for k in range(twos.bit_length() - 1):
        mask = 4 * (2 * 2**k - 1)
        value = value + send_pts(value, lambda p, odd: p ^ mask)
    me, stride = lax.axis_index("pts"), 4 * twos
    for radix in radices(rest // twos):
        got = [value]
        for k in range(1, radix):

            def partner(p, odd):
                d = (p // stride) % radix
                return p + ((d + k) % radix - d) * stride

            got.append(send_pts(value, partner))
        mine, stack = (me // stride) % radix, jnp.stack(got)
        value = sum(lax.dynamic_index_in_dim(stack, (mine - d) % radix, 0, False) for d in range(radix))
        stride *= radix
    return value


def over_ctr(value):
    num_ctr = lax.axis_size("ctr")
    return [value] + [
        lax.ppermute(value, "ctr", [(c, (c + k) % num_ctr) for c in range(num_ctr)]) for k in range(1, num_ctr)
    ]


def sums_kernel(scale, steps, *refs):
    chunks, others = refs[: len(steps)], refs[len(steps) : -4]
    dir_ref, res_ref, pre_ref, sums_ref = refs[-4:]
    size = chunks[0].shape[1]
    targets = sums_ref.shape[0] // 4
    sums = [other[i * targets : (i + 1) * targets, :1] for other in others for i in range(4)]
    sums = sums or [jnp.zeros((targets, 1), F32)] * 4
    ids = chunk_ids()
    for chunk, step in zip(chunks, steps):
        col = tile_of(ids[step], size)
        direction, resid, pre = dir_ref[:, col], res_ref[:, col], pre_ref[:, col]
        image = chunk[...] * scale + 0.5 * direction
        terms = (resid * resid * pre, direction * image, resid * pre * image, image * image * pre)
        sums = [old + jnp.sum(term, axis=1, keepdims=True) for old, term in zip(sums, terms)]
    for i, value in enumerate(sums):
        sums_ref[i * targets : (i + 1) * targets, :] = jnp.broadcast_to(value, (targets, 128))


def step_kernel(scale, groups, *refs):
    chunks, (dir_ref, res_ref, pre_ref, coef_ref) = refs[groups : groups + 4], refs[groups + 4 : groups + 8]
    coef_out, res_out, dir_out = refs[groups + 8 :]
    targets, size = chunks[0].shape
    total = refs[0][...]
    for ref in refs[1:groups]:
        total = total + ref[...]
    rz, curv, cross, square = [total[i * targets : (i + 1) * targets, :1] for i in range(4)]
    alpha = rz / curv
    beta = (rz - alpha * (2.0 * cross - alpha * square)) / rz
    for chunk, place in zip(chunks, chunk_ids()):
        col = tile_of(place, size)
        direction = dir_ref[:, col]
        coef_out[:, col] = coef_ref[:, col] + alpha * direction
        resid = res_ref[:, col] - alpha * (chunk[...] * scale + 0.5 * direction)
        res_out[:, col] = resid
        dir_out[:, col] = pre_ref[:, col] * resid + beta * direction


def sums_over(chunks, steps, others, scale, direction, resid, pre):
    args = [*chunks, *others, direction, resid, pre]
    return pl.pallas_call(
        functools.partial(sums_kernel, scale, steps),
        out_shape=jax.ShapeDtypeStruct((4 * direction.shape[0], 128), F32),
        in_specs=[VMEM] * len(args),
        out_specs=VMEM,
        compiler_params=pltpu.CompilerParams(vmem_limit_bytes=4 * MIB),
    )(*args)


def step_of(sums, chunks, scale, direction, resid, pre, coef):
    args = [*sums, *chunks, direction, resid, pre, coef]
    return pl.pallas_call(
        functools.partial(step_kernel, scale, len(sums)),
        out_shape=[jax.ShapeDtypeStruct(direction.shape, F32)] * 3,
        in_specs=[VMEM] * len(args),
        out_specs=[VMEM] * 3,
        compiler_params=pltpu.CompilerParams(vmem_limit_bytes=8 * MIB),
    )(*args)


def shards(points, centres, coef, resid, direction, precond):
    num_pts, num_ctr = lax.axis_size("pts"), lax.axis_size("ctr")
    num, full = points.shape[1], direction.shape
    kern, part = fit_parts(points, centres, direction)
    fits = over_ctr(part)
    give_a = col_sums(fits, kern[0])
    got_a = send_pts(give_a, along(0))
    keep_a = col_sums(fits, kern[2])
    give_b = col_sums(fits, kern[1])
    got_b = send_pts(give_b, along(0))
    moved = send_pts(keep_a + got_a, along(1))
    keep_b = col_sums(fits, kern[3])
    mine = sum_over_rest(moved + (keep_b + got_b))
    near = send_pts(mine, along(1))
    far = send_pts(mine, along(0))
    last = send_pts(mine, lambda p, odd: p ^ 3)
    scale = 2048.0 / (num * num_pts)
    pre = precond.reshape(1, full[1])
    rest = (scale, direction, resid, pre)
    early = sums_over([last, mine], (0, 3), [], *rest)
    sums = sums_over([far, near], (1, 2), [early], *rest)
    return step_of(over_ctr(sums), [last, far, near, mine], *rest, coef)


def solution(mesh):
    return jax.shard_map(
        shards,
        mesh=mesh,
        in_specs=(
            P(None, "pts"),
            P(None, "ctr"),
            P(None, "ctr"),
            P(None, "ctr"),
            P(None, "ctr"),
            P("ctr"),
        ),
        out_specs=(P(None, "ctr"), P(None, "ctr"), P(None, "ctr")),
        check_vma=False,
    )
```

time: 56.6 us -> 55.1 us (0.973)
  waiting for transfers between devices: 15.1 us -> 13.2 us
    ppermute x8, waiting for transfers between devices: 13 us -> 11.1 us  [send_pts(): return lax.ppermute(value, ('pts', 'ctr'), pairs)]
    pallas_call x7 -> x8, Pallas kernels: 25.2 us -> 25.7 us  [the longest x1 14.8 us: fit_parts(): pl.pallas_call(functools.partial(fit_kernel, width_of(ctr // 4, 2048), wi...]
  transfers between devices with their start and end apart: 10 -> 10, of which waited for: 10 -> 8; matrix products, arithmetic and copies ran while one was open for 0% -> 0% of each run, Pallas kernels for 6% -> 13%
where the time goes in v6:
time: 55.1 us; the launch traced here: 55 us
  Pallas kernels  25.7 us (47%)
  starting transfers between devices  15.3 us (28%)
  waiting for transfers between devices  13.2 us (24%)
  between operations  0.7 us (1%)
    ppermute x8, starting transfers between devices, send_pts(): return lax.ppermute(value, ('pts', 'ctr'), pairs)  14.8 us
    pallas_call x1, Pallas kernels, fit_parts(): pl.pallas_call(functools.partial(fit_kernel, width_of(ctr // 4, 2048), wi...  14.8 us
    ppermute x8, waiting for transfers between devices, send_pts(): return lax.ppermute(value, ('pts', 'ctr'), pairs)  11.1 us
    pallas_call x4, Pallas kernels, col_sums(): pl.pallas_call(functools.partial(col_kernel, width_of(size, 2048)), out_s...  9.05 us
    ppermute x2, waiting for transfers between devices, over_ctr(): lax.ppermute(value, 'ctr', [(c, (c + k) % num_ctr) for c in range(num_ctr)])  2.1 us
    pallas_call x1, Pallas kernels, step_of(): pl.pallas_call(functools.partial(step_kernel, scale, len(sums)), out_shap...  1.32 us
  transfers between devices with their start and end apart: 10, of which 8 were waited for; matrix products, arithmetic and copies ran while one was open for 0% of the time, Pallas kernels for 13%

profile of v6, /device:TPU:0, one launch (start us, length us, event | category | flops | bytes accessed | tf_op | source)
XLA Modules:
  0.0 55.0 jit_solution(1123664633545099015)
XLA Ops:
  0.6 14.8 %shard_map.85 = (bf16[2048,2048]{1,0:T(8,128)(2,1)S(1)}, bf16[2048,2048]{1,0:T(8,128)(2,1)S(1)}, bf16[2048,2048]{1,0:T(8,128)(2,1)S(1)}, bf16[2048,2048]{1,0:T(8,128)(2,1)S(1)}, bf16[16,2048]{1,0:T(8,128)(2,1)S(1)}) custom-call(bf16[32,2048]{1,0:T(8,128)(2,1)} %pts_hbm.1, bf16[32,8192]{1,0:T(8,128)(2,1)} %cen_hbm.1, f32[16,8192]{1,0:T(8,128)} %refs_6_.1), custom_call_target="tpu_custom_call" | custom-call | tf_op jit(solution)/shard_map/pallas_call | solution.py:112
  15.4 0.5 collective-permute-start
  15.9 0.9 %collective-permute-done.refs_1_ = bf16[16,2048]{1,0:T(8,128)(2,1)S(1)} collective-permute-done((bf16[16,2048]{1,0:T(8,128)(2,1)S(1)}, bf16[16,2048]{1,0:T(8,128)(2,1)S(1)}, u32[]{:S(2)}, u32[]{:S(2)}) %collective-permute-start) | collective-permute-done | bytes 65568 | tf_op jit(solution)/shard_map/ppermute | solution.py:189
  16.8 2.3 %shard_map.87 = f32[16,2048]{1,0:T(8,128)S(1)} custom-call(bf16[16,2048]{1,0:T(8,128)(2,1)S(1)} %get-tuple-element.8.refs_0_, bf16[16,2048]{1,0:T(8,128)(2,1)S(1)} %collective-permute-done.refs_1_, bf16[2048,2048]{1,0:T(8,128)(2,1)S(1)} %get-tuple-element.10.refs_2_), custom_call_target="tpu_custom_call" | custom-call | tf_op jit(solution)/shard_map/pallas_call | solution.py:135
  19.1 2.9 %collective-permute-start.1 = (f32[16,2048]{1,0:T(8,128)S(1)}, f32[16,2048]{1,0:T(8,128)S(1)}, u32[]{:S(2)}, u32[]{:S(2)}) collective-permute-start(f32[16,2048]{1,0:T(8,128)S(1)} %shard_map.87), channel_id=1, source_target_pairs={{0,2},{1,5},{2,0},{3,7},{4,6},{5,1},{6,4},{7,3},{8,10},{9,13},{10,... | collective-permute-start | bytes 393224 | tf_op jit(solution)/shard_map/ppermute | solution.py:157
  21.9 2.3 %shard_map.89 = f32[16,2048]{1,0:T(8,128)S(1)} custom-call(bf16[16,2048]{1,0:T(8,128)(2,1)S(1)} %get-tuple-element.8.refs_0_, bf16[16,2048]{1,0:T(8,128)(2,1)S(1)} %collective-permute-done.refs_1_, bf16[2048,2048]{1,0:T(8,128)(2,1)S(1)} %get-tuple-element.12.refs_2_), custom_call_target="tpu_custom_call" | custom-call | tf_op jit(solution)/shard_map/pallas_call | solution.py:135
  24.2 0.0 collective-permute-start.3
  24.2 0.0 copy-start.3
  24.2 2.3 %shard_map.86 = f32[16,2048]{1,0:T(8,128)S(1)} custom-call(bf16[16,2048]{1,0:T(8,128)(2,1)S(1)} %get-tuple-element.8.refs_0_, bf16[16,2048]{1,0:T(8,128)(2,1)S(1)} %collective-permute-done.refs_1_, bf16[2048,2048]{1,0:T(8,128)(2,1)S(1)} %get-tuple-element.9.refs_2_), custom_call_target="tpu_custom_call" | custom-call | tf_op jit(solution)/shard_map/pallas_call | solution.py:135
  26.5 0.0 collective-permute-done.1
  26.6 2.1 %collective-permute-start.2 = (f32[16,2048]{1,0:T(8,128)S(1)}, f32[16,2048]{1,0:T(8,128)S(1)}, u32[]{:S(2)}, u32[]{:S(2)}) collective-permute-start(f32[16,2048]{1,0:T(8,128)S(1)} %add.15), channel_id=1, source_target_pairs={{0,4},{1,3},{2,6},{3,1},{4,0},{5,7},{6,2},{7,5},{8,12},{9,11},{10,... | collective-permute-start | bytes 393224 | tf_op jit(solution)/shard_map/ppermute | solution.py:157
  28.7 2.3 %shard_map.88 = f32[16,2048]{1,0:T(8,128)S(1)} custom-call(bf16[16,2048]{1,0:T(8,128)(2,1)S(1)} %get-tuple-element.8.refs_0_, bf16[16,2048]{1,0:T(8,128)(2,1)S(1)} %collective-permute-done.refs_1_, bf16[2048,2048]{1,0:T(8,128)(2,1)S(1)} %get-tuple-element.11.refs_2_), custom_call_target="tpu_custom_call" | custom-call | tf_op jit(solution)/shard_map/pallas_call | solution.py:135
  30.9 0.0 collective-permute-done.3
  30.9 0.7 %collective-permute-done.2 = f32[16,2048]{1,0:T(8,128)S(1)} collective-permute-done((f32[16,2048]{1,0:T(8,128)S(1)}, f32[16,2048]{1,0:T(8,128)S(1)}, u32[]{:S(2)}, u32[]{:S(2)}) %collective-permute-start.2) | collective-permute-done | bytes 131104 | tf_op jit(solution)/shard_map/ppermute | solution.py:157
  31.6 2.1 %collective-permute-start.4 = (f32[16,2048]{1,0:T(8,128)S(1)}, f32[16,2048]{1,0:T(8,128)S(1)}, u32[]{:S(2)}, u32[]{:S(2)}) collective-permute-start(f32[16,2048]{1,0:T(8,128)S(1)} %add_add_fusion), channel_id=1, source_target_pairs={{0,8},{1,9},{2,10},{3,11},{4,12},{5,13},{6,14},{7,15},{8,0},{9,1},... | collective-permute-start | bytes 393224 | tf_op jit(solution)/shard_map/ppermute | solution.py:157
  33.8 2.9 %collective-permute-done.4 = f32[16,2048]{1,0:T(8,128)S(1)} collective-permute-done((f32[16,2048]{1,0:T(8,128)S(1)}, f32[16,2048]{1,0:T(8,128)S(1)}, u32[]{:S(2)}, u32[]{:S(2)}) %collective-permute-start.4) | collective-permute-done | bytes 131104 | tf_op jit(solution)/shard_map/ppermute | solution.py:157
  36.7 4.1 %collective-permute-start.5 = (f32[16,2048]{1,0:T(8,128)S(1)}, f32[16,2048]{1,0:T(8,128)S(1)}, u32[]{:S(2)}, u32[]{:S(2)}) collective-permute-start(f32[16,2048]{1,0:T(8,128)S(1)} %add.18), channel_id=1, source_target_pairs={{0,24},{1,25},{2,26},{3,27},{4,28},{5,29},{6,30},{7,31},{8,16},{9,... | collective-permute-start | bytes 393224 | tf_op jit(solution)/shard_map/ppermute | solution.py:157
  40.8 3.1 %collective-permute-done.5 = f32[16,2048]{1,0:T(8,128)S(1)} collective-permute-done((f32[16,2048]{1,0:T(8,128)S(1)}, f32[16,2048]{1,0:T(8,128)S(1)}, u32[]{:S(2)}, u32[]{:S(2)}) %collective-permute-start.5) | collective-permute-done | bytes 131104 | tf_op jit(solution)/shard_map/ppermute | solution.py:157
  43.9 2.7 %collective-permute-start.8 = (f32[16,2048]{1,0:T(8,128)S(1)}, f32[16,2048]{1,0:T(8,128)S(1)}, u32[]{:S(2)}, u32[]{:S(2)}) collective-permute-start(f32[16,2048]{1,0:T(8,128)S(1)} %add.19.refs_1_.refs_5_), channel_id=1, source_target_pairs={{0,6},{1,7},{2,4},{3,5},{4,2},{5,3},{6,0},{7,1},{8,14},{9,15},{10,... | collective-permute-start | bytes 393224 | tf_op jit(solution)/shard_map/ppermute | solution.py:157
  46.7 0.5 collective-permute-start.7
  47.2 0.3 collective-permute-start.6
  47.5 2.4 %collective-permute-done.8.refs_0_.refs_2_ = f32[16,2048]{1,0:T(8,128)S(1)} collective-permute-done((f32[16,2048]{1,0:T(8,128)S(1)}, f32[16,2048]{1,0:T(8,128)S(1)}, u32[]{:S(2)}, u32[]{:S(2)}) %collective-permute-start.8) | collective-permute-done | bytes 131104 | tf_op jit(solution)/shard_map/ppermute | solution.py:157
  49.9 0.0 copy-done
  49.9 0.0 copy-done.1
  49.9 0.0 copy-done.3
  49.9 0.2 shard_map.90.refs_2_
  50.1 1.5 %collective-permute-done.7.refs_1_.refs_4_ = f32[16,2048]{1,0:T(8,128)S(1)} collective-permute-done((f32[16,2048]{1,0:T(8,128)S(1)}, f32[16,2048]{1,0:T(8,128)S(1)}, u32[]{:S(2)}, u32[]{:S(2)}) %collective-permute-start.7) | collective-permute-done | bytes 131104 | tf_op jit(solution)/shard_map/ppermute | solution.py:157
  51.6 0.5 collective-permute-done.6.refs_0_.refs_3_
  52.1 0.3 shard_map.91.refs_0_
  52.4 0.0 collective-permute-start.9
  52.5 1.2 %collective-permute-done.9.refs_1_ = f32[64,128]{1,0:T(8,128)S(1)} collective-permute-done((f32[64,128]{1,0:T(8,128)S(1)}, f32[64,128]{1,0:T(8,128)S(1)}, u32[]{:S(2)}, u32[]{:S(2)}) %collective-permute-start.9) | collective-permute-done | bytes 32800 | tf_op jit(solution)/shard_map/ppermute | solution.py:189
  53.7 1.3 %shard_map.92 = (f32[16,8192]{1,0:T(8,128)}, f32[16,8192]{1,0:T(8,128)}, f32[16,8192]{1,0:T(8,128)}) custom-call(f32[64,128]{1,0:T(8,128)S(1)} %shard_map.91.refs_0_, f32[64,128]{1,0:T(8,128)S(1)} %collective-permute-done.9.refs_1_, f32[16,2048]{1,0:T(8,128)S(1)} %collective-permute-done.8.refs_0_.refs_2_, ...), custom_call_target="tpu_custom_call" | custom-call | tf_op jit(solution)/shard_map/pallas_call | solution.py:243
  (8 shorter events, 0.1 us)
Async XLA Ops:
  15.4 1.4 %collective-permute-start = (bf16[16,2048]{1,0:T(8,128)(2,1)S(1)}, bf16[16,2048]{1,0:T(8,128)(2,1)S(1)}, u32[]{:S(2)}, u32[]{:S(2)}) collective-permute-start(bf16[16,2048]{1,0:T(8,128)(2,1)S(1)} %get-tuple-element.8.refs_0_), channel_id=1, source_target_pairs={{0,1},{1,0},{2,3},{3,2},{4,5},{5,4},{6,7},{7,6},{8,9},{9,8},{10,11... | collective-permute-start | bytes 196616 | tf_op jit(solution)/shard_map/ppermute | solution.py:189
  19.1 7.4 %collective-permute-start.1 = (f32[16,2048]{1,0:T(8,128)S(1)}, f32[16,2048]{1,0:T(8,128)S(1)}, u32[]{:S(2)}, u32[]{:S(2)}) collective-permute-start(f32[16,2048]{1,0:T(8,128)S(1)} %shard_map.87), channel_id=1, source_target_pairs={{0,2},{1,5},{2,0},{3,7},{4,6},{5,1},{6,4},{7,3},{8,10},{9,13},{10,... | collective-permute-start | bytes 393224 | tf_op jit(solution)/shard_map/ppermute | solution.py:157
  24.2 6.7 %collective-permute-start.3 = (f32[16,2048]{1,0:T(8,128)S(1)}, f32[16,2048]{1,0:T(8,128)S(1)}, u32[]{:S(2)}, u32[]{:S(2)}) collective-permute-start(f32[16,2048]{1,0:T(8,128)S(1)} %shard_map.89), channel_id=1, source_target_pairs={{0,2},{1,5},{2,0},{3,7},{4,6},{5,1},{6,4},{7,3},{8,10},{9,13},{10,... | collective-permute-start | bytes 393224 | tf_op jit(solution)/shard_map/ppermute | solution.py:157
  24.2 25.6 %copy-start = (f32[16,8192]{1,0:T(8,128)S(1)}, f32[16,8192]{1,0:T(8,128)}, u32[]{:S(2)}) copy-start(f32[16,8192]{1,0:T(8,128)} %refs_6_.1) | copy-start | bytes 1572868
  24.2 25.6 %copy-start.1 = (f32[16,8192]{1,0:T(8,128)S(1)}, f32[16,8192]{1,0:T(8,128)}, u32[]{:S(2)}) copy-start(f32[16,8192]{1,0:T(8,128)} %refs_7_.1) | copy-start | bytes 1572868
  24.2 25.6 %copy-start.3 = (f32[8192]{0:T(1024)S(1)}, f32[8192]{0:T(1024)}, u32[]{:S(2)}) copy-start(f32[8192]{0:T(1024)} %param.11) | copy-start | bytes 98308
  26.5 27.2 %copy-start.2 = (f32[16,8192]{1,0:T(8,128)S(1)}, f32[16,8192]{1,0:T(8,128)}, u32[]{:S(2)}) copy-start(f32[16,8192]{1,0:T(8,128)} %refs_9_.1) | copy-start | bytes 1572868
  26.6 5.0 %collective-permute-start.2 = (f32[16,2048]{1,0:T(8,128)S(1)}, f32[16,2048]{1,0:T(8,128)S(1)}, u32[]{:S(2)}, u32[]{:S(2)}) collective-permute-start(f32[16,2048]{1,0:T(8,128)S(1)} %add.15), channel_id=1, source_target_pairs={{0,4},{1,3},{2,6},{3,1},{4,0},{5,7},{6,2},{7,5},{8,12},{9,11},{10,... | collective-permute-start | bytes 393224 | tf_op jit(solution)/shard_map/ppermute | solution.py:157
  31.6 5.1 %collective-permute-start.4 = (f32[16,2048]{1,0:T(8,128)S(1)}, f32[16,2048]{1,0:T(8,128)S(1)}, u32[]{:S(2)}, u32[]{:S(2)}) collective-permute-start(f32[16,2048]{1,0:T(8,128)S(1)} %add_add_fusion), channel_id=1, source_target_pairs={{0,8},{1,9},{2,10},{3,11},{4,12},{5,13},{6,14},{7,15},{8,0},{9,1},... | collective-permute-start | bytes 393224 | tf_op jit(solution)/shard_map/ppermute | solution.py:157
  36.7 7.2 %collective-permute-start.5 = (f32[16,2048]{1,0:T(8,128)S(1)}, f32[16,2048]{1,0:T(8,128)S(1)}, u32[]{:S(2)}, u32[]{:S(2)}) collective-permute-start(f32[16,2048]{1,0:T(8,128)S(1)} %add.18), channel_id=1, source_target_pairs={{0,24},{1,25},{2,26},{3,27},{4,28},{5,29},{6,30},{7,31},{8,16},{9,... | collective-permute-start | bytes 393224 | tf_op jit(solution)/shard_map/ppermute | solution.py:157
  43.9 5.9 %collective-permute-start.8 = (f32[16,2048]{1,0:T(8,128)S(1)}, f32[16,2048]{1,0:T(8,128)S(1)}, u32[]{:S(2)}, u32[]{:S(2)}) collective-permute-start(f32[16,2048]{1,0:T(8,128)S(1)} %add.19.refs_1_.refs_5_), channel_id=1, source_target_pairs={{0,6},{1,7},{2,4},{3,5},{4,2},{5,3},{6,0},{7,1},{8,14},{9,15},{10,... | collective-permute-start | bytes 393224 | tf_op jit(solution)/shard_map/ppermute | solution.py:157
  46.7 5.0 %collective-permute-start.7 = (f32[16,2048]{1,0:T(8,128)S(1)}, f32[16,2048]{1,0:T(8,128)S(1)}, u32[]{:S(2)}, u32[]{:S(2)}) collective-permute-start(f32[16,2048]{1,0:T(8,128)S(1)} %add.19.refs_1_.refs_5_), channel_id=1, source_target_pairs={{0,4},{1,3},{2,6},{3,1},{4,0},{5,7},{6,2},{7,5},{8,12},{9,11},{10,... | collective-permute-start | bytes 393224 | tf_op jit(solution)/shard_map/ppermute | solution.py:157
  47.2 5.0 %collective-permute-start.6 = (f32[16,2048]{1,0:T(8,128)S(1)}, f32[16,2048]{1,0:T(8,128)S(1)}, u32[]{:S(2)}, u32[]{:S(2)}) collective-permute-start(f32[16,2048]{1,0:T(8,128)S(1)} %add.19.refs_1_.refs_5_), channel_id=1, source_target_pairs={{0,2},{1,5},{2,0},{3,7},{4,6},{5,1},{6,4},{7,3},{8,10},{9,13},{10,... | collective-permute-start | bytes 393224 | tf_op jit(solution)/shard_map/ppermute | solution.py:157
  52.4 1.2 %collective-permute-start.9 = (f32[64,128]{1,0:T(8,128)S(1)}, f32[64,128]{1,0:T(8,128)S(1)}, u32[]{:S(2)}, u32[]{:S(2)}) collective-permute-start(f32[64,128]{1,0:T(8,128)S(1)} %shard_map.91.refs_0_), channel_id=1, source_target_pairs={{0,1},{1,0},{2,3},{3,2},{4,5},{5,4},{6,7},{7,6},{8,9},{9,8},{10,11... | collective-permute-start | bytes 98312 | tf_op jit(solution)/shard_map/ppermute | solution.py:189

commit v7 on v6

--- a/solution.py
+++ b/solution.py
@@ -13,6 +13,7 @@
 BF16 = jnp.bfloat16
 RATE = 0.25 * math.log2(math.e)
 DEPTH = 128
+TURNED = (0, 2)
 VMEM = pl.BlockSpec(memory_space=pltpu.VMEM)
 
 
@@ -71,22 +72,25 @@
     db_ref[...] = dir_ref[...].astype(BF16)
     sum_ref[...] = jnp.zeros(sum_ref.shape, F32)
     steps = ctr // 4 // width
-    for i, out in zip(chunk_ids(), kern):
+    for i, chunk, out in zip(range(4), chunk_ids(), kern):
 
         @pl.loop(0, steps)
         def _(j):
-            col = tile_of(i * steps + j, width)
+            col, place = tile_of(chunk * steps + j, width), tile_of(j, width)
             cen = ca_ref[:, col].T
             for p in range(num // across):
                 row = slice(p * across, (p + 1) * across)
                 tile = jnp.exp2(jnp.dot(cen, xa_ref[:, row], preferred_element_type=F32)).astype(BF16)
-                out[tile_of(j, width), row] = tile
+                if i in TURNED:
+                    out[row, place] = tile.T
+                else:
+                    out[place, row] = tile
                 sum_ref[:, row] += jnp.dot(db_ref[:, col], tile, preferred_element_type=F32)
 
     fit_ref[...] = sum_ref[...].astype(BF16)
 
 
-def col_kernel(width, *refs):
+def col_kernel(width, turned, *refs):
     fits, kern, out = refs[:-2], refs[-2], refs[-1]
     fitted = fits[0][...].astype(F32)
     for ref in fits[1:]:
@@ -95,8 +99,10 @@
 
     @pl.loop(0, out.shape[1] // width)
     def _(j):
-        rows = tile_of(j, width)
-        out[:, rows] = lax.dot_general(fitted, kern[rows, :], (((1,), (1,)), ((), ())), preferred_element_type=F32)
+        place = tile_of(j, width)
+        tile = kern[:, place] if turned else kern[place, :]
+        dims = (((1,), (0 if turned else 1,)), ((), ()))
+        out[:, place] = lax.dot_general(fitted, tile, dims, preferred_element_type=F32)
 
 
 def width_of(size, most):
@@ -109,9 +115,10 @@
 def fit_parts(points, centres, direction):
     num, ctr = points.shape[1], centres.shape[1]
     targets = direction.shape[0]
+    shapes = [(num, ctr // 4) if i in TURNED else (ctr // 4, num) for i in range(4)] + [(targets, num)]
     out = pl.pallas_call(
         functools.partial(fit_kernel, width_of(ctr // 4, 2048), width_of(num, 512)),
-        out_shape=[jax.ShapeDtypeStruct((ctr // 4, num), BF16)] * 4 + [jax.ShapeDtypeStruct((targets, num), BF16)],
+        out_shape=[jax.ShapeDtypeStruct(shape, BF16) for shape in shapes],
         in_specs=[pl.BlockSpec(memory_space=pl.ANY)] * 3,
         out_specs=[VMEM] * 5,
         scratch_shapes=[
@@ -129,16 +136,16 @@
     return out[:4], out[4]
 
 
-def col_sums(fits, kern):
+def col_sums(fits, kern, i):
     targets = fits[0].shape[0]
-    size = kern.shape[0]
+    size = kern[i].shape[1 if i in TURNED else 0]
     return pl.pallas_call(
-        functools.partial(col_kernel, width_of(size, 2048)),
+        functools.partial(col_kernel, width_of(size, 2048), i in TURNED),
         out_shape=jax.ShapeDtypeStruct((targets, size), F32),
         in_specs=[VMEM] * (len(fits) + 1),
         out_specs=VMEM,
         compiler_params=pltpu.CompilerParams(vmem_limit_bytes=4 * MIB),
-    )(*fits, kern)
+    )(*fits, kern[i])
 
 
 def radices(size):
@@ -254,13 +261,13 @@
     num, full = points.shape[1], direction.shape
     kern, part = fit_parts(points, centres, direction)
     fits = over_ctr(part)
-    give_a = col_sums(fits, kern[0])
+    give_a = col_sums(fits, kern, 0)
     got_a = send_pts(give_a, along(0))
-    keep_a = col_sums(fits, kern[2])
-    give_b = col_sums(fits, kern[1])
+    keep_a = col_sums(fits, kern, 2)
+    give_b = col_sums(fits, kern, 1)
     got_b = send_pts(give_b, along(0))
     moved = send_pts(keep_a + got_a, along(1))
-    keep_b = col_sums(fits, kern[3])
+    keep_b = col_sums(fits, kern, 3)
     mine = sum_over_rest(moved + (keep_b + got_b))
     near = send_pts(mine, along(1))
     far = send_pts(mine, along(0))

time: 55.1 us -> 54.2 us (0.984)
  Pallas kernels: 25.7 us -> 24.7 us
    pallas_call x4, Pallas kernels: 9.05 us -> 6.9 us  [col_sums(): pl.pallas_call(functools.partial(col_kernel, width_of(size, 2048), i in T...]
    pallas_call x1, Pallas kernels: 14.8 us -> 16 us  [fit_parts(): pl.pallas_call(functools.partial(fit_kernel, width_of(ctr // 4, 2048), wi...]
  transfers between devices with their start and end apart: 10 -> 10, of which waited for: 8 -> 9; matrix products, arithmetic and copies ran while one was open for 0% -> 0% of each run, Pallas kernels for 13% -> 11%
where the time goes in v7:
time: 54.2 us; the launch traced here: 54 us
  Pallas kernels  24.7 us (46%)
  starting transfers between devices  14.9 us (27%)
  waiting for transfers between devices  13.6 us (25%)
  between operations  0.7 us (1%)
    pallas_call x1, Pallas kernels, fit_parts(): pl.pallas_call(functools.partial(fit_kernel, width_of(ctr // 4, 2048), wi...  16 us
    ppermute x8, starting transfers between devices, send_pts(): return lax.ppermute(value, ('pts', 'ctr'), pairs)  14.4 us
    ppermute x8, waiting for transfers between devices, send_pts(): return lax.ppermute(value, ('pts', 'ctr'), pairs)  11.5 us
    pallas_call x4, Pallas kernels, col_sums(): pl.pallas_call(functools.partial(col_kernel, width_of(size, 2048), i in T...  6.9 us
    ppermute x2, waiting for transfers between devices, over_ctr(): lax.ppermute(value, 'ctr', [(c, (c + k) % num_ctr) for c in range(num_ctr)])  2.1 us
    pallas_call x1, Pallas kernels, step_of(): pl.pallas_call(functools.partial(step_kernel, scale, len(sums)), out_shap...  1.32 us
  transfers between devices with their start and end apart: 10, of which 9 were waited for; matrix products, arithmetic and copies ran while one was open for 0% of the time, Pallas kernels for 11%

profile of v7, /device:TPU:0, one launch (start us, length us, event | category | flops | bytes accessed | tf_op | source)
XLA Modules:
  0.0 54.0 jit_solution(16467228383167638964)
XLA Ops:
  0.6 16.0 %shard_map.85 = (bf16[2048,2048]{1,0:T(8,128)(2,1)S(1)}, bf16[2048,2048]{1,0:T(8,128)(2,1)S(1)}, bf16[2048,2048]{1,0:T(8,128)(2,1)S(1)}, bf16[2048,2048]{1,0:T(8,128)(2,1)S(1)}, bf16[16,2048]{1,0:T(8,128)(2,1)S(1)}) custom-call(bf16[32,2048]{1,0:T(8,128)(2,1)} %pts_hbm.1, bf16[32,8192]{1,0:T(8,128)(2,1)} %cen_hbm.1, f32[16,8192]{1,0:T(8,128)} %refs_6_.1), custom_call_target="tpu_custom_call" | custom-call | tf_op jit(solution)/shard_map/pallas_call | solution.py:119
  16.6 0.5 collective-permute-start
  17.1 0.9 %collective-permute-done.refs_1_ = bf16[16,2048]{1,0:T(8,128)(2,1)S(1)} collective-permute-done((bf16[16,2048]{1,0:T(8,128)(2,1)S(1)}, bf16[16,2048]{1,0:T(8,128)(2,1)S(1)}, u32[]{:S(2)}, u32[]{:S(2)}) %collective-permute-start) | collective-permute-done | bytes 65568 | tf_op jit(solution)/shard_map/ppermute | solution.py:196
  18.0 1.2 %shard_map.87 = f32[16,2048]{1,0:T(8,128)S(1)} custom-call(bf16[16,2048]{1,0:T(8,128)(2,1)S(1)} %get-tuple-element.8.refs_0_, bf16[16,2048]{1,0:T(8,128)(2,1)S(1)} %collective-permute-done.refs_1_, bf16[2048,2048]{1,0:T(8,128)(2,1)S(1)} %get-tuple-element.10.refs_2_), custom_call_target="tpu_custom_call" | custom-call | tf_op jit(solution)/shard_map/pallas_call | solution.py:142
  19.2 2.9 %collective-permute-start.1 = (f32[16,2048]{1,0:T(8,128)S(1)}, f32[16,2048]{1,0:T(8,128)S(1)}, u32[]{:S(2)}, u32[]{:S(2)}) collective-permute-start(f32[16,2048]{1,0:T(8,128)S(1)} %shard_map.87), channel_id=1, source_target_pairs={{0,2},{1,5},{2,0},{3,7},{4,6},{5,1},{6,4},{7,3},{8,10},{9,13},{10,... | collective-permute-start | bytes 393224 | tf_op jit(solution)/shard_map/ppermute | solution.py:164
  22.1 2.3 %shard_map.89 = f32[16,2048]{1,0:T(8,128)S(1)} custom-call(bf16[16,2048]{1,0:T(8,128)(2,1)S(1)} %get-tuple-element.8.refs_0_, bf16[16,2048]{1,0:T(8,128)(2,1)S(1)} %collective-permute-done.refs_1_, bf16[2048,2048]{1,0:T(8,128)(2,1)S(1)} %get-tuple-element.12.refs_2_), custom_call_target="tpu_custom_call" | custom-call | tf_op jit(solution)/shard_map/pallas_call | solution.py:142
  24.3 0.0 collective-permute-start.3
  24.4 0.0 copy-start.3
  24.4 1.2 %shard_map.86 = f32[16,2048]{1,0:T(8,128)S(1)} custom-call(bf16[16,2048]{1,0:T(8,128)(2,1)S(1)} %get-tuple-element.8.refs_0_, bf16[16,2048]{1,0:T(8,128)(2,1)S(1)} %collective-permute-done.refs_1_, bf16[2048,2048]{1,0:T(8,128)(2,1)S(1)} %get-tuple-element.9.refs_2_), custom_call_target="tpu_custom_call" | custom-call | tf_op jit(solution)/shard_map/pallas_call | solution.py:142
  25.6 0.0 collective-permute-done.1
  25.6 2.1 %collective-permute-start.2 = (f32[16,2048]{1,0:T(8,128)S(1)}, f32[16,2048]{1,0:T(8,128)S(1)}, u32[]{:S(2)}, u32[]{:S(2)}) collective-permute-start(f32[16,2048]{1,0:T(8,128)S(1)} %add.15), channel_id=1, source_target_pairs={{0,4},{1,3},{2,6},{3,1},{4,0},{5,7},{6,2},{7,5},{8,12},{9,11},{10,... | collective-permute-start | bytes 393224 | tf_op jit(solution)/shard_map/ppermute | solution.py:164
  27.7 2.3 %shard_map.88 = f32[16,2048]{1,0:T(8,128)S(1)} custom-call(bf16[16,2048]{1,0:T(8,128)(2,1)S(1)} %get-tuple-element.8.refs_0_, bf16[16,2048]{1,0:T(8,128)(2,1)S(1)} %collective-permute-done.refs_1_, bf16[2048,2048]{1,0:T(8,128)(2,1)S(1)} %get-tuple-element.11.refs_2_), custom_call_target="tpu_custom_call" | custom-call | tf_op jit(solution)/shard_map/pallas_call | solution.py:142
  30.0 0.5 collective-permute-done.3
  30.5 0.2 collective-permute-done.2
  30.7 2.1 %collective-permute-start.4 = (f32[16,2048]{1,0:T(8,128)S(1)}, f32[16,2048]{1,0:T(8,128)S(1)}, u32[]{:S(2)}, u32[]{:S(2)}) collective-permute-start(f32[16,2048]{1,0:T(8,128)S(1)} %add_add_fusion), channel_id=1, source_target_pairs={{0,8},{1,9},{2,10},{3,11},{4,12},{5,13},{6,14},{7,15},{8,0},{9,1},... | collective-permute-start | bytes 393224 | tf_op jit(solution)/shard_map/ppermute | solution.py:164
  32.8 3.4 %collective-permute-done.4 = f32[16,2048]{1,0:T(8,128)S(1)} collective-permute-done((f32[16,2048]{1,0:T(8,128)S(1)}, f32[16,2048]{1,0:T(8,128)S(1)}, u32[]{:S(2)}, u32[]{:S(2)}) %collective-permute-start.4) | collective-permute-done | bytes 131104 | tf_op jit(solution)/shard_map/ppermute | solution.py:164
  36.3 3.7 %collective-permute-start.5 = (f32[16,2048]{1,0:T(8,128)S(1)}, f32[16,2048]{1,0:T(8,128)S(1)}, u32[]{:S(2)}, u32[]{:S(2)}) collective-permute-start(f32[16,2048]{1,0:T(8,128)S(1)} %add.18), channel_id=1, source_target_pairs={{0,24},{1,25},{2,26},{3,27},{4,28},{5,29},{6,30},{7,31},{8,16},{9,... | collective-permute-start | bytes 393224 | tf_op jit(solution)/shard_map/ppermute | solution.py:164
  40.0 3.2 %collective-permute-done.5 = f32[16,2048]{1,0:T(8,128)S(1)} collective-permute-done((f32[16,2048]{1,0:T(8,128)S(1)}, f32[16,2048]{1,0:T(8,128)S(1)}, u32[]{:S(2)}, u32[]{:S(2)}) %collective-permute-start.5) | collective-permute-done | bytes 131104 | tf_op jit(solution)/shard_map/ppermute | solution.py:164
  43.2 2.5 %collective-permute-start.8 = (f32[16,2048]{1,0:T(8,128)S(1)}, f32[16,2048]{1,0:T(8,128)S(1)}, u32[]{:S(2)}, u32[]{:S(2)}) collective-permute-start(f32[16,2048]{1,0:T(8,128)S(1)} %add.19.refs_1_.refs_5_), channel_id=1, source_target_pairs={{0,6},{1,7},{2,4},{3,5},{4,2},{5,3},{6,0},{7,1},{8,14},{9,15},{10,... | collective-permute-start | bytes 393224 | tf_op jit(solution)/shard_map/ppermute | solution.py:164
  45.7 0.5 collective-permute-start.7
  46.2 0.5 %collective-permute-start.6 = (f32[16,2048]{1,0:T(8,128)S(1)}, f32[16,2048]{1,0:T(8,128)S(1)}, u32[]{:S(2)}, u32[]{:S(2)}) collective-permute-start(f32[16,2048]{1,0:T(8,128)S(1)} %add.19.refs_1_.refs_5_), channel_id=1, source_target_pairs={{0,2},{1,5},{2,0},{3,7},{4,6},{5,1},{6,4},{7,3},{8,10},{9,13},{10,... | collective-permute-start | bytes 393224 | tf_op jit(solution)/shard_map/ppermute | solution.py:164
  46.7 2.4 %collective-permute-done.8.refs_0_.refs_2_ = f32[16,2048]{1,0:T(8,128)S(1)} collective-permute-done((f32[16,2048]{1,0:T(8,128)S(1)}, f32[16,2048]{1,0:T(8,128)S(1)}, u32[]{:S(2)}, u32[]{:S(2)}) %collective-permute-start.8) | collective-permute-done | bytes 131104 | tf_op jit(solution)/shard_map/ppermute | solution.py:164
  49.1 0.0 copy-done
  49.1 0.0 copy-done.1
  49.1 0.0 copy-done.3
  49.1 0.2 shard_map.90.refs_2_
  49.4 1.3 %collective-permute-done.7.refs_1_.refs_4_ = f32[16,2048]{1,0:T(8,128)S(1)} collective-permute-done((f32[16,2048]{1,0:T(8,128)S(1)}, f32[16,2048]{1,0:T(8,128)S(1)}, u32[]{:S(2)}, u32[]{:S(2)}) %collective-permute-start.7) | collective-permute-done | bytes 131104 | tf_op jit(solution)/shard_map/ppermute | solution.py:164
  50.7 0.5 collective-permute-done.6.refs_0_.refs_3_
  51.2 0.3 shard_map.91.refs_0_
  51.5 0.0 collective-permute-start.9
  51.5 1.2 %collective-permute-done.9.refs_1_ = f32[64,128]{1,0:T(8,128)S(1)} collective-permute-done((f32[64,128]{1,0:T(8,128)S(1)}, f32[64,128]{1,0:T(8,128)S(1)}, u32[]{:S(2)}, u32[]{:S(2)}) %collective-permute-start.9) | collective-permute-done | bytes 32800 | tf_op jit(solution)/shard_map/ppermute | solution.py:196
  52.7 1.3 %shard_map.92 = (f32[16,8192]{1,0:T(8,128)}, f32[16,8192]{1,0:T(8,128)}, f32[16,8192]{1,0:T(8,128)}) custom-call(f32[64,128]{1,0:T(8,128)S(1)} %shard_map.91.refs_0_, f32[64,128]{1,0:T(8,128)S(1)} %collective-permute-done.9.refs_1_, f32[16,2048]{1,0:T(8,128)S(1)} %collective-permute-done.8.refs_0_.refs_2_, ...), custom_call_target="tpu_custom_call" | custom-call | tf_op jit(solution)/shard_map/pallas_call | solution.py:250
  (8 shorter events, 0.1 us)
Async XLA Ops:
  16.6 1.4 %collective-permute-start = (bf16[16,2048]{1,0:T(8,128)(2,1)S(1)}, bf16[16,2048]{1,0:T(8,128)(2,1)S(1)}, u32[]{:S(2)}, u32[]{:S(2)}) collective-permute-start(bf16[16,2048]{1,0:T(8,128)(2,1)S(1)} %get-tuple-element.8.refs_0_), channel_id=1, source_target_pairs={{0,1},{1,0},{2,3},{3,2},{4,5},{5,4},{6,7},{7,6},{8,9},{9,8},{10,11... | collective-permute-start | bytes 196616 | tf_op jit(solution)/shard_map/ppermute | solution.py:196
  19.2 6.4 %collective-permute-start.1 = (f32[16,2048]{1,0:T(8,128)S(1)}, f32[16,2048]{1,0:T(8,128)S(1)}, u32[]{:S(2)}, u32[]{:S(2)}) collective-permute-start(f32[16,2048]{1,0:T(8,128)S(1)} %shard_map.87), channel_id=1, source_target_pairs={{0,2},{1,5},{2,0},{3,7},{4,6},{5,1},{6,4},{7,3},{8,10},{9,13},{10,... | collective-permute-start | bytes 393224 | tf_op jit(solution)/shard_map/ppermute | solution.py:164
  24.3 6.1 %collective-permute-start.3 = (f32[16,2048]{1,0:T(8,128)S(1)}, f32[16,2048]{1,0:T(8,128)S(1)}, u32[]{:S(2)}, u32[]{:S(2)}) collective-permute-start(f32[16,2048]{1,0:T(8,128)S(1)} %shard_map.89), channel_id=1, source_target_pairs={{0,2},{1,5},{2,0},{3,7},{4,6},{5,1},{6,4},{7,3},{8,10},{9,13},{10,... | collective-permute-start | bytes 393224 | tf_op jit(solution)/shard_map/ppermute | solution.py:164
  24.4 24.8 %copy-start = (f32[16,8192]{1,0:T(8,128)S(1)}, f32[16,8192]{1,0:T(8,128)}, u32[]{:S(2)}) copy-start(f32[16,8192]{1,0:T(8,128)} %refs_6_.1) | copy-start | bytes 1572868
  24.4 24.8 %copy-start.1 = (f32[16,8192]{1,0:T(8,128)S(1)}, f32[16,8192]{1,0:T(8,128)}, u32[]{:S(2)}) copy-start(f32[16,8192]{1,0:T(8,128)} %refs_7_.1) | copy-start | bytes 1572868
  24.4 24.8 %copy-start.3 = (f32[8192]{0:T(1024)S(1)}, f32[8192]{0:T(1024)}, u32[]{:S(2)}) copy-start(f32[8192]{0:T(1024)} %param.11) | copy-start | bytes 98308
  25.6 27.2 %copy-start.2 = (f32[16,8192]{1,0:T(8,128)S(1)}, f32[16,8192]{1,0:T(8,128)}, u32[]{:S(2)}) copy-start(f32[16,8192]{1,0:T(8,128)} %refs_9_.1) | copy-start | bytes 1572868
  25.6 5.0 %collective-permute-start.2 = (f32[16,2048]{1,0:T(8,128)S(1)}, f32[16,2048]{1,0:T(8,128)S(1)}, u32[]{:S(2)}, u32[]{:S(2)}) collective-permute-start(f32[16,2048]{1,0:T(8,128)S(1)} %add.15), channel_id=1, source_target_pairs={{0,4},{1,3},{2,6},{3,1},{4,0},{5,7},{6,2},{7,5},{8,12},{9,11},{10,... | collective-permute-start | bytes 393224 | tf_op jit(solution)/shard_map/ppermute | solution.py:164
  30.7 5.6 %collective-permute-start.4 = (f32[16,2048]{1,0:T(8,128)S(1)}, f32[16,2048]{1,0:T(8,128)S(1)}, u32[]{:S(2)}, u32[]{:S(2)}) collective-permute-start(f32[16,2048]{1,0:T(8,128)S(1)} %add_add_fusion), channel_id=1, source_target_pairs={{0,8},{1,9},{2,10},{3,11},{4,12},{5,13},{6,14},{7,15},{8,0},{9,1},... | collective-permute-start | bytes 393224 | tf_op jit(solution)/shard_map/ppermute | solution.py:164
  36.3 6.9 %collective-permute-start.5 = (f32[16,2048]{1,0:T(8,128)S(1)}, f32[16,2048]{1,0:T(8,128)S(1)}, u32[]{:S(2)}, u32[]{:S(2)}) collective-permute-start(f32[16,2048]{1,0:T(8,128)S(1)} %add.18), channel_id=1, source_target_pairs={{0,24},{1,25},{2,26},{3,27},{4,28},{5,29},{6,30},{7,31},{8,16},{9,... | collective-permute-start | bytes 393224 | tf_op jit(solution)/shard_map/ppermute | solution.py:164
  43.2 5.9 %collective-permute-start.8 = (f32[16,2048]{1,0:T(8,128)S(1)}, f32[16,2048]{1,0:T(8,128)S(1)}, u32[]{:S(2)}, u32[]{:S(2)}) collective-permute-start(f32[16,2048]{1,0:T(8,128)S(1)} %add.19.refs_1_.refs_5_), channel_id=1, source_target_pairs={{0,6},{1,7},{2,4},{3,5},{4,2},{5,3},{6,0},{7,1},{8,14},{9,15},{10,... | collective-permute-start | bytes 393224 | tf_op jit(solution)/shard_map/ppermute | solution.py:164
  45.7 5.0 %collective-permute-start.7 = (f32[16,2048]{1,0:T(8,128)S(1)}, f32[16,2048]{1,0:T(8,128)S(1)}, u32[]{:S(2)}, u32[]{:S(2)}) collective-permute-start(f32[16,2048]{1,0:T(8,128)S(1)} %add.19.refs_1_.refs_5_), channel_id=1, source_target_pairs={{0,4},{1,3},{2,6},{3,1},{4,0},{5,7},{6,2},{7,5},{8,12},{9,11},{10,... | collective-permute-start | bytes 393224 | tf_op jit(solution)/shard_map/ppermute | solution.py:164
  46.2 5.0 %collective-permute-start.6 = (f32[16,2048]{1,0:T(8,128)S(1)}, f32[16,2048]{1,0:T(8,128)S(1)}, u32[]{:S(2)}, u32[]{:S(2)}) collective-permute-start(f32[16,2048]{1,0:T(8,128)S(1)} %add.19.refs_1_.refs_5_), channel_id=1, source_target_pairs={{0,2},{1,5},{2,0},{3,7},{4,6},{5,1},{6,4},{7,3},{8,10},{9,13},{10,... | collective-permute-start | bytes 393224 | tf_op jit(solution)/shard_map/ppermute | solution.py:164
  51.5 1.2 %collective-permute-start.9 = (f32[64,128]{1,0:T(8,128)S(1)}, f32[64,128]{1,0:T(8,128)S(1)}, u32[]{:S(2)}, u32[]{:S(2)}) collective-permute-start(f32[64,128]{1,0:T(8,128)S(1)} %shard_map.91.refs_0_), channel_id=1, source_target_pairs={{0,1},{1,0},{2,3},{3,2},{4,5},{5,4},{6,7},{7,6},{8,9},{9,8},{10,11... | collective-permute-start | bytes 98312 | tf_op jit(solution)/shard_map/ppermute | solution.py:196

commit v8 on v7

--- a/solution.py
+++ b/solution.py
@@ -13,7 +13,7 @@
 BF16 = jnp.bfloat16
 RATE = 0.25 * math.log2(math.e)
 DEPTH = 128
-TURNED = (0, 2)
+TURNED = (0, 1, 2)
 VMEM = pl.BlockSpec(memory_space=pltpu.VMEM)
 
 
@@ -48,7 +48,8 @@
 
 
 def fit_kernel(width, across, pts_hbm, cen_hbm, dir_hbm, *refs):
-    kern, (fit_ref, pts_ref, cen_ref, dir_ref, xa_ref, ca_ref, db_ref, sum_ref, sems) = refs[:4], refs[4:]
+    kern, (fit_ref, pts_ref, cen_ref, dir_ref, xa_ref, sum_ref, sems) = refs[:4], refs[4:11]
+    ca_refs, db_refs = refs[11:15], refs[15:]
     pairs = ((pts_hbm, pts_ref), (cen_hbm, cen_ref), (dir_hbm, dir_ref))
     copies = [pltpu.make_async_copy(source, target, sems.at[i]) for i, (source, target) in enumerate(pairs)]
     for copy in copies:
@@ -61,32 +62,42 @@
     norm = split3(jnp.sum(pts * pts, axis=0, keepdims=True) * (-0.5 * RATE))
     terms.append(rows_of(list(norm) + [1.0, 1.0, 1.0], (DEPTH - 3 * feat, num)))
     xa_ref[...] = jnp.concatenate(terms, axis=0).astype(BF16)
+    size = ctr // 4
+    ids = chunk_ids()
+
+    def features(i):
+        col = tile_of(ids[i], size)
+        cen = cen_ref[:, col]
+        wide = cen.astype(F32)
+        norm = split3(jnp.sum(wide * wide, axis=0, keepdims=True) * (-0.5 * RATE))
+        block = rows_of([1.0, 1.0, 1.0] + list(norm), (DEPTH - 3 * feat, size)).astype(BF16)
+        ca_refs[i][...] = jnp.concatenate([cen, cen, cen, block], axis=0).T
+        db_refs[i][...] = dir_ref[:, col].astype(BF16)
+
     copies[1].wait()
-    cen = cen_ref[...]
-    for i in range(3):
-        ca_ref[i * feat : (i + 1) * feat, :] = cen
-    cen = cen.astype(F32)
-    norm = split3(jnp.sum(cen * cen, axis=0, keepdims=True) * (-0.5 * RATE))
-    ca_ref[3 * feat :, :] = rows_of([1.0, 1.0, 1.0] + list(norm), (DEPTH - 3 * feat, ctr)).astype(BF16)
     copies[2].wait()
-    db_ref[...] = dir_ref[...].astype(BF16)
+    features(0)
     sum_ref[...] = jnp.zeros(sum_ref.shape, F32)
-    steps = ctr // 4 // width
-    for i, chunk, out in zip(range(4), chunk_ids(), kern):
-
-        @pl.loop(0, steps)
-        def _(j):
-            col, place = tile_of(chunk * steps + j, width), tile_of(j, width)
-            cen = ca_ref[:, col].T
-            for p in range(num // across):
-                row = slice(p * across, (p + 1) * across)
-                tile = jnp.exp2(jnp.dot(cen, xa_ref[:, row], preferred_element_type=F32)).astype(BF16)
+    waiting = []
+    for i, out in enumerate(kern):
+        for p in range(num // across):
+            row = slice(p * across, (p + 1) * across)
+            for j in range(size // width):
+                place = slice(j * width, (j + 1) * width)
+                tile = jnp.exp2(jnp.dot(ca_refs[i][place, :], xa_ref[:, row], preferred_element_type=F32)).astype(BF16)
                 if i in TURNED:
                     out[row, place] = tile.T
                 else:
                     out[place, row] = tile
-                sum_ref[:, row] += jnp.dot(db_ref[:, col], tile, preferred_element_type=F32)
-
+                waiting.append((i, row, place, tile))
+                if len(waiting) > 2:
+                    k, old_row, old_place, old = waiting.pop(0)
+                    sum_ref[:, old_row] += jnp.dot(db_refs[k][:, old_place], old, preferred_element_type=F32)
+            if i < 3 and p == 0:
+                features(i + 1)
+
+    for k, old_row, old_place, old in waiting:
+        sum_ref[:, old_row] += jnp.dot(db_refs[k][:, old_place], old, preferred_element_type=F32)
     fit_ref[...] = sum_ref[...].astype(BF16)
 
 
@@ -117,7 +128,7 @@
     targets = direction.shape[0]
     shapes = [(num, ctr // 4) if i in TURNED else (ctr // 4, num) for i in range(4)] + [(targets, num)]
     out = pl.pallas_call(
-        functools.partial(fit_kernel, width_of(ctr // 4, 2048), width_of(num, 512)),
+        functools.partial(fit_kernel, width_of(ctr // 4, 2048), width_of(num, 256)),
         out_shape=[jax.ShapeDtypeStruct(shape, BF16) for shape in shapes],
         in_specs=[pl.BlockSpec(memory_space=pl.ANY)] * 3,
         out_specs=[VMEM] * 5,
@@ -126,11 +137,11 @@
             pltpu.VMEM(centres.shape, BF16),
             pltpu.VMEM(direction.shape, F32),
             pltpu.VMEM((DEPTH, num), BF16),
-            pltpu.VMEM((DEPTH, ctr), BF16),
-            pltpu.VMEM((targets, ctr), BF16),
             pltpu.VMEM((targets, num), F32),
             pltpu.SemaphoreType.DMA((3,)),
-        ],
+        ]
+        + [pltpu.VMEM((ctr // 4, DEPTH), BF16)] * 4
+        + [pltpu.VMEM((targets, ctr // 4), BF16)] * 4,
         compiler_params=pltpu.CompilerParams(vmem_limit_bytes=18 * MIB),
     )(*[pltpu.with_memory_space_constraint(value, pltpu.HBM) for value in (points, centres, direction)])
     return out[:4], out[4]

time: 54.2 us -> 53.3 us (0.983)
  Pallas kernels: 24.7 us -> 23.3 us
    pallas_call x4, Pallas kernels: 6.9 us -> 5.83 us  [col_sums(): pl.pallas_call(functools.partial(col_kernel, width_of(size, 2048), i in T...]
  transfers between devices with their start and end apart: 10 -> 10, of which waited for: 9 -> 9; matrix products, arithmetic and copies ran while one was open for 0% -> 0% of each run, Pallas kernels for 11% -> 9%
where the time goes in v8:
time: 53.3 us; the launch traced here: 53.2 us
  Pallas kernels  23.3 us (44%)
  starting transfers between devices  15.3 us (29%)
  waiting for transfers between devices  13.7 us (26%)
  between operations  0.69 us (1%)
    pallas_call x1, Pallas kernels, fit_parts(): pl.pallas_call(functools.partial(fit_kernel, width_of(ctr // 4, 2048), wi...  15.6 us
    ppermute x8, starting transfers between devices, send_pts(): return lax.ppermute(value, ('pts', 'ctr'), pairs)  14.8 us
    ppermute x8, waiting for transfers between devices, send_pts(): return lax.ppermute(value, ('pts', 'ctr'), pairs)  11.6 us
    pallas_call x4, Pallas kernels, col_sums(): pl.pallas_call(functools.partial(col_kernel, width_of(size, 2048), i in T...  5.83 us
    ppermute x2, waiting for transfers between devices, over_ctr(): lax.ppermute(value, 'ctr', [(c, (c + k) % num_ctr) for c in range(num_ctr)])  2.1 us
    pallas_call x1, Pallas kernels, step_of(): pl.pallas_call(functools.partial(step_kernel, scale, len(sums)), out_shap...  1.32 us
  transfers between devices with their start and end apart: 10, of which 9 were waited for; matrix products, arithmetic and copies ran while one was open for 0% of the time, Pallas kernels for 9%

profile of v8, /device:TPU:0, one launch (start us, length us, event | category | flops | bytes accessed | tf_op | source)
XLA Modules:
  0.0 53.2 jit_solution(9025360512299250972)
XLA Ops:
  0.6 15.6 %shard_map.85 = (bf16[2048,2048]{1,0:T(8,128)(2,1)S(1)}, bf16[2048,2048]{1,0:T(8,128)(2,1)S(1)}, bf16[2048,2048]{1,0:T(8,128)(2,1)S(1)}, bf16[2048,2048]{1,0:T(8,128)(2,1)S(1)}, bf16[16,2048]{1,0:T(8,128)(2,1)S(1)}) custom-call(bf16[32,2048]{1,0:T(8,128)(2,1)} %pts_hbm.1, bf16[32,8192]{1,0:T(8,128)(2,1)} %cen_hbm.1, f32[16,8192]{1,0:T(8,128)} %refs_6_.1), custom_call_target="tpu_custom_call" | custom-call | tf_op jit(solution)/shard_map/pallas_call | solution.py:130
  16.3 0.5 collective-permute-start
  16.8 0.9 %collective-permute-done.refs_1_ = bf16[16,2048]{1,0:T(8,128)(2,1)S(1)} collective-permute-done((bf16[16,2048]{1,0:T(8,128)(2,1)S(1)}, bf16[16,2048]{1,0:T(8,128)(2,1)S(1)}, u32[]{:S(2)}, u32[]{:S(2)}) %collective-permute-start) | collective-permute-done | bytes 65568 | tf_op jit(solution)/shard_map/ppermute | solution.py:207
  17.7 1.2 %shard_map.87 = f32[16,2048]{1,0:T(8,128)S(1)} custom-call(bf16[16,2048]{1,0:T(8,128)(2,1)S(1)} %get-tuple-element.8.refs_0_, bf16[16,2048]{1,0:T(8,128)(2,1)S(1)} %collective-permute-done.refs_1_, bf16[2048,2048]{1,0:T(8,128)(2,1)S(1)} %get-tuple-element.10.refs_2_), custom_call_target="tpu_custom_call" | custom-call | tf_op jit(solution)/shard_map/pallas_call | solution.py:153
  18.9 2.9 %collective-permute-start.1 = (f32[16,2048]{1,0:T(8,128)S(1)}, f32[16,2048]{1,0:T(8,128)S(1)}, u32[]{:S(2)}, u32[]{:S(2)}) collective-permute-start(f32[16,2048]{1,0:T(8,128)S(1)} %shard_map.87), channel_id=1, source_target_pairs={{0,2},{1,5},{2,0},{3,7},{4,6},{5,1},{6,4},{7,3},{8,10},{9,13},{10,... | collective-permute-start | bytes 393224 | tf_op jit(solution)/shard_map/ppermute | solution.py:175
  21.7 1.2 %shard_map.89 = f32[16,2048]{1,0:T(8,128)S(1)} custom-call(bf16[16,2048]{1,0:T(8,128)(2,1)S(1)} %get-tuple-element.8.refs_0_, bf16[16,2048]{1,0:T(8,128)(2,1)S(1)} %collective-permute-done.refs_1_, bf16[2048,2048]{1,0:T(8,128)(2,1)S(1)} %get-tuple-element.12.refs_2_), custom_call_target="tpu_custom_call" | custom-call | tf_op jit(solution)/shard_map/pallas_call | solution.py:153
  22.9 0.0 collective-permute-start.3
  23.0 0.0 copy-start.3
  23.0 1.2 %shard_map.86 = f32[16,2048]{1,0:T(8,128)S(1)} custom-call(bf16[16,2048]{1,0:T(8,128)(2,1)S(1)} %get-tuple-element.8.refs_0_, bf16[16,2048]{1,0:T(8,128)(2,1)S(1)} %collective-permute-done.refs_1_, bf16[2048,2048]{1,0:T(8,128)(2,1)S(1)} %get-tuple-element.9.refs_2_), custom_call_target="tpu_custom_call" | custom-call | tf_op jit(solution)/shard_map/pallas_call | solution.py:153
  24.2 0.5 collective-permute-done.1
  24.7 2.1 %collective-permute-start.2 = (f32[16,2048]{1,0:T(8,128)S(1)}, f32[16,2048]{1,0:T(8,128)S(1)}, u32[]{:S(2)}, u32[]{:S(2)}) collective-permute-start(f32[16,2048]{1,0:T(8,128)S(1)} %add.15), channel_id=1, source_target_pairs={{0,4},{1,3},{2,6},{3,1},{4,0},{5,7},{6,2},{7,5},{8,12},{9,11},{10,... | collective-permute-start | bytes 393224 | tf_op jit(solution)/shard_map/ppermute | solution.py:175
  26.8 2.3 %shard_map.88 = f32[16,2048]{1,0:T(8,128)S(1)} custom-call(bf16[16,2048]{1,0:T(8,128)(2,1)S(1)} %get-tuple-element.8.refs_0_, bf16[16,2048]{1,0:T(8,128)(2,1)S(1)} %collective-permute-done.refs_1_, bf16[2048,2048]{1,0:T(8,128)(2,1)S(1)} %get-tuple-element.11.refs_2_), custom_call_target="tpu_custom_call" | custom-call | tf_op jit(solution)/shard_map/pallas_call | solution.py:153
  29.1 0.0 collective-permute-done.3
  29.1 0.7 %collective-permute-done.2 = f32[16,2048]{1,0:T(8,128)S(1)} collective-permute-done((f32[16,2048]{1,0:T(8,128)S(1)}, f32[16,2048]{1,0:T(8,128)S(1)}, u32[]{:S(2)}, u32[]{:S(2)}) %collective-permute-start.2) | collective-permute-done | bytes 131104 | tf_op jit(solution)/shard_map/ppermute | solution.py:175
  29.8 2.1 %collective-permute-start.4 = (f32[16,2048]{1,0:T(8,128)S(1)}, f32[16,2048]{1,0:T(8,128)S(1)}, u32[]{:S(2)}, u32[]{:S(2)}) collective-permute-start(f32[16,2048]{1,0:T(8,128)S(1)} %add_add_fusion), channel_id=1, source_target_pairs={{0,8},{1,9},{2,10},{3,11},{4,12},{5,13},{6,14},{7,15},{8,0},{9,1},... | collective-permute-start | bytes 393224 | tf_op jit(solution)/shard_map/ppermute | solution.py:175
  31.9 3.0 %collective-permute-done.4 = f32[16,2048]{1,0:T(8,128)S(1)} collective-permute-done((f32[16,2048]{1,0:T(8,128)S(1)}, f32[16,2048]{1,0:T(8,128)S(1)}, u32[]{:S(2)}, u32[]{:S(2)}) %collective-permute-start.4) | collective-permute-done | bytes 131104 | tf_op jit(solution)/shard_map/ppermute | solution.py:175
  34.9 4.1 %collective-permute-start.5 = (f32[16,2048]{1,0:T(8,128)S(1)}, f32[16,2048]{1,0:T(8,128)S(1)}, u32[]{:S(2)}, u32[]{:S(2)}) collective-permute-start(f32[16,2048]{1,0:T(8,128)S(1)} %add.18), channel_id=1, source_target_pairs={{0,24},{1,25},{2,26},{3,27},{4,28},{5,29},{6,30},{7,31},{8,16},{9,... | collective-permute-start | bytes 393224 | tf_op jit(solution)/shard_map/ppermute | solution.py:175
  39.0 3.1 %collective-permute-done.5 = f32[16,2048]{1,0:T(8,128)S(1)} collective-permute-done((f32[16,2048]{1,0:T(8,128)S(1)}, f32[16,2048]{1,0:T(8,128)S(1)}, u32[]{:S(2)}, u32[]{:S(2)}) %collective-permute-start.5) | collective-permute-done | bytes 131104 | tf_op jit(solution)/shard_map/ppermute | solution.py:175
  42.1 2.7 %collective-permute-start.8 = (f32[16,2048]{1,0:T(8,128)S(1)}, f32[16,2048]{1,0:T(8,128)S(1)}, u32[]{:S(2)}, u32[]{:S(2)}) collective-permute-start(f32[16,2048]{1,0:T(8,128)S(1)} %add.19.refs_1_.refs_5_), channel_id=1, source_target_pairs={{0,6},{1,7},{2,4},{3,5},{4,2},{5,3},{6,0},{7,1},{8,14},{9,15},{10,... | collective-permute-start | bytes 393224 | tf_op jit(solution)/shard_map/ppermute | solution.py:175
  44.8 0.5 collective-permute-start.7
  45.3 0.3 collective-permute-start.6
  45.7 2.4 %collective-permute-done.8.refs_0_.refs_2_ = f32[16,2048]{1,0:T(8,128)S(1)} collective-permute-done((f32[16,2048]{1,0:T(8,128)S(1)}, f32[16,2048]{1,0:T(8,128)S(1)}, u32[]{:S(2)}, u32[]{:S(2)}) %collective-permute-start.8) | collective-permute-done | bytes 131104 | tf_op jit(solution)/shard_map/ppermute | solution.py:175
  48.0 0.0 copy-done
  48.0 0.0 copy-done.1
  48.0 0.0 copy-done.3
  48.0 0.2 shard_map.90.refs_2_
  48.3 1.5 %collective-permute-done.7.refs_1_.refs_4_ = f32[16,2048]{1,0:T(8,128)S(1)} collective-permute-done((f32[16,2048]{1,0:T(8,128)S(1)}, f32[16,2048]{1,0:T(8,128)S(1)}, u32[]{:S(2)}, u32[]{:S(2)}) %collective-permute-start.7) | collective-permute-done | bytes 131104 | tf_op jit(solution)/shard_map/ppermute | solution.py:175
  49.8 0.5 collective-permute-done.6.refs_0_.refs_3_
  50.3 0.3 shard_map.91.refs_0_
  50.6 0.0 collective-permute-start.9
  50.6 1.2 %collective-permute-done.9.refs_1_ = f32[64,128]{1,0:T(8,128)S(1)} collective-permute-done((f32[64,128]{1,0:T(8,128)S(1)}, f32[64,128]{1,0:T(8,128)S(1)}, u32[]{:S(2)}, u32[]{:S(2)}) %collective-permute-start.9) | collective-permute-done | bytes 32800 | tf_op jit(solution)/shard_map/ppermute | solution.py:207
  51.8 1.3 %shard_map.92 = (f32[16,8192]{1,0:T(8,128)}, f32[16,8192]{1,0:T(8,128)}, f32[16,8192]{1,0:T(8,128)}) custom-call(f32[64,128]{1,0:T(8,128)S(1)} %shard_map.91.refs_0_, f32[64,128]{1,0:T(8,128)S(1)} %collective-permute-done.9.refs_1_, f32[16,2048]{1,0:T(8,128)S(1)} %collective-permute-done.8.refs_0_.refs_2_, ...), custom_call_target="tpu_custom_call" | custom-call | tf_op jit(solution)/shard_map/pallas_call | solution.py:261
  (8 shorter events, 0.1 us)
Async XLA Ops:
  16.3 1.4 %collective-permute-start = (bf16[16,2048]{1,0:T(8,128)(2,1)S(1)}, bf16[16,2048]{1,0:T(8,128)(2,1)S(1)}, u32[]{:S(2)}, u32[]{:S(2)}) collective-permute-start(bf16[16,2048]{1,0:T(8,128)(2,1)S(1)} %get-tuple-element.8.refs_0_), channel_id=1, source_target_pairs={{0,1},{1,0},{2,3},{3,2},{4,5},{5,4},{6,7},{7,6},{8,9},{9,8},{10,11... | collective-permute-start | bytes 196616 | tf_op jit(solution)/shard_map/ppermute | solution.py:207
  18.9 5.8 %collective-permute-start.1 = (f32[16,2048]{1,0:T(8,128)S(1)}, f32[16,2048]{1,0:T(8,128)S(1)}, u32[]{:S(2)}, u32[]{:S(2)}) collective-permute-start(f32[16,2048]{1,0:T(8,128)S(1)} %shard_map.87), channel_id=1, source_target_pairs={{0,2},{1,5},{2,0},{3,7},{4,6},{5,1},{6,4},{7,3},{8,10},{9,13},{10,... | collective-permute-start | bytes 393224 | tf_op jit(solution)/shard_map/ppermute | solution.py:175
  22.9 6.2 %collective-permute-start.3 = (f32[16,2048]{1,0:T(8,128)S(1)}, f32[16,2048]{1,0:T(8,128)S(1)}, u32[]{:S(2)}, u32[]{:S(2)}) collective-permute-start(f32[16,2048]{1,0:T(8,128)S(1)} %shard_map.89), channel_id=1, source_target_pairs={{0,2},{1,5},{2,0},{3,7},{4,6},{5,1},{6,4},{7,3},{8,10},{9,13},{10,... | collective-permute-start | bytes 393224 | tf_op jit(solution)/shard_map/ppermute | solution.py:175
  22.9 25.1 %copy-start = (f32[16,8192]{1,0:T(8,128)S(1)}, f32[16,8192]{1,0:T(8,128)}, u32[]{:S(2)}) copy-start(f32[16,8192]{1,0:T(8,128)} %refs_6_.1) | copy-start | bytes 1572868
  23.0 25.1 %copy-start.1 = (f32[16,8192]{1,0:T(8,128)S(1)}, f32[16,8192]{1,0:T(8,128)}, u32[]{:S(2)}) copy-start(f32[16,8192]{1,0:T(8,128)} %refs_7_.1) | copy-start | bytes 1572868
  23.0 25.1 %copy-start.3 = (f32[8192]{0:T(1024)S(1)}, f32[8192]{0:T(1024)}, u32[]{:S(2)}) copy-start(f32[8192]{0:T(1024)} %param.11) | copy-start | bytes 98308
  24.2 27.7 %copy-start.2 = (f32[16,8192]{1,0:T(8,128)S(1)}, f32[16,8192]{1,0:T(8,128)}, u32[]{:S(2)}) copy-start(f32[16,8192]{1,0:T(8,128)} %refs_9_.1) | copy-start | bytes 1572868
  24.7 5.1 %collective-permute-start.2 = (f32[16,2048]{1,0:T(8,128)S(1)}, f32[16,2048]{1,0:T(8,128)S(1)}, u32[]{:S(2)}, u32[]{:S(2)}) collective-permute-start(f32[16,2048]{1,0:T(8,128)S(1)} %add.15), channel_id=1, source_target_pairs={{0,4},{1,3},{2,6},{3,1},{4,0},{5,7},{6,2},{7,5},{8,12},{9,11},{10,... | collective-permute-start | bytes 393224 | tf_op jit(solution)/shard_map/ppermute | solution.py:175
  29.8 5.1 %collective-permute-start.4 = (f32[16,2048]{1,0:T(8,128)S(1)}, f32[16,2048]{1,0:T(8,128)S(1)}, u32[]{:S(2)}, u32[]{:S(2)}) collective-permute-start(f32[16,2048]{1,0:T(8,128)S(1)} %add_add_fusion), channel_id=1, source_target_pairs={{0,8},{1,9},{2,10},{3,11},{4,12},{5,13},{6,14},{7,15},{8,0},{9,1},... | collective-permute-start | bytes 393224 | tf_op jit(solution)/shard_map/ppermute | solution.py:175
  34.9 7.1 %collective-permute-start.5 = (f32[16,2048]{1,0:T(8,128)S(1)}, f32[16,2048]{1,0:T(8,128)S(1)}, u32[]{:S(2)}, u32[]{:S(2)}) collective-permute-start(f32[16,2048]{1,0:T(8,128)S(1)} %add.18), channel_id=1, source_target_pairs={{0,24},{1,25},{2,26},{3,27},{4,28},{5,29},{6,30},{7,31},{8,16},{9,... | collective-permute-start | bytes 393224 | tf_op jit(solution)/shard_map/ppermute | solution.py:175
  42.1 5.9 %collective-permute-start.8 = (f32[16,2048]{1,0:T(8,128)S(1)}, f32[16,2048]{1,0:T(8,128)S(1)}, u32[]{:S(2)}, u32[]{:S(2)}) collective-permute-start(f32[16,2048]{1,0:T(8,128)S(1)} %add.19.refs_1_.refs_5_), channel_id=1, source_target_pairs={{0,6},{1,7},{2,4},{3,5},{4,2},{5,3},{6,0},{7,1},{8,14},{9,15},{10,... | collective-permute-start | bytes 393224 | tf_op jit(solution)/shard_map/ppermute | solution.py:175
  44.8 5.0 %collective-permute-start.7 = (f32[16,2048]{1,0:T(8,128)S(1)}, f32[16,2048]{1,0:T(8,128)S(1)}, u32[]{:S(2)}, u32[]{:S(2)}) collective-permute-start(f32[16,2048]{1,0:T(8,128)S(1)} %add.19.refs_1_.refs_5_), channel_id=1, source_target_pairs={{0,4},{1,3},{2,6},{3,1},{4,0},{5,7},{6,2},{7,5},{8,12},{9,11},{10,... | collective-permute-start | bytes 393224 | tf_op jit(solution)/shard_map/ppermute | solution.py:175
  45.3 5.0 %collective-permute-start.6 = (f32[16,2048]{1,0:T(8,128)S(1)}, f32[16,2048]{1,0:T(8,128)S(1)}, u32[]{:S(2)}, u32[]{:S(2)}) collective-permute-start(f32[16,2048]{1,0:T(8,128)S(1)} %add.19.refs_1_.refs_5_), channel_id=1, source_target_pairs={{0,2},{1,5},{2,0},{3,7},{4,6},{5,1},{6,4},{7,3},{8,10},{9,13},{10,... | collective-permute-start | bytes 393224 | tf_op jit(solution)/shard_map/ppermute | solution.py:175
  50.6 1.2 %collective-permute-start.9 = (f32[64,128]{1,0:T(8,128)S(1)}, f32[64,128]{1,0:T(8,128)S(1)}, u32[]{:S(2)}, u32[]{:S(2)}) collective-permute-start(f32[64,128]{1,0:T(8,128)S(1)} %shard_map.91.refs_0_), channel_id=1, source_target_pairs={{0,1},{1,0},{2,3},{3,2},{4,5},{5,4},{6,7},{7,6},{8,9},{9,8},{10,11... | collective-permute-start | bytes 98312 | tf_op jit(solution)/shard_map/ppermute | solution.py:207

commit v9 on v8

--- a/solution.py
+++ b/solution.py
@@ -90,7 +90,7 @@
                 else:
                     out[place, row] = tile
                 waiting.append((i, row, place, tile))
-                if len(waiting) > 2:
+                if len(waiting) > 1:
                     k, old_row, old_place, old = waiting.pop(0)
                     sum_ref[:, old_row] += jnp.dot(db_refs[k][:, old_place], old, preferred_element_type=F32)
             if i < 3 and p == 0:
@@ -142,7 +142,7 @@
         ]
         + [pltpu.VMEM((ctr // 4, DEPTH), BF16)] * 4
         + [pltpu.VMEM((targets, ctr // 4), BF16)] * 4,
-        compiler_params=pltpu.CompilerParams(vmem_limit_bytes=18 * MIB),
+        compiler_params=pltpu.CompilerParams(vmem_limit_bytes=12 * MIB),
     )(*[pltpu.with_memory_space_constraint(value, pltpu.HBM) for value in (points, centres, direction)])
     return out[:4], out[4]
 

time: 53.3 us -> 53.3 us (level)
  no operation moved by 1% of the time
where the time goes in v9:
time: 53.3 us; the launch traced here: 53.1 us
  Pallas kernels  23.3 us (44%)
  starting transfers between devices  15.3 us (29%)
  waiting for transfers between devices  13.8 us (26%)
  between operations  0.69 us (1%)
    pallas_call x1, Pallas kernels, fit_parts(): pl.pallas_call(functools.partial(fit_kernel, width_of(ctr // 4, 2048), wi...  15.6 us
    ppermute x8, starting transfers between devices, send_pts(): return lax.ppermute(value, ('pts', 'ctr'), pairs)  14.8 us
    ppermute x8, waiting for transfers between devices, send_pts(): return lax.ppermute(value, ('pts', 'ctr'), pairs)  11.7 us
    pallas_call x4, Pallas kernels, col_sums(): pl.pallas_call(functools.partial(col_kernel, width_of(size, 2048), i in T...  5.83 us
    ppermute x2, waiting for transfers between devices, over_ctr(): lax.ppermute(value, 'ctr', [(c, (c + k) % num_ctr) for c in range(num_ctr)])  2.1 us
    pallas_call x1, Pallas kernels, step_of(): pl.pallas_call(functools.partial(step_kernel, scale, len(sums)), out_shap...  1.32 us
  transfers between devices with their start and end apart: 10, of which 9 were waited for; matrix products, arithmetic and copies ran while one was open for 0% of the time, Pallas kernels for 9%

profile of v9, /device:TPU:0, one launch (start us, length us, event | category | flops | bytes accessed | tf_op | source)
XLA Modules:
  0.0 53.1 jit_solution(16955433463710490630)
XLA Ops:
  0.6 15.6 %shard_map.85 = (bf16[2048,2048]{1,0:T(8,128)(2,1)S(1)}, bf16[2048,2048]{1,0:T(8,128)(2,1)S(1)}, bf16[2048,2048]{1,0:T(8,128)(2,1)S(1)}, bf16[2048,2048]{1,0:T(8,128)(2,1)S(1)}, bf16[16,2048]{1,0:T(8,128)(2,1)S(1)}) custom-call(bf16[32,2048]{1,0:T(8,128)(2,1)} %pts_hbm.1, bf16[32,8192]{1,0:T(8,128)(2,1)} %cen_hbm.1, f32[16,8192]{1,0:T(8,128)} %refs_6_.1), custom_call_target="tpu_custom_call" | custom-call | tf_op jit(solution)/shard_map/pallas_call | solution.py:130
  16.2 0.5 collective-permute-start
  16.8 0.9 %collective-permute-done.refs_1_ = bf16[16,2048]{1,0:T(8,128)(2,1)S(1)} collective-permute-done((bf16[16,2048]{1,0:T(8,128)(2,1)S(1)}, bf16[16,2048]{1,0:T(8,128)(2,1)S(1)}, u32[]{:S(2)}, u32[]{:S(2)}) %collective-permute-start) | collective-permute-done | bytes 65568 | tf_op jit(solution)/shard_map/ppermute | solution.py:207
  17.7 1.2 %shard_map.87 = f32[16,2048]{1,0:T(8,128)S(1)} custom-call(bf16[16,2048]{1,0:T(8,128)(2,1)S(1)} %get-tuple-element.8.refs_0_, bf16[16,2048]{1,0:T(8,128)(2,1)S(1)} %collective-permute-done.refs_1_, bf16[2048,2048]{1,0:T(8,128)(2,1)S(1)} %get-tuple-element.10.refs_2_), custom_call_target="tpu_custom_call" | custom-call | tf_op jit(solution)/shard_map/pallas_call | solution.py:153
  18.9 2.9 %collective-permute-start.1 = (f32[16,2048]{1,0:T(8,128)S(1)}, f32[16,2048]{1,0:T(8,128)S(1)}, u32[]{:S(2)}, u32[]{:S(2)}) collective-permute-start(f32[16,2048]{1,0:T(8,128)S(1)} %shard_map.87), channel_id=1, source_target_pairs={{0,2},{1,5},{2,0},{3,7},{4,6},{5,1},{6,4},{7,3},{8,10},{9,13},{10,... | collective-permute-start | bytes 393224 | tf_op jit(solution)/shard_map/ppermute | solution.py:175
  21.7 1.2 %shard_map.89 = f32[16,2048]{1,0:T(8,128)S(1)} custom-call(bf16[16,2048]{1,0:T(8,128)(2,1)S(1)} %get-tuple-element.8.refs_0_, bf16[16,2048]{1,0:T(8,128)(2,1)S(1)} %collective-permute-done.refs_1_, bf16[2048,2048]{1,0:T(8,128)(2,1)S(1)} %get-tuple-element.12.refs_2_), custom_call_target="tpu_custom_call" | custom-call | tf_op jit(solution)/shard_map/pallas_call | solution.py:153
  22.9 0.0 collective-permute-start.3
  22.9 0.0 copy-start.3
  22.9 1.2 %shard_map.86 = f32[16,2048]{1,0:T(8,128)S(1)} custom-call(bf16[16,2048]{1,0:T(8,128)(2,1)S(1)} %get-tuple-element.8.refs_0_, bf16[16,2048]{1,0:T(8,128)(2,1)S(1)} %collective-permute-done.refs_1_, bf16[2048,2048]{1,0:T(8,128)(2,1)S(1)} %get-tuple-element.9.refs_2_), custom_call_target="tpu_custom_call" | custom-call | tf_op jit(solution)/shard_map/pallas_call | solution.py:153
  24.1 0.5 collective-permute-done.1
  24.7 2.1 %collective-permute-start.2 = (f32[16,2048]{1,0:T(8,128)S(1)}, f32[16,2048]{1,0:T(8,128)S(1)}, u32[]{:S(2)}, u32[]{:S(2)}) collective-permute-start(f32[16,2048]{1,0:T(8,128)S(1)} %add.15), channel_id=1, source_target_pairs={{0,4},{1,3},{2,6},{3,1},{4,0},{5,7},{6,2},{7,5},{8,12},{9,11},{10,... | collective-permute-start | bytes 393224 | tf_op jit(solution)/shard_map/ppermute | solution.py:175
  26.8 2.3 %shard_map.88 = f32[16,2048]{1,0:T(8,128)S(1)} custom-call(bf16[16,2048]{1,0:T(8,128)(2,1)S(1)} %get-tuple-element.8.refs_0_, bf16[16,2048]{1,0:T(8,128)(2,1)S(1)} %collective-permute-done.refs_1_, bf16[2048,2048]{1,0:T(8,128)(2,1)S(1)} %get-tuple-element.11.refs_2_), custom_call_target="tpu_custom_call" | custom-call | tf_op jit(solution)/shard_map/pallas_call | solution.py:153
  29.1 0.0 collective-permute-done.3
  29.1 0.7 %collective-permute-done.2 = f32[16,2048]{1,0:T(8,128)S(1)} collective-permute-done((f32[16,2048]{1,0:T(8,128)S(1)}, f32[16,2048]{1,0:T(8,128)S(1)}, u32[]{:S(2)}, u32[]{:S(2)}) %collective-permute-start.2) | collective-permute-done | bytes 131104 | tf_op jit(solution)/shard_map/ppermute | solution.py:175
  29.8 2.1 %collective-permute-start.4 = (f32[16,2048]{1,0:T(8,128)S(1)}, f32[16,2048]{1,0:T(8,128)S(1)}, u32[]{:S(2)}, u32[]{:S(2)}) collective-permute-start(f32[16,2048]{1,0:T(8,128)S(1)} %add_add_fusion), channel_id=1, source_target_pairs={{0,8},{1,9},{2,10},{3,11},{4,12},{5,13},{6,14},{7,15},{8,0},{9,1},... | collective-permute-start | bytes 393224 | tf_op jit(solution)/shard_map/ppermute | solution.py:175
  31.9 3.0 %collective-permute-done.4 = f32[16,2048]{1,0:T(8,128)S(1)} collective-permute-done((f32[16,2048]{1,0:T(8,128)S(1)}, f32[16,2048]{1,0:T(8,128)S(1)}, u32[]{:S(2)}, u32[]{:S(2)}) %collective-permute-start.4) | collective-permute-done | bytes 131104 | tf_op jit(solution)/shard_map/ppermute | solution.py:175
  34.9 4.1 %collective-permute-start.5 = (f32[16,2048]{1,0:T(8,128)S(1)}, f32[16,2048]{1,0:T(8,128)S(1)}, u32[]{:S(2)}, u32[]{:S(2)}) collective-permute-start(f32[16,2048]{1,0:T(8,128)S(1)} %add.18), channel_id=1, source_target_pairs={{0,24},{1,25},{2,26},{3,27},{4,28},{5,29},{6,30},{7,31},{8,16},{9,... | collective-permute-start | bytes 393224 | tf_op jit(solution)/shard_map/ppermute | solution.py:175
  39.0 3.1 %collective-permute-done.5 = f32[16,2048]{1,0:T(8,128)S(1)} collective-permute-done((f32[16,2048]{1,0:T(8,128)S(1)}, f32[16,2048]{1,0:T(8,128)S(1)}, u32[]{:S(2)}, u32[]{:S(2)}) %collective-permute-start.5) | collective-permute-done | bytes 131104 | tf_op jit(solution)/shard_map/ppermute | solution.py:175
  42.1 2.7 %collective-permute-start.8 = (f32[16,2048]{1,0:T(8,128)S(1)}, f32[16,2048]{1,0:T(8,128)S(1)}, u32[]{:S(2)}, u32[]{:S(2)}) collective-permute-start(f32[16,2048]{1,0:T(8,128)S(1)} %add.19.refs_1_.refs_5_), channel_id=1, source_target_pairs={{0,6},{1,7},{2,4},{3,5},{4,2},{5,3},{6,0},{7,1},{8,14},{9,15},{10,... | collective-permute-start | bytes 393224 | tf_op jit(solution)/shard_map/ppermute | solution.py:175
  44.8 0.5 collective-permute-start.7
  45.3 0.3 collective-permute-start.6
  45.6 2.4 %collective-permute-done.8.refs_0_.refs_2_ = f32[16,2048]{1,0:T(8,128)S(1)} collective-permute-done((f32[16,2048]{1,0:T(8,128)S(1)}, f32[16,2048]{1,0:T(8,128)S(1)}, u32[]{:S(2)}, u32[]{:S(2)}) %collective-permute-start.8) | collective-permute-done | bytes 131104 | tf_op jit(solution)/shard_map/ppermute | solution.py:175
  48.0 0.0 copy-done
  48.0 0.0 copy-done.1
  48.0 0.0 copy-done.3
  48.0 0.2 shard_map.90.refs_2_
  48.2 1.5 %collective-permute-done.7.refs_1_.refs_4_ = f32[16,2048]{1,0:T(8,128)S(1)} collective-permute-done((f32[16,2048]{1,0:T(8,128)S(1)}, f32[16,2048]{1,0:T(8,128)S(1)}, u32[]{:S(2)}, u32[]{:S(2)}) %collective-permute-start.7) | collective-permute-done | bytes 131104 | tf_op jit(solution)/shard_map/ppermute | solution.py:175
  49.8 0.5 collective-permute-done.6.refs_0_.refs_3_
  50.3 0.3 shard_map.91.refs_0_
  50.6 0.0 collective-permute-start.9
  50.6 1.2 %collective-permute-done.9.refs_1_ = f32[64,128]{1,0:T(8,128)S(1)} collective-permute-done((f32[64,128]{1,0:T(8,128)S(1)}, f32[64,128]{1,0:T(8,128)S(1)}, u32[]{:S(2)}, u32[]{:S(2)}) %collective-permute-start.9) | collective-permute-done | bytes 32800 | tf_op jit(solution)/shard_map/ppermute | solution.py:207
  51.8 1.3 %shard_map.92 = (f32[16,8192]{1,0:T(8,128)}, f32[16,8192]{1,0:T(8,128)}, f32[16,8192]{1,0:T(8,128)}) custom-call(f32[64,128]{1,0:T(8,128)S(1)} %shard_map.91.refs_0_, f32[64,128]{1,0:T(8,128)S(1)} %collective-permute-done.9.refs_1_, f32[16,2048]{1,0:T(8,128)S(1)} %collective-permute-done.8.refs_0_.refs_2_, ...), custom_call_target="tpu_custom_call" | custom-call | tf_op jit(solution)/shard_map/pallas_call | solution.py:261
  (8 shorter events, 0.1 us)
Async XLA Ops:
  16.2 1.4 %collective-permute-start = (bf16[16,2048]{1,0:T(8,128)(2,1)S(1)}, bf16[16,2048]{1,0:T(8,128)(2,1)S(1)}, u32[]{:S(2)}, u32[]{:S(2)}) collective-permute-start(bf16[16,2048]{1,0:T(8,128)(2,1)S(1)} %get-tuple-element.8.refs_0_), channel_id=1, source_target_pairs={{0,1},{1,0},{2,3},{3,2},{4,5},{5,4},{6,7},{7,6},{8,9},{9,8},{10,11... | collective-permute-start | bytes 196616 | tf_op jit(solution)/shard_map/ppermute | solution.py:207
  18.9 5.8 %collective-permute-start.1 = (f32[16,2048]{1,0:T(8,128)S(1)}, f32[16,2048]{1,0:T(8,128)S(1)}, u32[]{:S(2)}, u32[]{:S(2)}) collective-permute-start(f32[16,2048]{1,0:T(8,128)S(1)} %shard_map.87), channel_id=1, source_target_pairs={{0,2},{1,5},{2,0},{3,7},{4,6},{5,1},{6,4},{7,3},{8,10},{9,13},{10,... | collective-permute-start | bytes 393224 | tf_op jit(solution)/shard_map/ppermute | solution.py:175
  22.9 6.2 %collective-permute-start.3 = (f32[16,2048]{1,0:T(8,128)S(1)}, f32[16,2048]{1,0:T(8,128)S(1)}, u32[]{:S(2)}, u32[]{:S(2)}) collective-permute-start(f32[16,2048]{1,0:T(8,128)S(1)} %shard_map.89), channel_id=1, source_target_pairs={{0,2},{1,5},{2,0},{3,7},{4,6},{5,1},{6,4},{7,3},{8,10},{9,13},{10,... | collective-permute-start | bytes 393224 | tf_op jit(solution)/shard_map/ppermute | solution.py:175
  22.9 25.1 %copy-start = (f32[16,8192]{1,0:T(8,128)S(1)}, f32[16,8192]{1,0:T(8,128)}, u32[]{:S(2)}) copy-start(f32[16,8192]{1,0:T(8,128)} %refs_6_.1) | copy-start | bytes 1572868
  22.9 25.1 %copy-start.1 = (f32[16,8192]{1,0:T(8,128)S(1)}, f32[16,8192]{1,0:T(8,128)}, u32[]{:S(2)}) copy-start(f32[16,8192]{1,0:T(8,128)} %refs_7_.1) | copy-start | bytes 1572868
  22.9 25.1 %copy-start.3 = (f32[8192]{0:T(1024)S(1)}, f32[8192]{0:T(1024)}, u32[]{:S(2)}) copy-start(f32[8192]{0:T(1024)} %param.11) | copy-start | bytes 98308
  24.1 27.7 %copy-start.2 = (f32[16,8192]{1,0:T(8,128)S(1)}, f32[16,8192]{1,0:T(8,128)}, u32[]{:S(2)}) copy-start(f32[16,8192]{1,0:T(8,128)} %refs_9_.1) | copy-start | bytes 1572868
  24.7 5.1 %collective-permute-start.2 = (f32[16,2048]{1,0:T(8,128)S(1)}, f32[16,2048]{1,0:T(8,128)S(1)}, u32[]{:S(2)}, u32[]{:S(2)}) collective-permute-start(f32[16,2048]{1,0:T(8,128)S(1)} %add.15), channel_id=1, source_target_pairs={{0,4},{1,3},{2,6},{3,1},{4,0},{5,7},{6,2},{7,5},{8,12},{9,11},{10,... | collective-permute-start | bytes 393224 | tf_op jit(solution)/shard_map/ppermute | solution.py:175
  29.8 5.1 %collective-permute-start.4 = (f32[16,2048]{1,0:T(8,128)S(1)}, f32[16,2048]{1,0:T(8,128)S(1)}, u32[]{:S(2)}, u32[]{:S(2)}) collective-permute-start(f32[16,2048]{1,0:T(8,128)S(1)} %add_add_fusion), channel_id=1, source_target_pairs={{0,8},{1,9},{2,10},{3,11},{4,12},{5,13},{6,14},{7,15},{8,0},{9,1},... | collective-permute-start | bytes 393224 | tf_op jit(solution)/shard_map/ppermute | solution.py:175
  34.9 7.1 %collective-permute-start.5 = (f32[16,2048]{1,0:T(8,128)S(1)}, f32[16,2048]{1,0:T(8,128)S(1)}, u32[]{:S(2)}, u32[]{:S(2)}) collective-permute-start(f32[16,2048]{1,0:T(8,128)S(1)} %add.18), channel_id=1, source_target_pairs={{0,24},{1,25},{2,26},{3,27},{4,28},{5,29},{6,30},{7,31},{8,16},{9,... | collective-permute-start | bytes 393224 | tf_op jit(solution)/shard_map/ppermute | solution.py:175
  42.1 5.9 %collective-permute-start.8 = (f32[16,2048]{1,0:T(8,128)S(1)}, f32[16,2048]{1,0:T(8,128)S(1)}, u32[]{:S(2)}, u32[]{:S(2)}) collective-permute-start(f32[16,2048]{1,0:T(8,128)S(1)} %add.19.refs_1_.refs_5_), channel_id=1, source_target_pairs={{0,6},{1,7},{2,4},{3,5},{4,2},{5,3},{6,0},{7,1},{8,14},{9,15},{10,... | collective-permute-start | bytes 393224 | tf_op jit(solution)/shard_map/ppermute | solution.py:175
  44.8 5.0 %collective-permute-start.7 = (f32[16,2048]{1,0:T(8,128)S(1)}, f32[16,2048]{1,0:T(8,128)S(1)}, u32[]{:S(2)}, u32[]{:S(2)}) collective-permute-start(f32[16,2048]{1,0:T(8,128)S(1)} %add.19.refs_1_.refs_5_), channel_id=1, source_target_pairs={{0,4},{1,3},{2,6},{3,1},{4,0},{5,7},{6,2},{7,5},{8,12},{9,11},{10,... | collective-permute-start | bytes 393224 | tf_op jit(solution)/shard_map/ppermute | solution.py:175
  45.3 5.0 %collective-permute-start.6 = (f32[16,2048]{1,0:T(8,128)S(1)}, f32[16,2048]{1,0:T(8,128)S(1)}, u32[]{:S(2)}, u32[]{:S(2)}) collective-permute-start(f32[16,2048]{1,0:T(8,128)S(1)} %add.19.refs_1_.refs_5_), channel_id=1, source_target_pairs={{0,2},{1,5},{2,0},{3,7},{4,6},{5,1},{6,4},{7,3},{8,10},{9,13},{10,... | collective-permute-start | bytes 393224 | tf_op jit(solution)/shard_map/ppermute | solution.py:175
  50.6 1.2 %collective-permute-start.9 = (f32[64,128]{1,0:T(8,128)S(1)}, f32[64,128]{1,0:T(8,128)S(1)}, u32[]{:S(2)}, u32[]{:S(2)}) collective-permute-start(f32[64,128]{1,0:T(8,128)S(1)} %shard_map.91.refs_0_), channel_id=1, source_target_pairs={{0,1},{1,0},{2,3},{3,2},{4,5},{5,4},{6,7},{7,6},{8,9},{9,8},{10,11... | collective-permute-start | bytes 98312 | tf_op jit(solution)/shard_map/ppermute | solution.py:207
